TPU v7x, 32 devices: a whole 2x2x4 slice. The times are simulated.
32 devices in a mesh: wide: 8 (over z, y), narrow: 4 (over x, core).
Axes of the slice: x: 2, y: 2, z: 4, core: 2. Of those that a mesh axis runs over, the one named last changes fastest.
Arguments:
- daily_fields: bfloat16 [256, 704, 1440], P('narrow', 'wide'), may hold values from -6 to 6
- order_table: int32 [384], replicated, may hold values from 0 to 383, as said below
- lag_days: int32 [3], replicated, may hold values from 1 to 8, as said below
- lag_weights: float32 [3, 384, 384, 2], P(None, 'narrow', 'wide'), may hold values from -0.5 to 0.5
Outputs:
- noise_variance: float32 [384, 384, 2], P('narrow', 'wide')
- covariance_panel: float32 [384, 12, 1536], P('wide', None, 'narrow')
Inputs may be any that keep to these rules, and one draw needn't show every extreme that they name: `order_table`: slots 2k and 2k+1 hold the two orders m and 383 - m of one pair, the even one in slot 2k; every order appears once. `lag_days`: three different lags; one of them is 8.
All inputs are finite; a program needn't handle non-finite values.
Results may differ from a plain program's by a relative error of at most 0.0087.
Values may be sent and summed in bfloat16 or wider, within the bound.
No kernel may reach another device: no remote copies, remote signals or barrier semaphores. Data moves between devices by JAX's collectives and lax.ppermute only.
A program may use at most 128 MiB of HBM per device.

v0:
```python
import math

import jax
import jax.numpy as jnp
from jax import lax
from jax.sharding import PartitionSpec as P

NLAT = 704
NLON = 1440
M = 384
L = 384
LAGMAX = 8
ROW_DEG = 3


def dft_table(order_table):
    longitude = jnp.arange(NLON, dtype=jnp.int32)
    phase_turns = order_table[:, None] * longitude[None, :] % NLON
    angle = phase_turns.astype(jnp.float32) * (2.0 * math.pi / NLON)
    norm_scale = 1.0 / math.sqrt(NLON)
    return jnp.stack([jnp.cos(angle) * norm_scale, -jnp.sin(angle) * norm_scale], axis=1).astype(
        jnp.bfloat16
    )


def lat_basis():
    degree = jnp.arange(L, dtype=jnp.int32)
    odd_lat = 2 * jnp.arange(NLAT, dtype=jnp.int32) + 1
    period = 4 * NLAT
    even_turns = degree[:, None] * odd_lat[None, :] % period
    odd_turns = (degree[:, None] + 1) * odd_lat[None, :] % period
    angle_unit = math.pi / (2 * NLAT)
    norm_scale = math.sqrt(2.0 / NLAT)
    cosines = jnp.cos(even_turns.astype(jnp.float32) * angle_unit) * norm_scale
    sines = jnp.sin(odd_turns.astype(jnp.float32) * angle_unit) * norm_scale
    return jnp.stack([cosines, sines]).astype(jnp.bfloat16)


def body(daily_fields, order_table, lag_days, lag_weights):
    wide_count = lax.axis_size("wide")
    narrow_count = lax.axis_size("narrow")
    days_local, lat_local, lon_count = daily_fields.shape
    slot_local = M // wide_count
    pair_local = slot_local // 2
    deg_local = L // narrow_count
    times_all = days_local * narrow_count
    kept_days = times_all - LAGMAX
    dft_rows = dft_table(order_table).reshape(M * 2, lon_count)
    spectra = lax.dot_general(
        dft_rows, daily_fields, (((1,), (2,)), ((), ())), preferred_element_type=jnp.float32
    )
    spectra = spectra.astype(jnp.bfloat16).reshape(M // 2, 4, days_local * lat_local)
    received = lax.all_to_all(spectra, "wide", split_axis=0, concat_axis=0, tiled=True)
    received = received.reshape(wide_count, pair_local, 2, 2, days_local, lat_local)
    lat_table = lat_basis().reshape(2, L, wide_count, lat_local)
    coeffs = lax.dot_general(
        lat_table, received, (((2, 3), (0, 5)), ((0,), (2,))), preferred_element_type=jnp.float32
    )
    coeffs = coeffs.astype(jnp.bfloat16)
    packed = coeffs.reshape(2, L, pair_local, 2 * days_local)
    regrouped = lax.all_to_all(packed, "narrow", split_axis=1, concat_axis=0, tiled=True)
    series = regrouped.reshape(narrow_count, 2, deg_local, pair_local, 2, days_local)
    weights = jnp.transpose(lag_weights.reshape(3, deg_local, pair_local, 2, 2), (0, 3, 1, 2, 4))
    earlier = jnp.concatenate([jnp.zeros_like(series[:1]), series[:-1]], axis=0)
    joined = jnp.concatenate([earlier, series], axis=5)
    residual = series.astype(jnp.float32)
    for position in range(3):
        shifted = lax.dynamic_slice_in_dim(
            joined, days_local - lag_days[position], days_local, axis=5
        )
        residual = residual - weights[position][None, :, :, :, :, None] * shifted.astype(
            jnp.float32
        )
    day_index = (
        jnp.arange(narrow_count, dtype=jnp.int32)[:, None] * days_local
        + jnp.arange(days_local, dtype=jnp.int32)[None, :]
    )
    residual = jnp.where((day_index >= LAGMAX)[:, None, None, None, None, :], residual, 0.0)
    spread = jnp.sum(residual * residual, axis=(0, 5)) / kept_days
    noise_variance = jnp.transpose(spread, (1, 2, 0, 3)).reshape(deg_local, slot_local, 2)
    rounded = residual.astype(jnp.bfloat16)
    row_part = jnp.transpose(rounded[:, :, :ROW_DEG, :, 0, :], (3, 1, 2, 0, 4)).reshape(
        slot_local, ROW_DEG, times_all
    )
    row_series = lax.all_gather(row_part, "narrow", axis=1, tiled=True)
    column_part = jnp.transpose(rounded[:, :, ROW_DEG, :, 0, :], (2, 1, 0, 3)).reshape(
        slot_local, times_all
    )
    cov_panel = lax.dot_general(
        row_series,
        lax.all_gather(column_part, "wide", axis=0, tiled=True),
        (((2,), (1,)), ((), ())),
        preferred_element_type=jnp.float32,
    )
    cov_panel = cov_panel / math.sqrt(kept_days)
    return (noise_variance, cov_panel)


def solution(mesh):
    placed = (P("narrow", "wide", None), P(), P(), P(None, "narrow", "wide", None))
    return jax.shard_map(
        body,
        mesh=mesh,
        in_specs=placed,
        out_specs=(P("narrow", "wide", None), P("wide", None, "narrow")),
        check_vma=False,
    )
```

profile of v0, /device:TPU:0, one launch (start us, length us, event | category | flops | bytes accessed | tf_op | source)
XLA Modules:
  0.0 478.4 jit_solution(15029690995870323177)
XLA Ops:
  0.6 10.3 %multiply_convert_fusion.1 = (bf16[384,1,1440]{0,2,1:T(8,128)(2,1)S(1)}, bf16[384,1,1440]{0,2,1:T(8,128)(2,1)S(1)}) fusion(s32[384]{0:T(512)} %param.5), kind=kLoop, calls=%fused_computation.17 | loop fusion | flops 7741440 | bytes 2213376 | tf_op jit(solution)/shard_map/convert
  12.6 5.9 %copy.52 = bf16[384,2,1440]{2,1,0:T(2,128)(2,1)S(1)} copy(bf16[384,2,1440]{0,2,1:T(8,128)(2,1)} %pad_maximum_fusion) | data formatting | bytes 4423680 | tf_op jit(solution)/shard_map/stack | solution.py:21
  18.4 2.9 convert_element_type.67
  21.4 20.2 %convolution_convert_fusion = bf16[768,64,88]{0,2,1:T(8,128)(2,1)} fusion(bf16[64,88,1440]{2,1,0:T(8,128)(2,1)} %param.4, bf16[768,1440]{1,0:T(8,128)(2,1)} %convert_element_type.67), kind=kOutput, calls=%fused_computation.8 | convolution fusion | flops 12461408256 | bytes 27082752 | tf_op jit(solution)/shard_map/dot_general | solution.py:49
  41.6 15.9 %copy.54 = bf16[768,64,88]{2,1,0:T(8,128)(2,1)} copy(bf16[768,64,88]{0,2,1:T(8,128)(2,1)} %convolution_convert_fusion) | data formatting | bytes 17301504 | tf_op jit(solution)/shard_map/convert_element_type | solution.py:52
  57.5 28.0 %reshape.289 = bf16[192,4,5632]{2,1,0:T(4,128)(2,1)} reshape(bf16[768,64,88]{2,1,0:T(8,128)(2,1)} %copy.54) | data formatting | bytes 17301504 | tf_op jit(solution)/shard_map/reshape | solution.py:52
  85.5 7.3 %all-to-all-start = ((bf16[192,4,5632]{2,1,0:T(4,128)(2,1)}), bf16[192,4,5632]{2,1,0:T(4,128)(2,1)}, u32[]{:S(2)}, u32[]{:S(2)}) async-start(bf16[192,4,5632]{2,1,0:T(4,128)(2,1)} %reshape.289), calls=%async_computation | async-start | bytes 17301504 | tf_op jit(solution)/shard_map/all_to_all | solution.py:53
  92.8 8.7 %fusion.16 = (bf16[1,384,8,88]{1,3,2,0:T(8,128)(2,1)S(1)}, bf16[1,384,8,88]{1,3,2,0:T(8,128)(2,1)S(1)}) fusion(s32[8,88]{1,0:T(8,128)S(1)} %multiply_add_fusion, s32[384]{0:T(512)S(1)} %iota_add_fusion), kind=kLoop, calls=%fused_computation.29 | loop fusion | flops 5947392 | bytes 1085696 | tf_op jit(solution)/shard_map/convert.2
  101.5 180.1 %all-to-all-done = bf16[192,4,5632]{2,1,0:T(4,128)(2,1)} async-done(((bf16[192,4,5632]{2,1,0:T(4,128)(2,1)}), bf16[192,4,5632]{2,1,0:T(4,128)(2,1)}, u32[]{:S(2)}, u32[]{:S(2)}) %all-to-all-start) | async-done | bytes 8650784 | tf_op jit(solution)/shard_map/all_to_all | solution.py:53
  281.6 32.2 %reshape.301 = bf16[8,24,2,2,64,88]{5,4,3,2,1,0:T(8,128)(2,1)} reshape(bf16[192,4,5632]{2,1,0:T(4,128)(2,1)} %all-to-all-done) | data formatting | bytes 17301504 | tf_op jit(solution)/shard_map/reshape | solution.py:54
  313.8 10.2 %bitcast_convert_fusion = bf16[2,384,24,2,64]{1,4,3,2,0:T(8,128)(2,1)} fusion(bf16[8,24,2,2,64,88]{5,4,3,2,1,0:T(8,128)(2,1)} %reshape.301, bf16[1,384,8,88]{1,3,2,0:T(8,128)(2,1)S(1)} %get-tuple-element.12, bf16[1,384,8,88]{1,3,2,0:T(8,128)(2,1)S(1)} %get-tuple-element.11), kind=kOutput, calls=%fused_computation.7 | convolution fusion | flops 3326410752 | bytes 14450688 | tf_op jit(solution)/shard_map/dot_general | solution.py:56
  324.0 7.0 %copy.57 = bf16[2,384,24,128]{3,2,0,1:T(8,128)(2,1)} copy(bf16[2,384,24,128]{1,3,2,0:T(8,128)(2,1)} %bitcast.54) | data formatting | bytes 9437184 | tf_op jit(solution)/shard_map/reshape | solution.py:60
  331.0 5.3 %all-to-all-start.1 = ((bf16[2,384,24,128]{3,2,0,1:T(8,128)(2,1)}), bf16[2,384,24,128]{3,2,0,1:T(8,128)(2,1)}, u32[]{:S(2)}, u32[]{:S(2)}) async-start(bf16[2,384,24,128]{3,2,0,1:T(8,128)(2,1)} %copy.57), calls=%async_computation.1 | async-start | bytes 9437184 | tf_op jit(solution)/shard_map/all_to_all | solution.py:61
  341.5 48.5 %all-to-all-done.1 = bf16[2,384,24,128]{3,2,0,1:T(8,128)(2,1)} async-done(((bf16[2,384,24,128]{3,2,0,1:T(8,128)(2,1)}), bf16[2,384,24,128]{3,2,0,1:T(8,128)(2,1)}, u32[]{:S(2)}, u32[]{:S(2)}) %all-to-all-start.1) | async-done | bytes 4718624 | tf_op jit(solution)/shard_map/all_to_all | solution.py:61
  390.0 3.1 copy.58
  393.8 4.3 copy.61
  398.0 8.2 %copy.59 = bf16[4,2,96,24,128]{2,4,3,1,0:T(8,128)(2,1)} copy(bf16[4,2,96,24,128]{4,3,1,2,0:T(8,128)(2,1)} %bitcast.8) | data formatting | bytes 9437184 | tf_op jit(solution)/shard_map/all_to_all | solution.py:61
  406.3 7.7 %fusion.1 = bf16[4,2,96,24,2,128]{2,5,4,3,1,0:T(8,128)(2,1)S(1)} fusion(bf16[3,2,96,24,2,64]{2,5,4,3,1,0:T(8,128)(2,1)} %bitcast.52, bf16[4,2,96,24,2,64]{2,5,4,3,1,0:T(8,128)(2,1)} %bitcast.50), kind=kLoop, calls=%fused_computation.2 | loop fusion | flops 28311552 | bytes 17694720 | tf_op jit(solution)/shard_map/concatenate | solution.py:65
  414.0 16.2 %fusion.32 = (bf16[4,2,96,24,2,64]{2,5,4,3,1,0:T(8,128)(2,1)}, f32[2,96,24,2]{1,3,2,0:T(2,128)S(1)}) fusion(bf16[4,2,96,24,2,128]{2,5,4,3,1,0:T(8,128)(2,1)S(1)} %fusion.1, s32[]{:T(128)S(6)} %select_n.62, f32[2,96,24,2]{1,3,2,0:T(2,128)S(1)} %copy-done.2, s32[]{:T(128)S(6)} %select_n.61, f32[2,96,24,2]{1,3,2,0:T(2,128)S(1)} %copy-done.3, s32[]{:T(128)S(6)} %select_n.60, ...), kind=kLoop, calls=%fused_computation.57 | loop fusion | flops 44817408 | bytes 28459276 | tf_op jit(solution)/shard_map/convert_element_type | solution.py:81
  430.3 4.5 slice_reduce_fusion
  434.8 3.1 slice_bitcast_fusion
  438.6 1.7 copy.63
  440.6 30.7 %all_gather.7 = bf16[384,256]{1,0:T(8,128)(2,1)S(1)} all-gather(bf16[48,256]{1,0:T(8,128)(2,1)S(1)} %reshape.296), channel_id=1, replica_groups=mesh['wide'=8,'narrow'=4] {'wide'}, dimensions={0}, use_global_device_ids=true | all-gather | bytes 221184 | tf_op jit(solution)/shard_map/all_gather | solution.py:91
  471.3 5.9 %all_gather.6 = bf16[48,12,256]{2,0,1:T(8,128)(2,1)S(1)} all-gather(bf16[48,3,256]{2,0,1:T(8,128)(2,1)S(1)} %reshape.295), channel_id=1, replica_groups=mesh['wide'=8,'narrow'=4] {'narrow'}, dimensions={1}, use_global_device_ids=true | all-gather | bytes 368640 | tf_op jit(solution)/shard_map/all_gather | solution.py:85
  (28 shorter events, 5.9 us)
Async XLA Ops:
  85.5 196.1 %all-to-all-start = ((bf16[192,4,5632]{2,1,0:T(4,128)(2,1)}), bf16[192,4,5632]{2,1,0:T(4,128)(2,1)}, u32[]{:S(2)}, u32[]{:S(2)}) async-start(bf16[192,4,5632]{2,1,0:T(4,128)(2,1)} %reshape.289), calls=%async_computation | async-start | bytes 17301504 | tf_op jit(solution)/shard_map/all_to_all | solution.py:53
  331.0 5.3 %copy-start.5 = (s32[3]{0:T(128)S(1)}, s32[3]{0:T(128)}, u32[]{:S(2)}) copy-start(s32[3]{0:T(128)} %param.6) | copy-start | bytes 40
  331.0 9.6 %copy-start.4 = (f32[3,96,48,2]{1,3,2,0:T(2,128)S(1)}, f32[3,96,48,2]{1,3,2,0:T(2,128)}, u32[]{:S(2)}) copy-start(f32[3,96,48,2]{1,3,2,0:T(2,128)} %param.7) | copy-start | bytes 331780
  331.0 58.9 %all-to-all-start.1 = ((bf16[2,384,24,128]{3,2,0,1:T(8,128)(2,1)}), bf16[2,384,24,128]{3,2,0,1:T(8,128)(2,1)}, u32[]{:S(2)}, u32[]{:S(2)}) async-start(bf16[2,384,24,128]{3,2,0,1:T(8,128)(2,1)} %copy.57), calls=%async_computation.1 | async-start | bytes 9437184 | tf_op jit(solution)/shard_map/all_to_all | solution.py:61
  406.3 7.7 %copy-start = (bf16[4,2,96,24,128]{2,4,3,1,0:T(8,128)(2,1)S(1)}, bf16[4,2,96,24,128]{2,4,3,1,0:T(8,128)(2,1)}, u32[]{:S(2)}) copy-start(bf16[4,2,96,24,128]{2,4,3,1,0:T(8,128)(2,1)} %copy.59) | copy-start | bytes 14155780
  406.3 7.8 %copy-start.1 = (f32[2,96,24,2]{1,3,2,0:T(2,128)S(1)}, f32[2,96,24,2]{1,3,2,0:T(2,128)}, u32[]{:S(2)}) copy-start(f32[2,96,24,2]{1,3,2,0:T(2,128)} %get-tuple-element.8) | copy-start | bytes 110596
  406.3 7.8 %copy-start.2 = (f32[2,96,24,2]{1,3,2,0:T(2,128)S(1)}, f32[2,96,24,2]{1,3,2,0:T(2,128)}, u32[]{:S(2)}) copy-start(f32[2,96,24,2]{1,3,2,0:T(2,128)} %get-tuple-element.9) | copy-start | bytes 110596
  406.3 7.8 %copy-start.3 = (f32[2,96,24,2]{1,3,2,0:T(2,128)S(1)}, f32[2,96,24,2]{1,3,2,0:T(2,128)}, u32[]{:S(2)}) copy-start(f32[2,96,24,2]{1,3,2,0:T(2,128)} %get-tuple-element.10) | copy-start | bytes 110596
where the time goes:
time: 480 us; the launch traced here: 478 us
  waiting for transfers between devices  229 us (48%)
  local copies, waits for them, and re-layouts  120 us (25%)
  other arithmetic  44.7 us (9%)
  blocking collectives  36.6 us (8%)
  matrix products  31.7 us (7%)
  starting transfers between devices  12.6 us (3%)
    all_to_all x1, waiting for transfers between devices, body(): lax.all_to_all(spectra, 'wide', split_axis=0, concat_axis=0, tiled=True)  180 us
    all_to_all x1, waiting for transfers between devices, body(): lax.all_to_all(packed, 'narrow', split_axis=1, concat_axis=0, tiled=True)  48.5 us
    reshape x1, local copies, waits for them, and re-layouts, body(): received.reshape(wide_count, pair_local, 2, 2, days_local, lat_local)  32.2 us
    all_gather x1, blocking collectives, body(): lax.all_gather(column_part, 'wide', axis=0, tiled=True)  30.7 us
    reshape x1, local copies, waits for them, and re-layouts, body(): spectra.astype(jnp.bfloat16).reshape(M // 2, 4, days_local * lat_local)  28 us
    dot_general x1, matrix products, body(): lax.dot_general(dft_rows, daily_fields, (((1,), (2,)), ((), ())), preferr...  20.2 us
    another operation x2, other arithmetic  19 us
    convert_element_type x1, other arithmetic, body(): rounded = residual.astype(jnp.bfloat16)  16.2 us
  transfers between devices with their start and end apart: 2, of which 2 were waited for; matrix products, arithmetic and copies ran while one was open for 2% of the time, Pallas kernels for 0%

commit v1 on v0

v1 whole, which is shorter than its diff:
```python
import functools
import math

import jax
import jax.numpy as jnp
import numpy as np
from jax import lax
from jax.experimental import pallas as pl
from jax.experimental.pallas import tpu as pltpu
from jax.sharding import PartitionSpec as P

LAGMAX = 8
ROW_DEG = 3
VMEM = 48 * 2**20


def dft_parts(orders, longitudes):
    turns = np.arange(orders)[:, None] * np.arange(longitudes)[None, :] % longitudes
    angle = turns * (2.0 * np.pi / longitudes)
    scale = 1.0 / math.sqrt(longitudes)
    return np.stack([np.cos(angle) * scale, -np.sin(angle) * scale]).astype(jnp.bfloat16)


def lat_columns(degrees, latitudes):
    degree = np.arange(degrees)[None, :]
    odd_lat = 2 * np.arange(latitudes)[:, None] + 1
    period = 4 * latitudes
    unit = np.pi / (2 * latitudes)
    scale = math.sqrt(2.0 / latitudes)
    cosines = np.cos(degree * odd_lat % period * unit) * scale
    sines = np.sin((degree + 1) * odd_lat % period * unit) * scale
    return np.concatenate([cosines, sines], axis=1).astype(jnp.bfloat16)


def spectra_kernel(table_ref, field_ref, out_ref):
    out_ref[...] = lax.dot_general(
        table_ref[...],
        field_ref[...],
        (((1,), (1,)), ((), ())),
        preferred_element_type=jnp.float32,
    ).astype(jnp.bfloat16)


def spectra_of(table, fields, lat_local, day_block):
    rows, lon_count = table.shape
    cells = fields.shape[0]
    block = day_block * lat_local
    return pl.pallas_call(
        spectra_kernel,
        grid=(cells // block,),
        in_specs=[
            pl.BlockSpec((rows, lon_count), lambda i: (0, 0)),
            pl.BlockSpec((block, lon_count), lambda i: (i, 0)),
        ],
        out_specs=pl.BlockSpec((rows, block), lambda i: (0, i)),
        out_shape=jax.ShapeDtypeStruct((rows, cells), jnp.bfloat16),
        compiler_params=pltpu.CompilerParams(vmem_limit_bytes=VMEM),
        cost_estimate=pl.CostEstimate(
            flops=2 * rows * cells * lon_count,
            bytes_accessed=2 * (cells * lon_count + rows * cells + rows * lon_count),
            transcendentals=0,
        ),
    )(table, fields)


def coeffs_kernel(day_block, lat_local, recv_ref, lat_ref, out_ref, line_ref):
    sources, slots, _ = recv_ref.shape
    degrees = out_ref.shape[2]
    padded = line_ref.shape[1]
    for day in range(day_block):
        for source in range(sources):
            line_ref[day, :slots, source * lat_local : (source + 1) * lat_local] = recv_ref[
                source, :, day * lat_local : (day + 1) * lat_local
            ]
    both = jnp.dot(
        line_ref[...].reshape(day_block * padded, sources * lat_local),
        lat_ref[...],
        preferred_element_type=jnp.float32,
    ).reshape(day_block, padded, 2 * degrees)
    odd = lax.broadcasted_iota(jnp.int32, (day_block, padded, degrees), 1) % 2 == 1
    picked = jnp.where(odd, both[:, :, degrees:], both[:, :, :degrees])
    out_ref[...] = picked.astype(jnp.bfloat16)[:, :slots]


def coeffs_of(received, lat_table, days_local, day_block):
    sources, slots, cells = received.shape
    latitudes, degrees = lat_table.shape[0], lat_table.shape[1] // 2
    lat_local = latitudes // sources
    block = day_block * lat_local
    return pl.pallas_call(
        functools.partial(coeffs_kernel, day_block, lat_local),
        grid=(days_local // day_block,),
        in_specs=[
            pl.BlockSpec((sources, slots, block), lambda i: (0, 0, i)),
            pl.BlockSpec(lat_table.shape, lambda i: (0, 0)),
        ],
        out_specs=pl.BlockSpec((day_block, slots, degrees), lambda i: (i, 0, 0)),
        out_shape=jax.ShapeDtypeStruct((days_local, slots, degrees), jnp.bfloat16),
        scratch_shapes=[pltpu.VMEM((day_block, -(-slots // 16) * 16, latitudes), jnp.bfloat16)],
        compiler_params=pltpu.CompilerParams(vmem_limit_bytes=VMEM),
        cost_estimate=pl.CostEstimate(
            flops=4 * slots * cells * sources * degrees,
            bytes_accessed=2 * (sources * slots * cells + days_local * slots * degrees),
            transcendentals=0,
        ),
    )(received, lat_table)


def spread_kernel(lag_ref, series_ref, weight_ref, out_ref):
    days, slots, degrees = series_ref.shape
    step = 16 if slots % 16 == 0 else slots
    lags = [lag_ref[i] for i in range(3)]
    for first in range(0, slots, step):
        rows = pl.ds(first, step)
        weights = [weight_ref[i, rows, :] for i in range(3)]

        def add_day(day, total):
            residual = series_ref[day, rows, :].astype(jnp.float32)
            for lag, weight in zip(lags, weights):
                residual = residual - weight * series_ref[day - lag, rows, :].astype(jnp.float32)
            return total + residual * residual

        out_ref[rows, :] = lax.fori_loop(
            LAGMAX, days, add_day, jnp.zeros((step, degrees), jnp.float32), unroll=4
        )


def spread_of(lag_days, series, weights):
    days, slots, degrees = series.shape
    whole = pl.BlockSpec(memory_space=pltpu.VMEM)
    return pl.pallas_call(
        spread_kernel,
        in_specs=[pl.BlockSpec(memory_space=pltpu.SMEM), whole, whole],
        out_specs=whole,
        out_shape=jax.ShapeDtypeStruct((slots, degrees), jnp.float32),
        compiler_params=pltpu.CompilerParams(vmem_limit_bytes=VMEM),
        cost_estimate=pl.CostEstimate(
            flops=8 * days * slots * degrees,
            bytes_accessed=2 * days * slots * degrees + 16 * slots * degrees,
            transcendentals=0,
        ),
    )(lag_days, series, weights)


def swap_blocks(blocks, axis):
    count = lax.axis_size(axis)
    me = lax.axis_index(axis)
    got = [lax.dynamic_index_in_dim(blocks, me, 0, keepdims=False)]
    for hop in range(1, count):
        if count & (count - 1) == 0:
            target, pairs = me ^ hop, [(i, i ^ hop) for i in range(count)]
        else:
            target, pairs = (me + hop) % count, [(i, (i + hop) % count) for i in range(count)]
        block = lax.dynamic_index_in_dim(blocks, target, 0, keepdims=False)
        got.append(lax.ppermute(block, axis, pairs))
    order = jnp.arange(count, dtype=jnp.int32)
    order = (order ^ me) if count & (count - 1) == 0 else (me - order) % count
    return jnp.take(jnp.stack(got), order, axis=0)


def lagged_residual(series, weights, lag_days, days_axis, first, count):
    residual = lax.slice_in_dim(series, first, first + count, axis=days_axis).astype(jnp.float32)
    for position in range(3):
        shifted = lax.dynamic_slice_in_dim(
            series, first - lag_days[position], count, axis=days_axis
        )
        residual = residual - weights[position] * shifted.astype(jnp.float32)
    return residual


def body(daily_fields, order_table, lag_days, lag_weights):
    wide_count = lax.axis_size("wide")
    narrow_count = lax.axis_size("narrow")
    days_local, lat_local, lon_count = daily_fields.shape
    order_count = order_table.shape[0]
    slot_local = order_count // wide_count
    deg_local = lag_weights.shape[1]
    deg_count = deg_local * narrow_count
    times_all = days_local * narrow_count
    kept_days = times_all - LAGMAX
    day_block = math.gcd(128 // math.gcd(128, lat_local), days_local)

    fields = daily_fields.reshape(days_local * lat_local, lon_count)
    parts = jnp.asarray(dft_parts(order_count, lon_count))
    lat_table = jnp.asarray(lat_columns(deg_count, lat_local * wide_count))
    by_owner = order_table.reshape(wide_count, slot_local)

    if slot_local % 16 == 0 and slot_local > 16:
        chunks = [(0, 0, 16), (0, 16, slot_local), (1, 0, slot_local - 16), (1, slot_local - 16, slot_local)]
    else:
        chunks = [(0, 0, slot_local), (1, 0, slot_local)]

    own_weights = jnp.transpose(lag_weights, (3, 0, 2, 1))
    all_weights = lax.all_gather(own_weights, "narrow", axis=3, tiled=True)

    series = []
    spreads = []
    for part, first, last in chunks:
        count = last - first
        orders = by_owner[:, first:last].reshape(wide_count * count)
        pick = (orders[:, None] == jnp.arange(order_count, dtype=jnp.int32)[None, :]).astype(
            jnp.bfloat16
        )
        table = jnp.dot(pick, parts[part], preferred_element_type=jnp.float32).astype(jnp.bfloat16)
        spectra = spectra_of(table, fields, lat_local, day_block)
        spectra = spectra.reshape(wide_count, count, days_local * lat_local)
        received = lax.all_to_all(spectra, "wide", split_axis=0, concat_axis=0, tiled=True)
        coeffs = coeffs_of(received, lat_table, days_local, day_block)
        series.append((part, coeffs))
        inner = spread_of(lag_days, coeffs, all_weights[part, :, first:last])
        ends = jnp.concatenate([coeffs[:LAGMAX], coeffs[days_local - LAGMAX :]], axis=0)
        ends = jnp.transpose(
            ends.reshape(2 * LAGMAX, count, narrow_count, deg_local), (2, 0, 1, 3)
        )
        inner = jnp.transpose(inner.reshape(count, narrow_count, deg_local), (1, 0, 2))
        ends = swap_blocks(ends, "narrow")
        inner = swap_blocks(inner, "narrow")
        seams = jnp.concatenate([ends[:-1, LAGMAX:], ends[1:, :LAGMAX]], axis=1)
        seam = lagged_residual(
            seams, own_weights[part, :, first:last], lag_days, 1, LAGMAX, LAGMAX
        )
        spreads.append(jnp.sum(inner, axis=0) + jnp.sum(seam * seam, axis=(0, 1)))

    split = [sum(1 for p, _, _ in chunks if p == 0)]
    spread = jnp.stack(
        [jnp.concatenate(spreads[: split[0]], axis=0), jnp.concatenate(spreads[split[0] :], axis=0)],
        axis=2,
    )
    noise_variance = jnp.transpose(spread / kept_days, (1, 0, 2))

    picked = []
    for part, coeffs in series:
        if part == 0:
            by_block = coeffs.reshape(days_local, coeffs.shape[1], narrow_count, deg_local)
            picked.append(by_block[..., : ROW_DEG + 1])
    picked = jnp.transpose(jnp.concatenate(picked, axis=1), (1, 2, 3, 0))
    picked = lax.all_gather(picked, "narrow", axis=3, tiled=True)
    panel_weights = all_weights[0].reshape(3, slot_local, narrow_count, deg_local)
    panel_weights = panel_weights[..., : ROW_DEG + 1, None]
    kept = lagged_residual(picked, panel_weights, lag_days, 3, LAGMAX, kept_days)
    kept = kept.astype(jnp.bfloat16)
    rows = kept[:, :, :ROW_DEG].reshape(slot_local, narrow_count * ROW_DEG, kept_days)
    column = lax.dynamic_index_in_dim(kept[:, :, ROW_DEG], lax.axis_index("narrow"), 1, False)
    columns = lax.all_gather(column, "wide", axis=0, tiled=True)
    panel = lax.dot_general(
        rows, columns, (((2,), (1,)), ((), ())), preferred_element_type=jnp.float32
    )
    return (noise_variance, panel / math.sqrt(kept_days))


def solution(mesh):
    placed = (P("narrow", "wide", None), P(), P(), P(None, "narrow", "wide", None))
    return jax.shard_map(
        body,
        mesh=mesh,
        in_specs=placed,
        out_specs=(P("narrow", "wide", None), P("wide", None, "narrow")),
        check_vma=False,
    )
```

time: 480 us -> 341 us (0.71)
  waiting for transfers between devices: 229 us -> 109 us
  Pallas kernels: 0 us -> 66.3 us
  local copies, waits for them, and re-layouts: 120 us -> 55.8 us
  other arithmetic: 44.7 us -> 6.4 us
  matrix products: 31.7 us -> 5.16 us
  starting transfers between devices: 12.6 us -> 36.9 us
  blocking collectives: 36.6 us -> 51.8 us
    all_to_all x1 -> x4, waiting for transfers between devices: 180 us -> 98.7 us  [body(): lax.all_to_all(spectra, 'wide', split_axis=0, concat_axis=0, tiled=True)]
    pallas_call x0 -> x12, Pallas kernels: none -> 66.3 us  [the longest x4 40.8 us: spectra_of(): pl.pallas_call(spectra_kernel, grid=(cells // block,), in_specs=[pl.Block...]
    reshape x6 -> x11, local copies, waits for them, and re-layouts: 67.6 us -> 11.3 us  [the longest x2 9.11 us: body(): coeffs.reshape(days_local, coeffs.shape[1], narrow_count, deg_local)]
    all_to_all x1 -> x0, waiting for transfers between devices: 48.5 us -> none  [body(): lax.all_to_all(packed, 'narrow', split_axis=1, concat_axis=0, tiled=True)]
    dot_general x3 -> x5, matrix products: 31.7 us -> 5.16 us  [the longest x4 3.91 us: body(): jnp.dot(pick, parts[part], preferred_element_type=jnp.float32)]
    another operation x3 -> x8, other arithmetic: 20.6 us -> 0.45 us  [swap_blocks(): return jnp.take(jnp.stack(got), order, axis=0)]
    convert_element_type x2 -> x4, local copies, waits for them, and re-layouts: 18.8 us -> 0.92 us  [body(): jnp.dot(pick, parts[part], preferred_element_type=jnp.float32)]
    ppermute x0 -> x24, starting transfers between devices: none -> 16.1 us  [swap_blocks(): got.append(lax.ppermute(block, axis, pairs))]
  transfers between devices with their start and end apart: 2 -> 28, of which waited for: 2 -> 10; matrix products, arithmetic and copies ran while one was open for 2% -> 17% of each run, Pallas kernels for 0% -> 14%
where the time goes in v1:
time: 341 us; the launch traced here: 339 us
  waiting for transfers between devices  109 us (32%)
  Pallas kernels  66.3 us (19%)
  local copies, waits for them, and re-layouts  55.8 us (16%)
  blocking collectives  51.8 us (15%)
  starting transfers between devices  36.9 us (11%)
  between operations  7.47 us (2%)
  other arithmetic  6.4 us (2%)
  matrix products  5.16 us (2%)
    all_to_all x4, waiting for transfers between devices, body(): lax.all_to_all(spectra, 'wide', split_axis=0, concat_axis=0, tiled=True)  98.7 us
    pallas_call x4, Pallas kernels, spectra_of(): pl.pallas_call(spectra_kernel, grid=(cells // block,), in_specs=[pl.Block...  40.8 us
    all_gather x1, blocking collectives, body(): columns = lax.all_gather(column, 'wide', axis=0, tiled=True)  31.1 us
    all_to_all x4, starting transfers between devices, body(): lax.all_to_all(spectra, 'wide', split_axis=0, concat_axis=0, tiled=True)  20.8 us
    pallas_call x4, Pallas kernels, coeffs_of(): pl.pallas_call(functools.partial(coeffs_kernel, day_block, lat_local), gr...  19.8 us
    ppermute x24, starting transfers between devices, swap_blocks(): got.append(lax.ppermute(block, axis, pairs))  16.1 us
    all_gather x1, blocking collectives, body(): all_weights = lax.all_gather(own_weights, 'narrow', axis=3, tiled=True)  10.7 us
    ppermute x24, waiting for transfers between devices, swap_blocks(): got.append(lax.ppermute(block, axis, pairs))  10.7 us
  transfers between devices with their start and end apart: 28, of which 10 were waited for; matrix products, arithmetic and copies ran while one was open for 17% of the time, Pallas kernels for 14%

profile of v1, /device:TPU:0, one launch (start us, length us, event | category | flops | bytes accessed | tf_op | source)
XLA Modules:
  0.0 339.3 jit_solution(12231716531186187562)
XLA Ops:
  3.6 10.0 %shard_map.86 = bf16[128,5632]{1,0:T(8,128)(2,1)} custom-call(bf16[128,1440]{1,0:T(8,128)(2,1)S(1)} %copy.204.table_ref, bf16[5632,1440]{1,0:T(8,128)(2,1)} %bitcast.152), custom_call_target="tpu_custom_call" | custom-call | flops 2076180480 | bytes 18030592 | tf_op jit(solution)/shard_map/pallas_call | solution.py:48
  13.7 7.4 %all-to-all-start.3 = ((bf16[8,16,5632]{2,1,0:T(8,128)(2,1)}), bf16[8,16,5632]{2,1,0:T(8,128)(2,1)S(1)}, u32[]{:S(2)}, u32[]{:S(2)}) async-start(bf16[8,16,5632]{2,1,0:T(8,128)(2,1)} %bitcast.66), calls=%async_computation.3 | async-start | bytes 2883584 | tf_op jit(solution)/shard_map/all_to_all | solution.py:207
  22.0 10.1 %shard_map.77 = bf16[128,5632]{1,0:T(8,128)(2,1)} custom-call(bf16[128,1440]{1,0:T(8,128)(2,1)S(1)} %copy.176.table_ref, bf16[5632,1440]{1,0:T(8,128)(2,1)} %bitcast.153), custom_call_target="tpu_custom_call" | custom-call | flops 2076180480 | bytes 18030592 | tf_op jit(solution)/shard_map/pallas_call | solution.py:48
  32.0 23.2 %all-to-all-done.3.recv_ref = bf16[8,16,5632]{2,1,0:T(8,128)(2,1)S(1)} async-done(((bf16[8,16,5632]{2,1,0:T(8,128)(2,1)}), bf16[8,16,5632]{2,1,0:T(8,128)(2,1)S(1)}, u32[]{:S(2)}, u32[]{:S(2)}) %all-to-all-start.3) | async-done | bytes 1441824 | tf_op jit(solution)/shard_map/all_to_all | solution.py:207
  55.3 4.3 %all-to-all-start = ((bf16[8,16,5632]{2,1,0:T(8,128)(2,1)}), bf16[8,16,5632]{2,1,0:T(8,128)(2,1)}, u32[]{:S(2)}, u32[]{:S(2)}) async-start(bf16[8,16,5632]{2,1,0:T(8,128)(2,1)} %bitcast.1), calls=%async_computation | async-start | bytes 2883584 | tf_op jit(solution)/shard_map/all_to_all | solution.py:207
  60.7 10.3 %shard_map.80 = bf16[256,5632]{1,0:T(8,128)(2,1)} custom-call(bf16[256,1440]{1,0:T(8,128)(2,1)S(1)} %copy.186.table_ref, bf16[5632,1440]{1,0:T(8,128)(2,1)} %bitcast.154), custom_call_target="tpu_custom_call" | custom-call | flops 4152360960 | bytes 19841024 | tf_op jit(solution)/shard_map/pallas_call | solution.py:48
  71.0 22.4 %all-to-all-done.recv_ref = bf16[8,16,5632]{2,1,0:T(8,128)(2,1)} async-done(((bf16[8,16,5632]{2,1,0:T(8,128)(2,1)}), bf16[8,16,5632]{2,1,0:T(8,128)(2,1)}, u32[]{:S(2)}, u32[]{:S(2)}) %all-to-all-start) | async-done | bytes 1441824 | tf_op jit(solution)/shard_map/all_to_all | solution.py:207
  93.4 4.6 %all-to-all-start.1 = ((bf16[8,32,5632]{2,1,0:T(8,128)(2,1)}), bf16[8,32,5632]{2,1,0:T(8,128)(2,1)}, u32[]{:S(2)}, u32[]{:S(2)}) async-start(bf16[8,32,5632]{2,1,0:T(8,128)(2,1)} %bitcast.27), calls=%async_computation.1 | async-start | bytes 5767168 | tf_op jit(solution)/shard_map/all_to_all | solution.py:207
  99.1 10.4 %shard_map.83 = bf16[256,5632]{1,0:T(8,128)(2,1)} custom-call(bf16[256,1440]{1,0:T(8,128)(2,1)S(1)} %copy.195.table_ref, bf16[5632,1440]{1,0:T(8,128)(2,1)} %bitcast.155), custom_call_target="tpu_custom_call" | custom-call | flops 4152360960 | bytes 19841024 | tf_op jit(solution)/shard_map/pallas_call | solution.py:48
  109.4 53.1 %all-to-all-done.1.recv_ref = bf16[8,32,5632]{2,1,0:T(8,128)(2,1)} async-done(((bf16[8,32,5632]{2,1,0:T(8,128)(2,1)}), bf16[8,32,5632]{2,1,0:T(8,128)(2,1)}, u32[]{:S(2)}, u32[]{:S(2)}) %all-to-all-start.1) | async-done | bytes 2883616 | tf_op jit(solution)/shard_map/all_to_all | solution.py:207
  162.6 4.6 %all-to-all-start.2 = ((bf16[8,32,5632]{2,1,0:T(8,128)(2,1)}), bf16[8,32,5632]{2,1,0:T(8,128)(2,1)}, u32[]{:S(2)}, u32[]{:S(2)}) async-start(bf16[8,32,5632]{2,1,0:T(8,128)(2,1)} %bitcast.47), calls=%async_computation.2 | async-start | bytes 5767168 | tf_op jit(solution)/shard_map/all_to_all | solution.py:207
  181.5 10.7 %all_gather.9 = f32[2,3,48,384]{2,0,1,3:T(2,128)S(1)} all-gather(f32[2,3,48,96]{2,0,1,3:T(2,128)S(1)} %bitcast.161), channel_id=1, replica_groups=mesh['wide'=8,'narrow'=4] {'narrow'}, dimensions={3}, use_global_device_ids=true | all-gather | bytes 552960 | tf_op jit(solution)/shard_map/all_gather | solution.py:194
  197.3 2.6 fusion.20
  202.0 2.6 fusion.21
  210.8 3.1 shard_map.87.series_ref
  215.4 4.2 %shard_map.78.series_ref = bf16[64,16,384]{2,1,0:T(8,128)(2,1)S(1)} custom-call(bf16[8,16,5632]{2,1,0:T(8,128)(2,1)} %all-to-all-done.recv_ref, bf16[704,768]{1,0:T(8,128)(2,1)S(1)} %copy-done.2), custom_call_target="tpu_custom_call" | custom-call | flops 1107296256 | bytes 2228224 | tf_op jit(solution)/shard_map/pallas_call | solution.py:90
  225.6 4.6 %copy.222 = bf16[64,16,384]{1,2,0:T(8,128)(2,1)} copy(bf16[64,16,384]{2,1,0:T(8,128)(2,1)S(1)} %shard_map.78.series_ref) | data formatting | bytes 1572864 | tf_op jit(solution)/shard_map/reshape | solution.py:234
  246.3 6.2 %shard_map.81.series_ref = bf16[64,32,384]{2,1,0:T(8,128)(2,1)S(1)} custom-call(bf16[8,32,5632]{2,1,0:T(8,128)(2,1)} %all-to-all-done.1.recv_ref, bf16[704,768]{1,0:T(8,128)(2,1)S(1)} %copy-done.3), custom_call_target="tpu_custom_call" | custom-call | flops 2214592512 | bytes 4456448 | tf_op jit(solution)/shard_map/pallas_call | solution.py:90
  252.5 4.5 %copy.223 = bf16[64,32,384]{1,2,0:T(8,128)(2,1)} copy(bf16[64,32,384]{2,1,0:T(8,128)(2,1)S(1)} %shard_map.81.series_ref) | data formatting | bytes 3145728 | tf_op jit(solution)/shard_map/reshape | solution.py:234
  257.8 6.2 %shard_map.84.series_ref = bf16[64,32,384]{2,1,0:T(8,128)(2,1)S(1)} custom-call(bf16[8,32,5632]{2,1,0:T(8,128)(2,1)} %all-to-all-done.2.recv_ref, bf16[704,768]{1,0:T(8,128)(2,1)S(1)} %copy-done.3), custom_call_target="tpu_custom_call" | custom-call | flops 2214592512 | bytes 4456448 | tf_op jit(solution)/shard_map/pallas_call | solution.py:90
  272.9 10.0 %all_gather.10 = bf16[48,4,4,256]{0,2,1,3:T(4,128)(2,1)S(1)} all-gather(bf16[48,4,4,64]{0,2,1,3:T(4,128)(2,1)S(1)} %maximum_bitcast_fusion), channel_id=1, replica_groups=mesh['wide'=8,'narrow'=4] {'narrow'}, dimensions={3}, use_global_device_ids=true | all-gather | bytes 491520 | tf_op jit(solution)/shard_map/all_gather | solution.py:237
  285.9 31.1 %all-gather = bf16[384,1,1,248]{3,0,2,1:T(8,128)(2,1)S(1)} all-gather(bf16[48,1,1,248]{3,0,2,1:T(8,128)(2,1)S(1)} %copy.220), channel_id=2, replica_groups=mesh['wide'=8,'narrow'=4] {'wide'}, dimensions={0}, use_global_device_ids=true | all-gather | bytes 214272 | tf_op jit(solution)/shard_map/all_gather | solution.py:244
  318.2 2.7 constant_dynamic-slice_fusion.9
  333.6 2.3 collective-permute-done.16
  (226 shorter events, 80.5 us)
Async XLA Ops:
  13.7 41.6 %all-to-all-start.3 = ((bf16[8,16,5632]{2,1,0:T(8,128)(2,1)}), bf16[8,16,5632]{2,1,0:T(8,128)(2,1)S(1)}, u32[]{:S(2)}, u32[]{:S(2)}) async-start(bf16[8,16,5632]{2,1,0:T(8,128)(2,1)} %bitcast.66), calls=%async_computation.3 | async-start | bytes 2883584 | tf_op jit(solution)/shard_map/all_to_all | solution.py:207
  55.3 38.1 %all-to-all-start = ((bf16[8,16,5632]{2,1,0:T(8,128)(2,1)}), bf16[8,16,5632]{2,1,0:T(8,128)(2,1)}, u32[]{:S(2)}, u32[]{:S(2)}) async-start(bf16[8,16,5632]{2,1,0:T(8,128)(2,1)} %bitcast.1), calls=%async_computation | async-start | bytes 2883584 | tf_op jit(solution)/shard_map/all_to_all | solution.py:207
  93.4 69.2 %all-to-all-start.1 = ((bf16[8,32,5632]{2,1,0:T(8,128)(2,1)}), bf16[8,32,5632]{2,1,0:T(8,128)(2,1)}, u32[]{:S(2)}, u32[]{:S(2)}) async-start(bf16[8,32,5632]{2,1,0:T(8,128)(2,1)} %bitcast.27), calls=%async_computation.1 | async-start | bytes 5767168 | tf_op jit(solution)/shard_map/all_to_all | solution.py:207
  162.6 95.2 %all-to-all-start.2 = ((bf16[8,32,5632]{2,1,0:T(8,128)(2,1)}), bf16[8,32,5632]{2,1,0:T(8,128)(2,1)}, u32[]{:S(2)}, u32[]{:S(2)}) async-start(bf16[8,32,5632]{2,1,0:T(8,128)(2,1)} %bitcast.47), calls=%async_computation.2 | async-start | bytes 5767168 | tf_op jit(solution)/shard_map/all_to_all | solution.py:207
  222.4 10.6 %collective-permute-start.20 = (f32[16,96]{1,0:T(8,128)S(1)}, f32[16,96]{1,0:T(8,128)S(1)}, u32[]{:S(2)}, u32[]{:S(2)}) collective-permute-start(f32[16,96]{1,0:T(8,128)S(1)} %bitcast.226), channel_id=1, source_target_pairs={{0,3},{1,2},{2,1},{3,0},{4,7},{5,6},{6,5},{7,4},{8,11},{9,10},{10,... | collective-permute-start | bytes 18440 | tf_op jit(solution)/shard_map/ppermute | solution.py:155
  222.9 10.3 %collective-permute-start.19 = (f32[16,96]{1,0:T(8,128)S(1)}, f32[16,96]{1,0:T(8,128)S(1)}, u32[]{:S(2)}, u32[]{:S(2)}) collective-permute-start(f32[16,96]{1,0:T(8,128)S(1)} %bitcast.225), channel_id=1, source_target_pairs={{0,2},{1,3},{2,0},{3,1},{4,6},{5,7},{6,4},{7,5},{8,10},{9,11},{10,... | collective-permute-start | bytes 18440 | tf_op jit(solution)/shard_map/ppermute | solution.py:155
  224.4 10.3 %collective-permute-start.18 = (f32[16,96]{1,0:T(8,128)S(1)}, f32[16,96]{1,0:T(8,128)S(1)}, u32[]{:S(2)}, u32[]{:S(2)}) collective-permute-start(f32[16,96]{1,0:T(8,128)S(1)} %bitcast.224), channel_id=1, source_target_pairs={{0,1},{1,0},{2,3},{3,2},{4,5},{5,4},{6,7},{7,6},{8,9},{9,8},{10,11... | collective-permute-start | bytes 18440 | tf_op jit(solution)/shard_map/ppermute | solution.py:155
  230.3 8.9 %collective-permute-start.4 = (bf16[16,16,96]{2,1,0:T(8,128)(2,1)S(1)}, bf16[16,16,96]{2,1,0:T(8,128)(2,1)S(1)}, u32[]{:S(2)}, u32[]{:S(2)}) collective-permute-start(bf16[16,16,96]{2,1,0:T(8,128)(2,1)S(1)} %bitcast.198), channel_id=1, source_target_pairs={{0,2},{1,3},{2,0},{3,1},{4,6},{5,7},{6,4},{7,5},{8,10},{9,11},{10,... | collective-permute-start | bytes 147464 | tf_op jit(solution)/shard_map/ppermute | solution.py:155
  230.9 9.1 %collective-permute-start.3 = (bf16[16,16,96]{2,1,0:T(8,128)(2,1)S(1)}, bf16[16,16,96]{2,1,0:T(8,128)(2,1)S(1)}, u32[]{:S(2)}, u32[]{:S(2)}) collective-permute-start(bf16[16,16,96]{2,1,0:T(8,128)(2,1)S(1)} %bitcast.197), channel_id=1, source_target_pairs={{0,1},{1,0},{2,3},{3,2},{4,5},{5,4},{6,7},{7,6},{8,9},{9,8},{10,11... | collective-permute-start | bytes 147464 | tf_op jit(solution)/shard_map/ppermute | solution.py:155
  235.4 4.6 %collective-permute-start.5 = (bf16[16,16,96]{2,1,0:T(8,128)(2,1)S(1)}, bf16[16,16,96]{2,1,0:T(8,128)(2,1)S(1)}, u32[]{:S(2)}, u32[]{:S(2)}) collective-permute-start(bf16[16,16,96]{2,1,0:T(8,128)(2,1)S(1)} %bitcast.196), channel_id=1, source_target_pairs={{0,3},{1,2},{2,1},{3,0},{4,7},{5,6},{6,5},{7,4},{8,11},{9,10},{10,... | collective-permute-start | bytes 147464 | tf_op jit(solution)/shard_map/ppermute | solution.py:155
  237.2 4.3 %collective-permute-start.23 = (bf16[16,16,96]{2,1,0:T(8,128)(2,1)S(1)}, bf16[16,16,96]{2,1,0:T(8,128)(2,1)S(1)}, u32[]{:S(2)}, u32[]{:S(2)}) collective-permute-start(bf16[16,16,96]{2,1,0:T(8,128)(2,1)S(1)} %bitcast.195), channel_id=1, source_target_pairs={{0,3},{1,2},{2,1},{3,0},{4,7},{5,6},{6,5},{7,4},{8,11},{9,10},{10,... | collective-permute-start | bytes 147464 | tf_op jit(solution)/shard_map/ppermute | solution.py:155
  239.2 4.3 %collective-permute-start.22 = (bf16[16,16,96]{2,1,0:T(8,128)(2,1)S(1)}, bf16[16,16,96]{2,1,0:T(8,128)(2,1)S(1)}, u32[]{:S(2)}, u32[]{:S(2)}) collective-permute-start(bf16[16,16,96]{2,1,0:T(8,128)(2,1)S(1)} %bitcast.193), channel_id=1, source_target_pairs={{0,2},{1,3},{2,0},{3,1},{4,6},{5,7},{6,4},{7,5},{8,10},{9,11},{10,... | collective-permute-start | bytes 147464 | tf_op jit(solution)/shard_map/ppermute | solution.py:155
  268.3 52.9 %collective-permute-start.14 = (f32[32,96]{1,0:T(8,128)S(1)}, f32[32,96]{1,0:T(8,128)S(1)}, u32[]{:S(2)}, u32[]{:S(2)}) collective-permute-start(f32[32,96]{1,0:T(8,128)S(1)} %bitcast.214), channel_id=1, source_target_pairs={{0,3},{1,2},{2,1},{3,0},{4,7},{5,6},{6,5},{7,4},{8,11},{9,10},{10,... | collective-permute-start | bytes 36872 | tf_op jit(solution)/shard_map/ppermute | solution.py:155
  268.4 52.9 %collective-permute-start.13 = (f32[32,96]{1,0:T(8,128)S(1)}, f32[32,96]{1,0:T(8,128)S(1)}, u32[]{:S(2)}, u32[]{:S(2)}) collective-permute-start(f32[32,96]{1,0:T(8,128)S(1)} %bitcast.213), channel_id=1, source_target_pairs={{0,2},{1,3},{2,0},{3,1},{4,6},{5,7},{6,4},{7,5},{8,10},{9,11},{10,... | collective-permute-start | bytes 36872 | tf_op jit(solution)/shard_map/ppermute | solution.py:155
  269.2 53.5 %collective-permute-start.12 = (f32[32,96]{1,0:T(8,128)S(1)}, f32[32,96]{1,0:T(8,128)S(1)}, u32[]{:S(2)}, u32[]{:S(2)}) collective-permute-start(f32[32,96]{1,0:T(8,128)S(1)} %bitcast.212), channel_id=1, source_target_pairs={{0,1},{1,0},{2,3},{3,2},{4,5},{5,4},{6,7},{7,6},{8,9},{9,8},{10,11... | collective-permute-start | bytes 36872 | tf_op jit(solution)/shard_map/ppermute | solution.py:155
  270.2 53.5 %collective-permute-start.6 = (f32[32,96]{1,0:T(8,128)S(1)}, f32[32,96]{1,0:T(8,128)S(1)}, u32[]{:S(2)}, u32[]{:S(2)}) collective-permute-start(f32[32,96]{1,0:T(8,128)S(1)} %bitcast.211), channel_id=1, source_target_pairs={{0,1},{1,0},{2,3},{3,2},{4,5},{5,4},{6,7},{7,6},{8,9},{9,8},{10,11... | collective-permute-start | bytes 36872 | tf_op jit(solution)/shard_map/ppermute | solution.py:155
  270.2 54.5 %collective-permute-start.7 = (f32[32,96]{1,0:T(8,128)S(1)}, f32[32,96]{1,0:T(8,128)S(1)}, u32[]{:S(2)}, u32[]{:S(2)}) collective-permute-start(f32[32,96]{1,0:T(8,128)S(1)} %bitcast.210), channel_id=1, source_target_pairs={{0,2},{1,3},{2,0},{3,1},{4,6},{5,7},{6,4},{7,5},{8,10},{9,11},{10,... | collective-permute-start | bytes 36872 | tf_op jit(solution)/shard_map/ppermute | solution.py:155
  321.2 4.3 %collective-permute-start.8 = (f32[32,96]{1,0:T(8,128)S(1)}, f32[32,96]{1,0:T(8,128)S(1)}, u32[]{:S(2)}, u32[]{:S(2)}) collective-permute-start(f32[32,96]{1,0:T(8,128)S(1)} %bitcast.209), channel_id=1, source_target_pairs={{0,3},{1,2},{2,1},{3,0},{4,7},{5,6},{6,5},{7,4},{8,11},{9,10},{10,... | collective-permute-start | bytes 36872 | tf_op jit(solution)/shard_map/ppermute | solution.py:155
  321.3 6.2 %collective-permute-start.10 = (bf16[16,32,96]{2,1,0:T(8,128)(2,1)S(1)}, bf16[16,32,96]{2,1,0:T(8,128)(2,1)S(1)}, u32[]{:S(2)}, u32[]{:S(2)}) collective-permute-start(bf16[16,32,96]{2,1,0:T(8,128)(2,1)S(1)} %bitcast.184), channel_id=1, source_target_pairs={{0,2},{1,3},{2,0},{3,1},{4,6},{5,7},{6,4},{7,5},{8,10},{9,11},{10,... | collective-permute-start | bytes 294920 | tf_op jit(solution)/shard_map/ppermute | solution.py:155
  322.7 6.4 %collective-permute-start.9 = (bf16[16,32,96]{2,1,0:T(8,128)(2,1)S(1)}, bf16[16,32,96]{2,1,0:T(8,128)(2,1)S(1)}, u32[]{:S(2)}, u32[]{:S(2)}) collective-permute-start(bf16[16,32,96]{2,1,0:T(8,128)(2,1)S(1)} %bitcast.183), channel_id=1, source_target_pairs={{0,1},{1,0},{2,3},{3,2},{4,5},{5,4},{6,7},{7,6},{8,9},{9,8},{10,11... | collective-permute-start | bytes 294920 | tf_op jit(solution)/shard_map/ppermute | solution.py:155
  323.7 7.1 %collective-permute-start.11 = (bf16[16,32,96]{2,1,0:T(8,128)(2,1)S(1)}, bf16[16,32,96]{2,1,0:T(8,128)(2,1)S(1)}, u32[]{:S(2)}, u32[]{:S(2)}) collective-permute-start(bf16[16,32,96]{2,1,0:T(8,128)(2,1)S(1)} %bitcast.182), channel_id=1, source_target_pairs={{0,3},{1,2},{2,1},{3,0},{4,7},{5,6},{6,5},{7,4},{8,11},{9,10},{10,... | collective-permute-start | bytes 294920 | tf_op jit(solution)/shard_map/ppermute | solution.py:155
  324.7 8.9 %collective-permute-start.17 = (bf16[16,32,96]{2,1,0:T(8,128)(2,1)S(1)}, bf16[16,32,96]{2,1,0:T(8,128)(2,1)S(1)}, u32[]{:S(2)}, u32[]{:S(2)}) collective-permute-start(bf16[16,32,96]{2,1,0:T(8,128)(2,1)S(1)} %bitcast.181), channel_id=1, source_target_pairs={{0,3},{1,2},{2,1},{3,0},{4,7},{5,6},{6,5},{7,4},{8,11},{9,10},{10,... | collective-permute-start | bytes 294920 | tf_op jit(solution)/shard_map/ppermute | solution.py:155
  325.5 8.1 %collective-permute-start.15 = (bf16[16,32,96]{2,1,0:T(8,128)(2,1)S(1)}, bf16[16,32,96]{2,1,0:T(8,128)(2,1)S(1)}, u32[]{:S(2)}, u32[]{:S(2)}) collective-permute-start(bf16[16,32,96]{2,1,0:T(8,128)(2,1)S(1)} %bitcast.180), channel_id=1, source_target_pairs={{0,1},{1,0},{2,3},{3,2},{4,5},{5,4},{6,7},{7,6},{8,9},{9,8},{10,11... | collective-permute-start | bytes 294920 | tf_op jit(solution)/shard_map/ppermute | solution.py:155
  327.5 8.4 %collective-permute-start.16 = (bf16[16,32,96]{2,1,0:T(8,128)(2,1)S(1)}, bf16[16,32,96]{2,1,0:T(8,128)(2,1)S(1)}, u32[]{:S(2)}, u32[]{:S(2)}) collective-permute-start(bf16[16,32,96]{2,1,0:T(8,128)(2,1)S(1)} %bitcast.179), channel_id=1, source_target_pairs={{0,2},{1,3},{2,0},{3,1},{4,6},{5,7},{6,4},{7,5},{8,10},{9,11},{10,... | collective-permute-start | bytes 294920 | tf_op jit(solution)/shard_map/ppermute | solution.py:155
  (29 other events, 143.3 us)

commit v2 on v0

v2 whole, which is shorter than its diff:
```python
import functools
import math

import jax
import jax.numpy as jnp
import numpy as np
from jax import lax
from jax.experimental import pallas as pl
from jax.experimental.pallas import tpu as pltpu
from jax.sharding import PartitionSpec as P

LAGMAX = 8
ROW_DEG = 3
VMEM = 48 * 2**20


def dft_columns(orders, longitudes):
    turns = np.arange(longitudes)[:, None] * np.arange(orders)[None, :] % longitudes
    angle = turns * (2.0 * np.pi / longitudes)
    scale = 1.0 / math.sqrt(longitudes)
    return [(np.cos(angle) * scale).astype(jnp.bfloat16), (-np.sin(angle) * scale).astype(jnp.bfloat16)]


def lat_columns(degrees, latitudes):
    degree = np.arange(degrees)[None, :]
    odd_lat = 2 * np.arange(latitudes)[:, None] + 1
    period = 4 * latitudes
    unit = np.pi / (2 * latitudes)
    scale = math.sqrt(2.0 / latitudes)
    cosines = np.cos(degree * odd_lat % period * unit) * scale
    sines = np.sin((degree + 1) * odd_lat % period * unit) * scale
    return np.concatenate([cosines, sines], axis=1).astype(jnp.bfloat16)


ANY = pl.BlockSpec(memory_space=pl.ANY)
IN_VMEM = pl.BlockSpec(memory_space=pltpu.VMEM)
IN_SMEM = pl.BlockSpec(memory_space=pltpu.SMEM)


def spectra_kernel(field_ref, table_ref, *refs):
    out_ref = refs[-1]
    cells = jnp.dot(field_ref[...], table_ref[...], preferred_element_type=jnp.float32)
    out_ref[...] = cells.T.astype(jnp.bfloat16)


def spectra_of(fields, table, block, after):
    cells, lon_count = fields.shape
    rows = table.shape[1]
    return pl.pallas_call(
        spectra_kernel,
        grid=(cells // block,),
        in_specs=[
            pl.BlockSpec((block, lon_count), lambda i: (i, 0)),
            pl.BlockSpec((lon_count, rows), lambda i: (0, 0)),
        ]
        + [ANY] * len(after),
        out_specs=pl.BlockSpec((rows, block), lambda i: (0, i)),
        out_shape=jax.ShapeDtypeStruct((rows, cells), jnp.bfloat16),
        compiler_params=pltpu.CompilerParams(vmem_limit_bytes=VMEM),
        cost_estimate=pl.CostEstimate(
            flops=2 * rows * cells * lon_count,
            bytes_accessed=2 * (cells * lon_count + rows * cells + rows * lon_count),
            transcendentals=0,
        ),
    )(fields, table, *after)


def peer(me, hop, count):
    if count & (count - 1) == 0:
        return me ^ hop, me ^ hop
    return (me + hop) % count, (me - hop + count) % count


def digest_kernel(shape, lag_ref, me_ref, recv_ref, lat_ref, weight_ref, *refs):
    narrow_count, lat_local, n_after = shape
    sends, pick_ref = refs[n_after : n_after + narrow_count], refs[n_after + narrow_count]
    line_ref, series_ref, block_ref = refs[n_after + narrow_count + 1 :]
    sources, slots, _ = recv_ref.shape
    days, _, degrees = series_ref.shape
    half, padded = slots // 2, line_ref.shape[1] // 2
    for day in range(days):
        for source in range(sources):
            block = recv_ref[source, :, day * lat_local : (day + 1) * lat_local]
            lats = slice(source * lat_local, (source + 1) * lat_local)
            if half == padded:
                line_ref[day, :, lats] = block
            else:
                line_ref[day, :half, lats] = block[:half]
                line_ref[day, padded : padded + half, lats] = block[half:]
    for parity in range(2):
        lines = line_ref[:, parity * padded : (parity + 1) * padded, :]
        coeffs = jnp.dot(
            lines.reshape(days * padded, sources * lat_local),
            lat_ref[:, parity * degrees : (parity + 1) * degrees],
            preferred_element_type=jnp.float32,
        )
        coeffs = coeffs.astype(jnp.bfloat16).reshape(days, padded, degrees)
        series_ref[:, parity * half : (parity + 1) * half, :] = coeffs[:, :half]

    step = 16 if slots % 16 == 0 else slots
    lags = [lag_ref[i] for i in range(3)]
    deg_local = degrees // narrow_count
    for first in range(0, slots, step):
        rows = pl.ds(first, step)
        weights = [weight_ref[i, rows, :] for i in range(3)]

        def add_day(day, total):
            residual = series_ref[day, rows, :].astype(jnp.float32)
            for lag, weight in zip(lags, weights):
                residual = residual - weight * series_ref[day - lag, rows, :].astype(jnp.float32)
            return total + residual * residual

        total = lax.fori_loop(
            LAGMAX, days, add_day, jnp.zeros((step, degrees), jnp.float32), unroll=4
        )
        coarse = total.astype(jnp.bfloat16)
        fine = (total - coarse.astype(jnp.float32)).astype(jnp.bfloat16)
        for owner in range(narrow_count):
            own = slice(owner * deg_local, (owner + 1) * deg_local)
            block_ref[owner, :LAGMAX, rows, :] = series_ref[:LAGMAX, rows, own]
            block_ref[owner, LAGMAX : 2 * LAGMAX, rows, :] = series_ref[days - LAGMAX :, rows, own]
            block_ref[owner, 2 * LAGMAX, rows, :] = coarse[:, own]
            block_ref[owner, 2 * LAGMAX + 1, rows, :] = fine[:, own]
    for owner in range(narrow_count):
        kept = slice(owner * (ROW_DEG + 1), (owner + 1) * (ROW_DEG + 1))
        first = owner * deg_local
        pick_ref[:, :, kept] = series_ref[:, :, first : first + ROW_DEG + 1]
    me = me_ref[0]
    for hop, send in enumerate(sends):
        send[...] = block_ref[peer(me, hop, narrow_count)[0]]


def digest(lag_days, me, received, lat_table, weights, days_local, narrow_count, after):
    sources, slots, cells = received.shape
    latitudes, degrees = lat_table.shape[0], lat_table.shape[1] // 2
    lat_local = latitudes // sources
    deg_local = degrees // narrow_count
    padded = 2 * (-(-(slots // 2) // 8) * 8)
    message = (2 * LAGMAX + 2, slots, deg_local)
    picked = (days_local, slots, narrow_count * (ROW_DEG + 1))
    return pl.pallas_call(
        functools.partial(digest_kernel, (narrow_count, lat_local, len(after))),
        in_specs=[IN_SMEM, IN_SMEM, IN_VMEM, IN_VMEM, IN_VMEM] + [ANY] * len(after),
        out_specs=[IN_VMEM] * (narrow_count + 1),
        out_shape=[jax.ShapeDtypeStruct(message, jnp.bfloat16)] * narrow_count
        + [jax.ShapeDtypeStruct(picked, jnp.bfloat16)],
        scratch_shapes=[
            pltpu.VMEM((days_local, padded, latitudes), jnp.bfloat16),
            pltpu.VMEM((days_local, slots, degrees), jnp.bfloat16),
            pltpu.VMEM((narrow_count,) + message, jnp.bfloat16),
        ],
        compiler_params=pltpu.CompilerParams(vmem_limit_bytes=VMEM),
        cost_estimate=pl.CostEstimate(
            flops=4 * slots * cells * sources * degrees,
            bytes_accessed=2 * (sources * slots * cells + days_local * slots * degrees),
            transcendentals=0,
        ),
    )(lag_days, me, received, lat_table, weights, *after)


def combine_kernel(count, lag_ref, me_ref, weight_ref, *refs):
    got, out_ref, seam_ref, sum_ref = refs[:count], refs[count], refs[count + 1], refs[count + 2]
    me = me_ref[0]
    total = jnp.zeros(out_ref.shape, jnp.float32)
    for hop in range(count):
        source = peer(me, hop, count)[1]
        seam_ref[source, LAGMAX:] = got[hop][:LAGMAX]
        seam_ref[source + 1, :LAGMAX] = got[hop][LAGMAX : 2 * LAGMAX]
        sums = got[hop][2 * LAGMAX :].astype(jnp.float32)
        sum_ref[source] = sums[0] + sums[1]
    for source in range(count):
        total = total + sum_ref[source]
    lags = [lag_ref[i] for i in range(3)]
    weights = [weight_ref[i] for i in range(3)]
    for block in range(1, count):
        for day in range(LAGMAX, 2 * LAGMAX):
            residual = seam_ref[block, day].astype(jnp.float32)
            for lag, weight in zip(lags, weights):
                residual = residual - weight * seam_ref[block, day - lag].astype(jnp.float32)
            total = total + residual * residual
    out_ref[...] = total


def combine(lag_days, me, weights, got):
    count = len(got)
    days, slots, degrees = got[0].shape
    return pl.pallas_call(
        functools.partial(combine_kernel, count),
        in_specs=[IN_SMEM, IN_SMEM] + [IN_VMEM] * (count + 1),
        out_specs=IN_VMEM,
        out_shape=jax.ShapeDtypeStruct((slots, degrees), jnp.float32),
        scratch_shapes=[
            pltpu.VMEM((count + 1, 2 * LAGMAX, slots, degrees), jnp.bfloat16),
            pltpu.VMEM((count, slots, degrees), jnp.float32),
        ],
        compiler_params=pltpu.CompilerParams(vmem_limit_bytes=VMEM),
        cost_estimate=pl.CostEstimate(
            flops=8 * count * LAGMAX * slots * degrees,
            bytes_accessed=2 * count * days * slots * degrees,
            transcendentals=0,
        ),
    )(lag_days, me, weights, *got)


def swap(sends, axis):
    count = lax.axis_size(axis)
    return [sends[0]] + [
        lax.ppermute(sends[hop], axis, [(i, peer(i, hop, count)[0]) for i in range(count)])
        for hop in range(1, count)
    ]


def by_source(got, axis):
    count = lax.axis_size(axis)
    me = lax.axis_index(axis)
    hops = jnp.arange(count, dtype=jnp.int32)
    hops = hops ^ me if count & (count - 1) == 0 else (me - hops + count) % count
    return jnp.take(jnp.stack(got), hops, axis=0)


def segments_of(slot_local):
    pairs = slot_local // 2
    if slot_local % 48 == 0:
        cut = pairs * 2 // 3
        return [[(0, 0, cut)], [(0, cut, pairs), (1, 0, cut)], [(1, cut, pairs)]]
    return [[(0, 0, pairs)], [(1, 0, pairs)]]


def body(daily_fields, order_table, lag_days, lag_weights):
    wide_count = lax.axis_size("wide")
    narrow_count = lax.axis_size("narrow")
    days_local, lat_local, lon_count = daily_fields.shape
    order_count = order_table.shape[0]
    slot_local = order_count // wide_count
    pair_local = slot_local // 2
    deg_local = lag_weights.shape[1]
    deg_count = deg_local * narrow_count
    kept_days = days_local * narrow_count - LAGMAX
    day_block = math.gcd(128 // math.gcd(128, lat_local), days_local)
    me = lax.axis_index("narrow").astype(jnp.int32).reshape(1)

    fields = daily_fields.reshape(days_local * lat_local, lon_count)
    parts = [jnp.asarray(p) for p in dft_columns(order_count, lon_count)]
    lat_table = jnp.asarray(lat_columns(deg_count, lat_local * wide_count))
    by_owner = order_table.reshape(wide_count, pair_local, 2)
    every_order = jnp.arange(order_count, dtype=jnp.int32)[:, None]

    def table_of(segments):
        columns = []
        for parity in range(2):
            for part, first, last in segments:
                orders = by_owner[:, first:last, parity]
                columns.append((part, orders))
        picks = []
        for part in range(2):
            if any(p == part for p, _ in columns):
                chosen = jnp.concatenate(
                    [orders if p == part else jnp.full_like(orders, -1) for p, orders in columns], axis=1
                ).reshape(1, -1)
                picks.append(
                    jnp.dot(
                        parts[part],
                        (every_order == chosen).astype(jnp.bfloat16),
                        preferred_element_type=jnp.float32,
                    )
                )
        return sum(picks[1:], picks[0]).astype(jnp.bfloat16)

    own_weights = jnp.transpose(
        lag_weights.reshape(3, deg_local, pair_local, 2, 2), (4, 3, 0, 2, 1)
    )
    all_weights = by_source(swap([own_weights] * narrow_count, "narrow"), "narrow")
    all_weights = jnp.moveaxis(all_weights, 0, 4).reshape(2, 2, 3, pair_local, deg_count)

    def rows_of(weights, segments):
        return jnp.concatenate(
            [weights[p, parity, :, a:b] for parity in range(2) for p, a, b in segments], axis=1
        )

    plan = segments_of(slot_local)
    spreads = {}
    picked = {}
    results = []
    received = []
    panel = None

    def exchange(segments, after):
        spectra = spectra_of(fields, table_of(segments), day_block * lat_local, after)
        spectra = spectra.reshape(wide_count, -1, days_local * lat_local)
        return lax.all_to_all(spectra, "wide", split_axis=0, concat_axis=0, tiled=True)

    def finish(segments, received, after):
        *sends, picks = digest(
            lag_days,
            me,
            received,
            lat_table,
            rows_of(all_weights, segments),
            days_local,
            narrow_count,
            after,
        )
        total = combine(lag_days, me, rows_of(own_weights, segments), swap(sends, "narrow"))
        at = 0
        for parity in range(2):
            for part, first, last in segments:
                rows = slice(at, at + last - first)
                spreads[part, parity, first] = total[rows]
                if part == 0:
                    picked[parity, first] = picks[:, rows]
                at += last - first
        return total

    def panel_of():
        series = jnp.stack(
            [
                jnp.concatenate([picked[k] for k in sorted(picked) if k[0] == parity], axis=1)
                for parity in range(2)
            ],
            axis=2,
        )
        series = series.reshape(days_local, slot_local, narrow_count * (ROW_DEG + 1))
        series = jnp.transpose(series, (1, 2, 0))
        series = by_source(swap([series] * narrow_count, "narrow"), "narrow")
        series = jnp.moveaxis(series, 0, 2).reshape(
            slot_local, narrow_count, ROW_DEG + 1, days_local * narrow_count
        )
        weights = all_weights[0].reshape(2, 3, pair_local, narrow_count, deg_local)
        weights = jnp.transpose(weights[..., : ROW_DEG + 1], (1, 2, 0, 3, 4)).reshape(
            3, slot_local, narrow_count, ROW_DEG + 1, 1
        )
        residual = series[..., LAGMAX:].astype(jnp.float32)
        for position in range(3):
            shifted = lax.dynamic_slice_in_dim(series, LAGMAX - lag_days[position], kept_days, axis=3)
            residual = residual - weights[position] * shifted.astype(jnp.float32)
        rounded = residual.astype(jnp.bfloat16)
        rows = rounded[:, :, :ROW_DEG].reshape(slot_local, narrow_count * ROW_DEG, kept_days)
        column = lax.dynamic_index_in_dim(rounded[:, :, ROW_DEG], me[0], 1, False)
        columns = by_source(swap([column] * wide_count, "wide"), "wide")
        columns = columns.reshape(order_count, kept_days)
        product = lax.dot_general(
            rows, columns, (((2,), (1,)), ((), ())), preferred_element_type=jnp.float32
        )
        return product / math.sqrt(kept_days)

    for index, segments in enumerate(plan):
        if index >= 2:
            results.append(finish(plan[index - 2], received[index - 2], results[-1:]))
        received.append(exchange(segments, results[-1:]))
    results.append(finish(plan[-2], received[-2], results[-1:]))
    panel = panel_of()
    finish(plan[-1], received[-1], results[-1:] + [panel])

    spread = jnp.stack(
        [
            jnp.stack(
                [
                    jnp.concatenate(
                        [spreads[k] for k in sorted(spreads) if k[:2] == (part, parity)], axis=0
                    )
                    for part in range(2)
                ]
            )
            for parity in range(2)
        ]
    )
    noise_variance = jnp.transpose(spread / kept_days, (3, 2, 0, 1)).reshape(deg_local, slot_local, 2)
    return (noise_variance, panel)


def solution(mesh):
    placed = (P("narrow", "wide", None), P(), P(), P(None, "narrow", "wide", None))
    return jax.shard_map(
        body,
        mesh=mesh,
        in_specs=placed,
        out_specs=(P("narrow", "wide", None), P("wide", None, "narrow")),
        check_vma=False,
    )
```

time: 480 us -> 275 us (0.57)
  waiting for transfers between devices: 229 us -> 127 us
  local copies, waits for them, and re-layouts: 120 us -> 29.1 us
  Pallas kernels: 0 us -> 54.8 us
  blocking collectives: 36.6 us -> 0 us
  other arithmetic: 44.7 us -> 10.5 us
  starting transfers between devices: 12.6 us -> 41 us
  matrix products: 31.7 us -> 6.95 us
    all_to_all x2 -> x3, waiting for transfers between devices: 229 us -> 95 us  [exchange(): lax.all_to_all(spectra, 'wide', split_axis=0, concat_axis=0, tiled=True)]
    reshape x5 -> x3, local copies, waits for them, and re-layouts: 67.5 us -> 3.42 us  [the longest x1 2.12 us: body(): jnp.moveaxis(all_weights, 0, 4).reshape(2, 2, 3, pair_local, deg_count)]
    pallas_call x0 -> x9, Pallas kernels: none -> 54.8 us  [the longest x3 32.3 us: spectra_of(): pl.pallas_call(spectra_kernel, grid=(cells // block,), in_specs=[pl.Block...]
    all_gather x2 -> x0, blocking collectives: 36.6 us -> none  [the longest x1 30.7 us: body(): lax.all_gather(column_part, 'wide', axis=0, tiled=True)]
    ppermute x0 -> x22, waiting for transfers between devices: none -> 31.9 us  [swap(): lax.ppermute(sends[hop], axis, [(i, peer(i, hop, count)[0]) for i in rang...]
    ppermute x0 -> x22, starting transfers between devices: none -> 25.2 us  [swap(): lax.ppermute(sends[hop], axis, [(i, peer(i, hop, count)[0]) for i in rang...]
    dot_general x3 -> x5, matrix products: 31.7 us -> 6.95 us  [the longest x4 6.61 us: table_of(): jnp.dot(parts[part], (every_order == chosen).astype(jnp.bfloat16), prefer...]
    convert_element_type x2 -> x0, local copies, waits for them, and re-layouts: 18.8 us -> none  [the longest x1 15.9 us: body(): spectra.astype(jnp.bfloat16).reshape(M // 2, 4, days_local * lat_local)]
  transfers between devices with their start and end apart: 2 -> 25, of which waited for: 2 -> 11; matrix products, arithmetic and copies ran while one was open for 2% -> 13% of each run, Pallas kernels for 0% -> 11%
where the time goes in v2:
time: 275 us; the launch traced here: 274 us
  waiting for transfers between devices  127 us (46%)
  Pallas kernels  54.8 us (20%)
  starting transfers between devices  41 us (15%)
  local copies, waits for them, and re-layouts  29.1 us (11%)
  other arithmetic  10.5 us (4%)
  matrix products  6.95 us (3%)
  between operations  5.06 us (2%)
    all_to_all x3, waiting for transfers between devices, exchange(): lax.all_to_all(spectra, 'wide', split_axis=0, concat_axis=0, tiled=True)  95 us
    pallas_call x3, Pallas kernels, spectra_of(): pl.pallas_call(spectra_kernel, grid=(cells // block,), in_specs=[pl.Block...  32.3 us
    ppermute x22, waiting for transfers between devices, swap(): lax.ppermute(sends[hop], axis, [(i, peer(i, hop, count)[0]) for i in rang...  31.9 us
    ppermute x22, starting transfers between devices, swap(): lax.ppermute(sends[hop], axis, [(i, peer(i, hop, count)[0]) for i in rang...  25.2 us
    pallas_call x3, Pallas kernels, digest(): pl.pallas_call(functools.partial(digest_kernel, (narrow_count, lat_local,...  19.7 us
    all_to_all x3, starting transfers between devices, exchange(): lax.all_to_all(spectra, 'wide', split_axis=0, concat_axis=0, tiled=True)  15.7 us
    unnamed x57, local copies, waits for them, and re-layouts  7.68 us
    dot_general x4, matrix products, table_of(): jnp.dot(parts[part], (every_order == chosen).astype(jnp.bfloat16), prefer...  6.61 us
  transfers between devices with their start and end apart: 25, of which 11 were waited for; matrix products, arithmetic and copies ran while one was open for 13% of the time, Pallas kernels for 11%

profile of v2, /device:TPU:0, one launch (start us, length us, event | category | flops | bytes accessed | tf_op | source)
XLA Modules:
  0.0 274.3 jit_solution(4899448415892255065)
XLA Ops:
  3.8 10.1 %shard_map.86 = bf16[256,5632]{1,0:T(8,128)(2,1)} custom-call(bf16[5632,1440]{1,0:T(8,128)(2,1)} %bitcast.136, bf16[1440,256]{1,0:T(8,128)(2,1)S(1)} %fusion.2.table_ref), custom_call_target="tpu_custom_call" | custom-call | flops 4152360960 | bytes 19841024 | tf_op jit(solution)/shard_map/pallas_call | solution.py:49
  14.0 7.3 %all-to-all-start = ((bf16[8,32,5632]{2,1,0:T(8,128)(2,1)}), bf16[8,32,5632]{2,1,0:T(8,128)(2,1)S(1)}, u32[]{:S(2)}, u32[]{:S(2)}) async-start(bf16[8,32,5632]{2,1,0:T(8,128)(2,1)} %bitcast.7), calls=%async_computation | async-start | bytes 5767168 | tf_op jit(solution)/shard_map/all_to_all | solution.py:290
  22.0 2.2 fusion.4
  25.1 12.5 %shard_map.89 = bf16[384,5632]{1,0:T(8,128)(2,1)S(1)} custom-call(bf16[5632,1440]{1,0:T(8,128)(2,1)} %bitcast.137, bf16[1440,384]{1,0:T(8,128)(2,1)S(1)} %fusion.1.table_ref), custom_call_target="tpu_custom_call" | custom-call | flops 6228541440 | bytes 21651456 | tf_op jit(solution)/shard_map/pallas_call | solution.py:49
  37.6 2.1 copy-done
  39.6 46.7 %all-to-all-done.recv_ref = bf16[8,32,5632]{2,1,0:T(8,128)(2,1)S(1)} async-done(((bf16[8,32,5632]{2,1,0:T(8,128)(2,1)}), bf16[8,32,5632]{2,1,0:T(8,128)(2,1)S(1)}, u32[]{:S(2)}, u32[]{:S(2)}) %all-to-all-start) | async-done | bytes 2883616 | tf_op jit(solution)/shard_map/all_to_all | solution.py:290
  86.3 4.9 %all-to-all-start.1 = ((bf16[8,48,5632]{2,1,0:T(8,128)(2,1)}), bf16[8,48,5632]{2,1,0:T(8,128)(2,1)}, u32[]{:S(2)}, u32[]{:S(2)}) async-start(bf16[8,48,5632]{2,1,0:T(8,128)(2,1)} %bitcast.135), calls=%async_computation.1 | async-start | bytes 8650752 | tf_op jit(solution)/shard_map/all_to_all | solution.py:290
  104.2 2.5 gather_fusion
  109.8 2.1 reshape.155
  120.9 5.7 %shard_map.87 = (bf16[18,32,96]{2,1,0:T(8,128)(2,1)S(1)}, bf16[18,32,96]{2,1,0:T(8,128)(2,1)}, bf16[18,32,96]{2,1,0:T(8,128)(2,1)}, bf16[18,32,96]{2,1,0:T(8,128)(2,1)}, bf16[64,32,16]{2,1,0:T(8,128)(2,1)S(1)}) custom-call(s32[3]{0:T(128)S(1)} %copy-done.6, s32[1]{0:T(128)} %bitcast.me_ref, bf16[8,32,5632]{2,1,0:T(8,128)(2,1)S(1)} %all-to-all-done.recv_ref, ...), custom_call_target="tpu_custom_call" | custom-call | flops 2214592512 | bytes 4456448 | tf_op jit(solution)/shard_map/pallas_call | solution.py:141
  129.1 4.5 %collective-permute-done.4.refs_2_ = bf16[18,32,96]{2,1,0:T(8,128)(2,1)S(1)} collective-permute-done((bf16[18,32,96]{2,1,0:T(8,128)(2,1)}, bf16[18,32,96]{2,1,0:T(8,128)(2,1)S(1)}, u32[]{:S(2)}, u32[]{:S(2)}) %collective-permute-start.4) | collective-permute-done | bytes 110624 | tf_op jit(solution)/shard_map/ppermute | solution.py:208
  133.6 2.3 collective-permute-done.5.refs_3_
  138.2 48.3 %all-to-all-done.1.recv_ref = bf16[8,48,5632]{2,1,0:T(8,128)(2,1)} async-done(((bf16[8,48,5632]{2,1,0:T(8,128)(2,1)}), bf16[8,48,5632]{2,1,0:T(8,128)(2,1)}, u32[]{:S(2)}, u32[]{:S(2)}) %all-to-all-start.1) | async-done | bytes 4325408 | tf_op jit(solution)/shard_map/all_to_all | solution.py:290
  186.5 10.0 %shard_map.90 = (bf16[18,48,96]{2,1,0:T(8,128)(2,1)S(1)}, bf16[18,48,96]{2,1,0:T(8,128)(2,1)}, bf16[18,48,96]{2,1,0:T(8,128)(2,1)}, bf16[18,48,96]{2,1,0:T(8,128)(2,1)}, bf16[64,48,16]{2,1,0:T(8,128)(2,1)S(1)}) custom-call(s32[3]{0:T(128)S(1)} %copy-done.6, s32[1]{0:T(128)} %bitcast.me_ref, bf16[8,48,5632]{2,1,0:T(8,128)(2,1)} %all-to-all-done.1.recv_ref, ...), custom_call_target="tpu_custom_call" | custom-call | flops 3321888768 | bytes 6684672 | tf_op jit(solution)/shard_map/pallas_call | solution.py:141
  198.8 9.7 %shard_map.92 = bf16[128,5632]{1,0:T(8,128)(2,1)} custom-call(bf16[5632,1440]{1,0:T(8,128)(2,1)} %bitcast.138, bf16[1440,128]{1,0:T(8,128)(2,1)S(1)} %fusion.3.table_ref, f32[32,96]{1,0:T(8,128)S(1)} %shard_map.88.refs_0_), custom_call_target="tpu_custom_call" | custom-call | flops 2076180480 | bytes 18030592 | tf_op jit(solution)/shard_map/pallas_call | solution.py:49
  208.5 3.6 %all-to-all-start.2 = ((bf16[8,16,5632]{2,1,0:T(8,128)(2,1)}), bf16[8,16,5632]{2,1,0:T(8,128)(2,1)S(1)}, u32[]{:S(2)}, u32[]{:S(2)}) async-start(bf16[8,16,5632]{2,1,0:T(8,128)(2,1)} %bitcast.30), calls=%async_computation.2 | async-start | bytes 2883584 | tf_op jit(solution)/shard_map/all_to_all | solution.py:290
  226.0 2.7 collective-permute-start.14
  228.7 9.5 %collective-permute-done.13 = bf16[48,248]{1,0:T(8,128)(2,1)S(1)} collective-permute-done((bf16[48,248]{1,0:T(8,128)(2,1)S(1)}, bf16[48,248]{1,0:T(8,128)(2,1)S(1)}, u32[]{:S(2)}, u32[]{:S(2)}) %collective-permute-start.13) | collective-permute-done | bytes 23840 | tf_op jit(solution)/shard_map/ppermute | solution.py:208
  238.2 3.4 %collective-permute-start.15 = (bf16[48,248]{1,0:T(8,128)(2,1)S(1)}, bf16[48,248]{1,0:T(8,128)(2,1)S(1)}, u32[]{:S(2)}, u32[]{:S(2)}) collective-permute-start(bf16[48,248]{1,0:T(8,128)(2,1)S(1)} %dynamic-slice_bitcast_fusion), channel_id=1, source_target_pairs={{0,16},{4,20},{8,24},{12,28},{16,0},{20,4},{24,8},{28,12},{1,17},{... | collective-permute-start | bytes 71432 | tf_op jit(solution)/shard_map/ppermute | solution.py:208
  242.8 6.0 %collective-permute-done.15 = bf16[48,248]{1,0:T(8,128)(2,1)S(1)} collective-permute-done((bf16[48,248]{1,0:T(8,128)(2,1)S(1)}, bf16[48,248]{1,0:T(8,128)(2,1)S(1)}, u32[]{:S(2)}, u32[]{:S(2)}) %collective-permute-start.15) | collective-permute-done | bytes 23840 | tf_op jit(solution)/shard_map/ppermute | solution.py:208
  250.9 2.6 collective-permute-start.18
  254.5 2.9 %collective-permute-done.18 = bf16[48,248]{1,0:T(8,128)(2,1)S(1)} collective-permute-done((bf16[48,248]{1,0:T(8,128)(2,1)S(1)}, bf16[48,248]{1,0:T(8,128)(2,1)S(1)}, u32[]{:S(2)}, u32[]{:S(2)}) %collective-permute-start.18) | collective-permute-done | bytes 23840 | tf_op jit(solution)/shard_map/ppermute | solution.py:208
  262.8 4.0 %shard_map.93 = (bf16[18,16,96]{2,1,0:T(8,128)(2,1)S(1)}, bf16[18,16,96]{2,1,0:T(8,128)(2,1)S(1)}, bf16[18,16,96]{2,1,0:T(8,128)(2,1)S(1)}, bf16[18,16,96]{2,1,0:T(8,128)(2,1)S(1)}, bf16[64,16,16]{2,1,0:T(8,128)(2,1)}) custom-call(s32[3]{0:T(128)S(1)} %copy-done.6, s32[1]{0:T(128)} %bitcast.me_ref, bf16[8,16,5632]{2,1,0:T(8,128)(2,1)S(1)} %all-to-all-done.2.recv_ref, ...), custom_call_target="tpu_custom_call" | custom-call | flops 1107296256 | bytes 2228224 | tf_op jit(solution)/shard_map/pallas_call | solution.py:141
  268.7 3.0 %collective-permute-done.20.refs_2_ = bf16[18,16,96]{2,1,0:T(8,128)(2,1)S(1)} collective-permute-done((bf16[18,16,96]{2,1,0:T(8,128)(2,1)S(1)}, bf16[18,16,96]{2,1,0:T(8,128)(2,1)S(1)}, u32[]{:S(2)}, u32[]{:S(2)}) %collective-permute-start.20) | collective-permute-done | bytes 55328 | tf_op jit(solution)/shard_map/ppermute | solution.py:208
  (174 shorter events, 60.7 us)
Async XLA Ops:
  14.0 72.4 %all-to-all-start = ((bf16[8,32,5632]{2,1,0:T(8,128)(2,1)}), bf16[8,32,5632]{2,1,0:T(8,128)(2,1)S(1)}, u32[]{:S(2)}, u32[]{:S(2)}) async-start(bf16[8,32,5632]{2,1,0:T(8,128)(2,1)} %bitcast.7), calls=%async_computation | async-start | bytes 5767168 | tf_op jit(solution)/shard_map/all_to_all | solution.py:290
  86.3 100.1 %all-to-all-start.1 = ((bf16[8,48,5632]{2,1,0:T(8,128)(2,1)}), bf16[8,48,5632]{2,1,0:T(8,128)(2,1)}, u32[]{:S(2)}, u32[]{:S(2)}) async-start(bf16[8,48,5632]{2,1,0:T(8,128)(2,1)} %bitcast.135), calls=%async_computation.1 | async-start | bytes 8650752 | tf_op jit(solution)/shard_map/all_to_all | solution.py:290
  91.3 11.0 %collective-permute-start.1 = (f32[2,2,3,24,96]{4,3,2,1,0:T(8,128)S(1)}, f32[2,2,3,24,96]{4,3,2,1,0:T(8,128)}, u32[]{:S(2)}, u32[]{:S(2)}) collective-permute-start(f32[2,2,3,24,96]{4,3,2,1,0:T(8,128)S(1)} %bitcast.139), channel_id=1, source_target_pairs={{0,2},{1,3},{2,0},{3,1},{4,6},{5,7},{6,4},{7,5},{8,10},{9,11},{10,... | collective-permute-start | bytes 331784 | tf_op jit(solution)/shard_map/ppermute | solution.py:208
  92.8 9.4 %collective-permute-start.2 = (f32[2,2,3,24,96]{4,3,2,1,0:T(8,128)S(1)}, f32[2,2,3,24,96]{4,3,2,1,0:T(8,128)}, u32[]{:S(2)}, u32[]{:S(2)}) collective-permute-start(f32[2,2,3,24,96]{4,3,2,1,0:T(8,128)S(1)} %bitcast.140), channel_id=1, source_target_pairs={{0,3},{1,2},{2,1},{3,0},{4,7},{5,6},{6,5},{7,4},{8,11},{9,10},{10,... | collective-permute-start | bytes 331784 | tf_op jit(solution)/shard_map/ppermute | solution.py:208
  92.8 9.4 %collective-permute-start = (f32[2,2,3,24,96]{4,3,2,1,0:T(8,128)S(1)}, f32[2,2,3,24,96]{4,3,2,1,0:T(8,128)}, u32[]{:S(2)}, u32[]{:S(2)}) collective-permute-start(f32[2,2,3,24,96]{4,3,2,1,0:T(8,128)S(1)} %bitcast.141), channel_id=1, source_target_pairs={{0,1},{1,0},{2,3},{3,2},{4,5},{5,4},{6,7},{7,6},{8,9},{9,8},{10,11... | collective-permute-start | bytes 331784 | tf_op jit(solution)/shard_map/ppermute | solution.py:208
  126.6 2.5 collective-permute-start.3
  126.7 6.9 %collective-permute-start.4 = (bf16[18,32,96]{2,1,0:T(8,128)(2,1)}, bf16[18,32,96]{2,1,0:T(8,128)(2,1)S(1)}, u32[]{:S(2)}, u32[]{:S(2)}) collective-permute-start(bf16[18,32,96]{2,1,0:T(8,128)(2,1)} %get-tuple-element.18), channel_id=1, source_target_pairs={{0,2},{1,3},{2,0},{3,1},{4,6},{5,7},{6,4},{7,5},{8,10},{9,11},{10,... | collective-permute-start | bytes 331784 | tf_op jit(solution)/shard_map/ppermute | solution.py:208
  128.3 7.6 %collective-permute-start.5 = (bf16[18,32,96]{2,1,0:T(8,128)(2,1)}, bf16[18,32,96]{2,1,0:T(8,128)(2,1)S(1)}, u32[]{:S(2)}, u32[]{:S(2)}) collective-permute-start(bf16[18,32,96]{2,1,0:T(8,128)(2,1)} %get-tuple-element.19), channel_id=1, source_target_pairs={{0,3},{1,2},{2,1},{3,0},{4,7},{5,6},{6,5},{7,4},{8,11},{9,10},{10,... | collective-permute-start | bytes 331784 | tf_op jit(solution)/shard_map/ppermute | solution.py:208
  196.8 17.2 %collective-permute-start.9 = (bf16[48,16,64]{2,1,0:T(8,128)(2,1)S(1)}, bf16[48,16,64]{2,1,0:T(8,128)(2,1)S(1)}, u32[]{:S(2)}, u32[]{:S(2)}) collective-permute-start(bf16[48,16,64]{2,1,0:T(8,128)(2,1)S(1)} %bitcast.146), channel_id=1, source_target_pairs={{0,1},{1,0},{2,3},{3,2},{4,5},{5,4},{6,7},{7,6},{8,9},{9,8},{10,11... | collective-permute-start | bytes 294920 | tf_op jit(solution)/shard_map/ppermute | solution.py:208
  196.9 17.1 %collective-permute-start.10 = (bf16[48,16,64]{2,1,0:T(8,128)(2,1)S(1)}, bf16[48,16,64]{2,1,0:T(8,128)(2,1)S(1)}, u32[]{:S(2)}, u32[]{:S(2)}) collective-permute-start(bf16[48,16,64]{2,1,0:T(8,128)(2,1)S(1)} %bitcast.147), channel_id=1, source_target_pairs={{0,2},{1,3},{2,0},{3,1},{4,6},{5,7},{6,4},{7,5},{8,10},{9,11},{10,... | collective-permute-start | bytes 294920 | tf_op jit(solution)/shard_map/ppermute | solution.py:208
  198.5 15.6 %collective-permute-start.11 = (bf16[48,16,64]{2,1,0:T(8,128)(2,1)S(1)}, bf16[48,16,64]{2,1,0:T(8,128)(2,1)S(1)}, u32[]{:S(2)}, u32[]{:S(2)}) collective-permute-start(bf16[48,16,64]{2,1,0:T(8,128)(2,1)S(1)} %bitcast.148), channel_id=1, source_target_pairs={{0,3},{1,2},{2,1},{3,0},{4,7},{5,6},{6,5},{7,4},{8,11},{9,10},{10,... | collective-permute-start | bytes 294920 | tf_op jit(solution)/shard_map/ppermute | solution.py:208
  208.5 53.0 %all-to-all-start.2 = ((bf16[8,16,5632]{2,1,0:T(8,128)(2,1)}), bf16[8,16,5632]{2,1,0:T(8,128)(2,1)S(1)}, u32[]{:S(2)}, u32[]{:S(2)}) async-start(bf16[8,16,5632]{2,1,0:T(8,128)(2,1)} %bitcast.30), calls=%async_computation.2 | async-start | bytes 2883584 | tf_op jit(solution)/shard_map/all_to_all | solution.py:290
  212.1 48.0 %collective-permute-start.6 = (bf16[18,48,96]{2,1,0:T(8,128)(2,1)}, bf16[18,48,96]{2,1,0:T(8,128)(2,1)S(1)}, u32[]{:S(2)}, u32[]{:S(2)}) collective-permute-start(bf16[18,48,96]{2,1,0:T(8,128)(2,1)} %get-tuple-element.21), channel_id=1, source_target_pairs={{0,1},{1,0},{2,3},{3,2},{4,5},{5,4},{6,7},{7,6},{8,9},{9,8},{10,11... | collective-permute-start | bytes 497672 | tf_op jit(solution)/shard_map/ppermute | solution.py:208
  212.5 47.6 %collective-permute-start.7 = (bf16[18,48,96]{2,1,0:T(8,128)(2,1)}, bf16[18,48,96]{2,1,0:T(8,128)(2,1)S(1)}, u32[]{:S(2)}, u32[]{:S(2)}) collective-permute-start(bf16[18,48,96]{2,1,0:T(8,128)(2,1)} %get-tuple-element.22), channel_id=1, source_target_pairs={{0,2},{1,3},{2,0},{3,1},{4,6},{5,7},{6,4},{7,5},{8,10},{9,11},{10,... | collective-permute-start | bytes 497672 | tf_op jit(solution)/shard_map/ppermute | solution.py:208
  214.0 46.1 %collective-permute-start.8 = (bf16[18,48,96]{2,1,0:T(8,128)(2,1)}, bf16[18,48,96]{2,1,0:T(8,128)(2,1)}, u32[]{:S(2)}, u32[]{:S(2)}) collective-permute-start(bf16[18,48,96]{2,1,0:T(8,128)(2,1)} %get-tuple-element.23), channel_id=1, source_target_pairs={{0,3},{1,2},{2,1},{3,0},{4,7},{5,6},{6,5},{7,4},{8,11},{9,10},{10,... | collective-permute-start | bytes 497672 | tf_op jit(solution)/shard_map/ppermute | solution.py:208
  221.0 5.0 %collective-permute-start.12 = (bf16[48,248]{1,0:T(8,128)(2,1)S(1)}, bf16[48,248]{1,0:T(8,128)(2,1)S(1)}, u32[]{:S(2)}, u32[]{:S(2)}) collective-permute-start(bf16[48,248]{1,0:T(8,128)(2,1)S(1)} %dynamic-slice_bitcast_fusion), channel_id=1, source_target_pairs={{0,4},{4,0},{8,12},{12,8},{16,20},{20,16},{24,28},{28,24},{1,5},{5... | collective-permute-start | bytes 71432 | tf_op jit(solution)/shard_map/ppermute | solution.py:208
  223.0 15.2 %collective-permute-start.13 = (bf16[48,248]{1,0:T(8,128)(2,1)S(1)}, bf16[48,248]{1,0:T(8,128)(2,1)S(1)}, u32[]{:S(2)}, u32[]{:S(2)}) collective-permute-start(bf16[48,248]{1,0:T(8,128)(2,1)S(1)} %dynamic-slice_bitcast_fusion), channel_id=1, source_target_pairs={{0,8},{4,12},{8,0},{12,4},{16,24},{20,28},{24,16},{28,20},{1,9},{5... | collective-permute-start | bytes 71432 | tf_op jit(solution)/shard_map/ppermute | solution.py:208
  226.0 15.6 %collective-permute-start.14 = (bf16[48,248]{1,0:T(8,128)(2,1)S(1)}, bf16[48,248]{1,0:T(8,128)(2,1)S(1)}, u32[]{:S(2)}, u32[]{:S(2)}) collective-permute-start(bf16[48,248]{1,0:T(8,128)(2,1)S(1)} %dynamic-slice_bitcast_fusion), channel_id=1, source_target_pairs={{0,12},{4,8},{8,4},{12,0},{16,28},{20,24},{24,20},{28,16},{1,13},{... | collective-permute-start | bytes 71432 | tf_op jit(solution)/shard_map/ppermute | solution.py:208
  238.2 10.6 %collective-permute-start.15 = (bf16[48,248]{1,0:T(8,128)(2,1)S(1)}, bf16[48,248]{1,0:T(8,128)(2,1)S(1)}, u32[]{:S(2)}, u32[]{:S(2)}) collective-permute-start(bf16[48,248]{1,0:T(8,128)(2,1)S(1)} %dynamic-slice_bitcast_fusion), channel_id=1, source_target_pairs={{0,16},{4,20},{8,24},{12,28},{16,0},{20,4},{24,8},{28,12},{1,17},{... | collective-permute-start | bytes 71432 | tf_op jit(solution)/shard_map/ppermute | solution.py:208
  241.7 9.2 %collective-permute-start.16 = (bf16[48,248]{1,0:T(8,128)(2,1)S(1)}, bf16[48,248]{1,0:T(8,128)(2,1)S(1)}, u32[]{:S(2)}, u32[]{:S(2)}) collective-permute-start(bf16[48,248]{1,0:T(8,128)(2,1)S(1)} %dynamic-slice_bitcast_fusion), channel_id=1, source_target_pairs={{0,20},{4,16},{8,28},{12,24},{16,4},{20,0},{24,12},{28,8},{1,21},{... | collective-permute-start | bytes 71432 | tf_op jit(solution)/shard_map/ppermute | solution.py:208
  248.9 5.6 %collective-permute-start.17 = (bf16[48,248]{1,0:T(8,128)(2,1)S(1)}, bf16[48,248]{1,0:T(8,128)(2,1)S(1)}, u32[]{:S(2)}, u32[]{:S(2)}) collective-permute-start(bf16[48,248]{1,0:T(8,128)(2,1)S(1)} %dynamic-slice_bitcast_fusion), channel_id=1, source_target_pairs={{0,24},{4,28},{8,16},{12,20},{16,8},{20,12},{24,0},{28,4},{1,25},{... | collective-permute-start | bytes 71432 | tf_op jit(solution)/shard_map/ppermute | solution.py:208
  250.9 6.5 %collective-permute-start.18 = (bf16[48,248]{1,0:T(8,128)(2,1)S(1)}, bf16[48,248]{1,0:T(8,128)(2,1)S(1)}, u32[]{:S(2)}, u32[]{:S(2)}) collective-permute-start(bf16[48,248]{1,0:T(8,128)(2,1)S(1)} %dynamic-slice_bitcast_fusion), channel_id=1, source_target_pairs={{0,28},{4,24},{8,20},{12,16},{16,12},{20,8},{24,4},{28,0},{1,29},{... | collective-permute-start | bytes 71432 | tf_op jit(solution)/shard_map/ppermute | solution.py:208
  266.8 4.9 %collective-permute-start.20 = (bf16[18,16,96]{2,1,0:T(8,128)(2,1)S(1)}, bf16[18,16,96]{2,1,0:T(8,128)(2,1)S(1)}, u32[]{:S(2)}, u32[]{:S(2)}) collective-permute-start(bf16[18,16,96]{2,1,0:T(8,128)(2,1)S(1)} %get-tuple-element.28), channel_id=1, source_target_pairs={{0,2},{1,3},{2,0},{3,1},{4,6},{5,7},{6,4},{7,5},{8,10},{9,11},{10,... | collective-permute-start | bytes 165896 | tf_op jit(solution)/shard_map/ppermute | solution.py:208
  268.3 4.5 %collective-permute-start.21 = (bf16[18,16,96]{2,1,0:T(8,128)(2,1)S(1)}, bf16[18,16,96]{2,1,0:T(8,128)(2,1)S(1)}, u32[]{:S(2)}, u32[]{:S(2)}) collective-permute-start(bf16[18,16,96]{2,1,0:T(8,128)(2,1)S(1)} %get-tuple-element.29), channel_id=1, source_target_pairs={{0,3},{1,2},{2,1},{3,0},{4,7},{5,6},{6,5},{7,4},{8,11},{9,10},{10,... | collective-permute-start | bytes 165896 | tf_op jit(solution)/shard_map/ppermute | solution.py:208
  (25 other events, 171.4 us)

commit v3 on v2

--- a/solution.py
+++ b/solution.py
@@ -33,36 +33,106 @@
 
 
 ANY = pl.BlockSpec(memory_space=pl.ANY)
+IN_HBM = pl.BlockSpec(memory_space=pltpu.HBM)
 IN_VMEM = pl.BlockSpec(memory_space=pltpu.VMEM)
 IN_SMEM = pl.BlockSpec(memory_space=pltpu.SMEM)
 
 
-def spectra_kernel(field_ref, table_ref, *refs):
-    out_ref = refs[-1]
+def table_from(owned, order_ref, part):
+    slot_local, first, last = owned
+    slots = order_ref.shape[1]
+    held = last - first
+    rows = slots // slot_local * 2 * held
+    column = lax.broadcasted_iota(jnp.int32, (1, rows), 1)
+    owner, place = lax.div(column, 2 * held), lax.rem(column, 2 * held)
+    odd = (place >= held).astype(jnp.int32)
+    slot = owner * slot_local + 2 * (first + place - held * odd) + odd
+    here = lax.broadcasted_iota(jnp.int32, (slots, rows), 0)
+    orders = jnp.broadcast_to(order_ref[...].astype(jnp.float32), (8, slots))
+    chosen = jnp.dot(
+        orders,
+        (here == slot).astype(jnp.float32),
+        precision=lax.Precision.HIGHEST,
+        preferred_element_type=jnp.float32,
+    )
+    picks = (here.astype(jnp.float32) == chosen[:1]).astype(jnp.bfloat16)
+    return jnp.dot(part, picks, preferred_element_type=jnp.float32).astype(jnp.bfloat16)
+
+
+def spectra_kernel(owned, order_ref, part_ref, field_ref, *refs):
+    out_ref, table_ref = refs[-2:]
+
+    @pl.when(pl.program_id(0) == 0)
+    def _():
+        table_ref[...] = table_from(owned, order_ref, part_ref[...])
+
     cells = jnp.dot(field_ref[...], table_ref[...], preferred_element_type=jnp.float32)
     out_ref[...] = cells.T.astype(jnp.bfloat16)
 
 
-def spectra_of(fields, table, block, after):
-    cells, lon_count = fields.shape
-    rows = table.shape[1]
+def first_spectra_kernel(owned, order_ref, part_hbm, field_hbm, out_ref, part_ref, field_ref, sems):
+    block = out_ref.shape[1]
+    cut = block // 256 * 128
+    pieces = [(0, cut), (cut, block)]
+    copies = [pltpu.make_async_copy(part_hbm, part_ref, sems.at[0])]
+    for index, (start, stop) in enumerate(pieces):
+        rows = pl.ds(start, stop - start)
+        copies.append(
+            pltpu.make_async_copy(field_hbm.at[rows], field_ref.at[rows], sems.at[index + 1])
+        )
+    for copy in copies:
+        copy.start()
+    copies[0].wait()
+    table = table_from(owned, order_ref, part_ref[...])
+    for (start, stop), copy in zip(pieces, copies[1:]):
+        copy.wait()
+        cells = jnp.dot(field_ref[start:stop], table, preferred_element_type=jnp.float32)
+        out_ref[:, start:stop] = cells.T.astype(jnp.bfloat16)
+
+
+def spectra_of(order_row, owned, part, fields, block, blocks, after):
+    lon_count = fields.shape[1]
+    first, last = blocks
+    slot_local, first_pair, last_pair = owned
+    rows = order_row.shape[1] // slot_local * 2 * (last_pair - first_pair)
+    cells = (last - first) * block
+    alone = blocks == (0, 1) and block % 128 == 0 and block > 128 and not after
+    cost = pl.CostEstimate(
+        flops=2 * rows * cells * lon_count,
+        bytes_accessed=2 * (cells * lon_count + rows * (cells + lon_count)),
+        transcendentals=0,
+    )
+    out_shape = jax.ShapeDtypeStruct((rows, cells), jnp.bfloat16)
+    params = pltpu.CompilerParams(vmem_limit_bytes=VMEM)
+    if alone:
+        return pl.pallas_call(
+            functools.partial(first_spectra_kernel, owned),
+            in_specs=[IN_VMEM, IN_HBM, IN_HBM],
+            out_specs=IN_VMEM,
+            out_shape=out_shape,
+            scratch_shapes=[
+                pltpu.VMEM(part.shape, jnp.bfloat16),
+                pltpu.VMEM((block, lon_count), jnp.bfloat16),
+                pltpu.SemaphoreType.DMA((3,)),
+            ],
+            compiler_params=params,
+            cost_estimate=cost,
+        )(order_row, part, fields)
     return pl.pallas_call(
-        spectra_kernel,
-        grid=(cells // block,),
+        functools.partial(spectra_kernel, owned),
+        grid=(last - first,),
         in_specs=[
-            pl.BlockSpec((block, lon_count), lambda i: (i, 0)),
-            pl.BlockSpec((lon_count, rows), lambda i: (0, 0)),
+            pl.BlockSpec(order_row.shape, lambda i: (0, 0)),
+            pl.BlockSpec(part.shape, lambda i: (0, 0)),
+            pl.BlockSpec((block, lon_count), lambda i: (i + first, 0)),
         ]
         + [ANY] * len(after),
         out_specs=pl.BlockSpec((rows, block), lambda i: (0, i)),
-        out_shape=jax.ShapeDtypeStruct((rows, cells), jnp.bfloat16),
-        compiler_params=pltpu.CompilerParams(vmem_limit_bytes=VMEM),
-        cost_estimate=pl.CostEstimate(
-            flops=2 * rows * cells * lon_count,
-            bytes_accessed=2 * (cells * lon_count + rows * cells + rows * lon_count),
-            transcendentals=0,
-        ),
-    )(fields, table, *after)
+        out_shape=out_shape,
+        scratch_shapes=[pltpu.VMEM((lon_count, rows), jnp.bfloat16)],
+        compiler_params=params,
+        cost_estimate=cost,
+    )(order_row, part, fields, *after)
 
 
 def peer(me, hop, count):
@@ -71,31 +141,41 @@
     return (me + hop) % count, (me - hop + count) % count
 
 
-def digest_kernel(shape, lag_ref, me_ref, recv_ref, lat_ref, weight_ref, *refs):
-    narrow_count, lat_local, n_after = shape
-    sends, pick_ref = refs[n_after : n_after + narrow_count], refs[n_after + narrow_count]
-    line_ref, series_ref, block_ref = refs[n_after + narrow_count + 1 :]
-    sources, slots, _ = recv_ref.shape
-    days, _, degrees = series_ref.shape
+def digest_kernel(shape, lag_ref, me_ref, weight_ref, lat_hbm, *refs):
+    groups, narrow_count, lat_local, n_after = shape
+    blocks, refs = refs[:groups], refs[groups + n_after :]
+    lat_ref, lat_sem = refs[-2:]
+    refs = refs[:-2]
+    lat_copy = pltpu.make_async_copy(lat_hbm, lat_ref, lat_sem)
+    lat_copy.start()
+    sends, pick_ref = refs[:narrow_count], refs[narrow_count]
+    line_ref, series_ref, block_ref = refs[narrow_count + 1 :]
+    days, slots, degrees = series_ref.shape
     half, padded = slots // 2, line_ref.shape[1] // 2
-    for day in range(days):
-        for source in range(sources):
-            block = recv_ref[source, :, day * lat_local : (day + 1) * lat_local]
-            lats = slice(source * lat_local, (source + 1) * lat_local)
-            if half == padded:
-                line_ref[day, :, lats] = block
-            else:
-                line_ref[day, :half, lats] = block[:half]
-                line_ref[day, padded : padded + half, lats] = block[half:]
-    for parity in range(2):
-        lines = line_ref[:, parity * padded : (parity + 1) * padded, :]
-        coeffs = jnp.dot(
-            lines.reshape(days * padded, sources * lat_local),
-            lat_ref[:, parity * degrees : (parity + 1) * degrees],
-            preferred_element_type=jnp.float32,
-        )
-        coeffs = coeffs.astype(jnp.bfloat16).reshape(days, padded, degrees)
-        series_ref[:, parity * half : (parity + 1) * half, :] = coeffs[:, :half]
+    start = 0
+    for block in blocks:
+        stop = start + block.shape[2] // lat_local
+        for day in range(start, stop):
+            cells = slice((day - start) * lat_local, (day - start + 1) * lat_local)
+            for source in range(block.shape[0]):
+                lats = slice(source * lat_local, (source + 1) * lat_local)
+                if half == padded:
+                    line_ref[day, :, lats] = block[source, :, cells]
+                else:
+                    line_ref[day, :half, lats] = block[source, :half, cells]
+                    line_ref[day, padded : padded + half, lats] = block[source, half:, cells]
+        if start == 0:
+            lat_copy.wait()
+        for parity in range(2):
+            lines = line_ref[start:stop, parity * padded : (parity + 1) * padded, :]
+            coeffs = jnp.dot(
+                lines.reshape((stop - start) * padded, lat_ref.shape[0]),
+                lat_ref[:, parity * degrees : (parity + 1) * degrees],
+                preferred_element_type=jnp.float32,
+            )
+            coeffs = coeffs.astype(jnp.bfloat16).reshape(stop - start, padded, degrees)
+            series_ref[start:stop, parity * half : (parity + 1) * half, :] = coeffs[:, :half]
+        start = stop
 
     step = 16 if slots % 16 == 0 else slots
     lags = [lag_ref[i] for i in range(3)]
@@ -130,17 +210,18 @@
         send[...] = block_ref[peer(me, hop, narrow_count)[0]]
 
 
-def digest(lag_days, me, received, lat_table, weights, days_local, narrow_count, after):
-    sources, slots, cells = received.shape
+def digest(lag_days, me, received, lat_table, weights, narrow_count, after):
+    sources, slots, _ = received[0].shape
     latitudes, degrees = lat_table.shape[0], lat_table.shape[1] // 2
     lat_local = latitudes // sources
+    days_local = sum(block.shape[2] for block in received) // lat_local
     deg_local = degrees // narrow_count
     padded = 2 * (-(-(slots // 2) // 8) * 8)
     message = (2 * LAGMAX + 2, slots, deg_local)
     picked = (days_local, slots, narrow_count * (ROW_DEG + 1))
     return pl.pallas_call(
-        functools.partial(digest_kernel, (narrow_count, lat_local, len(after))),
-        in_specs=[IN_SMEM, IN_SMEM, IN_VMEM, IN_VMEM, IN_VMEM] + [ANY] * len(after),
+        functools.partial(digest_kernel, (len(received), narrow_count, lat_local, len(after))),
+        in_specs=[IN_SMEM, IN_SMEM, IN_VMEM, IN_HBM] + [IN_VMEM] * len(received) + [ANY] * len(after),
         out_specs=[IN_VMEM] * (narrow_count + 1),
         out_shape=[jax.ShapeDtypeStruct(message, jnp.bfloat16)] * narrow_count
         + [jax.ShapeDtypeStruct(picked, jnp.bfloat16)],
@@ -148,14 +229,26 @@
             pltpu.VMEM((days_local, padded, latitudes), jnp.bfloat16),
             pltpu.VMEM((days_local, slots, degrees), jnp.bfloat16),
             pltpu.VMEM((narrow_count,) + message, jnp.bfloat16),
+            pltpu.VMEM(lat_table.shape, jnp.bfloat16),
+            pltpu.SemaphoreType.DMA(()),
         ],
         compiler_params=pltpu.CompilerParams(vmem_limit_bytes=VMEM),
         cost_estimate=pl.CostEstimate(
-            flops=4 * slots * cells * sources * degrees,
-            bytes_accessed=2 * (sources * slots * cells + days_local * slots * degrees),
+            flops=4 * slots * days_local * latitudes * degrees,
+            bytes_accessed=2 * slots * days_local * (latitudes + degrees),
             transcendentals=0,
         ),
-    )(lag_days, me, received, lat_table, weights, *after)
+    )(lag_days, me, weights, lat_table, *received, *after)
+
+
+def tie(array, after):
+    return pl.pallas_call(
+        lambda *refs: None,
+        in_specs=[ANY] * (1 + len(after)),
+        out_specs=ANY,
+        out_shape=jax.ShapeDtypeStruct(array.shape, array.dtype),
+        input_output_aliases={0: 0},
+    )(array, *after)
 
 
 def combine_kernel(count, lag_ref, me_ref, weight_ref, *refs):
@@ -210,20 +303,31 @@
     ]
 
 
-def by_source(got, axis):
+def gather(block, axis):
     count = lax.axis_size(axis)
+    if count & (count - 1):
+        return lax.all_gather(block, axis)
     me = lax.axis_index(axis)
-    hops = jnp.arange(count, dtype=jnp.int32)
-    hops = hops ^ me if count & (count - 1) == 0 else (me - hops + count) % count
-    return jnp.take(jnp.stack(got), hops, axis=0)
-
-
-def segments_of(slot_local):
-    pairs = slot_local // 2
-    if slot_local % 48 == 0:
+    held = block[None]
+    reach = 1
+    while reach < count:
+        other = lax.ppermute(held, axis, [(i, i ^ reach) for i in range(count)])
+        upper = (me & reach) != 0
+        held = jnp.concatenate(
+            [jnp.where(upper, other, held), jnp.where(upper, held, other)], axis=0
+        )
+        reach *= 2
+    return held
+
+
+def plan_of(slot_local, days_local, day_block):
+    pairs, blocks = slot_local // 2, days_local // day_block
+    every = (0, blocks)
+    if slot_local % 48 == 0 and blocks > 1:
         cut = pairs * 2 // 3
-        return [[(0, 0, cut)], [(0, cut, pairs), (1, 0, cut)], [(1, cut, pairs)]]
-    return [[(0, 0, pairs)], [(1, 0, pairs)]]
+        sent = [(0, 0, pairs, (0, 1)), (0, 0, pairs, (1, blocks)), (1, 0, cut, every), (1, cut, pairs, every)]
+        return sent, [(0, 1), (2,), (3,)]
+    return [(0, 0, pairs, every), (1, 0, pairs, every)], [(0,), (1,)]
 
 
 def body(daily_fields, order_table, lag_days, lag_weights):
@@ -242,73 +346,49 @@
     fields = daily_fields.reshape(days_local * lat_local, lon_count)
     parts = [jnp.asarray(p) for p in dft_columns(order_count, lon_count)]
     lat_table = jnp.asarray(lat_columns(deg_count, lat_local * wide_count))
-    by_owner = order_table.reshape(wide_count, pair_local, 2)
-    every_order = jnp.arange(order_count, dtype=jnp.int32)[:, None]
-
-    def table_of(segments):
-        columns = []
-        for parity in range(2):
-            for part, first, last in segments:
-                orders = by_owner[:, first:last, parity]
-                columns.append((part, orders))
-        picks = []
-        for part in range(2):
-            if any(p == part for p, _ in columns):
-                chosen = jnp.concatenate(
-                    [orders if p == part else jnp.full_like(orders, -1) for p, orders in columns], axis=1
-                ).reshape(1, -1)
-                picks.append(
-                    jnp.dot(
-                        parts[part],
-                        (every_order == chosen).astype(jnp.bfloat16),
-                        preferred_element_type=jnp.float32,
-                    )
-                )
-        return sum(picks[1:], picks[0]).astype(jnp.bfloat16)
+    order_row = order_table.reshape(1, order_count)
 
     own_weights = jnp.transpose(
         lag_weights.reshape(3, deg_local, pair_local, 2, 2), (4, 3, 0, 2, 1)
     )
-    all_weights = by_source(swap([own_weights] * narrow_count, "narrow"), "narrow")
+    all_weights = gather(own_weights, "narrow")
     all_weights = jnp.moveaxis(all_weights, 0, 4).reshape(2, 2, 3, pair_local, deg_count)
 
-    def rows_of(weights, segments):
-        return jnp.concatenate(
-            [weights[p, parity, :, a:b] for parity in range(2) for p, a, b in segments], axis=1
-        )
-
-    plan = segments_of(slot_local)
+    def rows_of(weights, part, first, last):
+        return jnp.concatenate([weights[part, parity, :, first:last] for parity in range(2)], axis=1)
+
+    sent, jobs = plan_of(slot_local, days_local, day_block)
     spreads = {}
     picked = {}
-    results = []
-    received = []
-    panel = None
-
-    def exchange(segments, after):
-        spectra = spectra_of(fields, table_of(segments), day_block * lat_local, after)
-        spectra = spectra.reshape(wide_count, -1, days_local * lat_local)
+
+    def product(index, after):
+        part, first, last, blocks = sent[index]
+        owned = (slot_local, first, last)
+        return spectra_of(order_row, owned, parts[part], fields, day_block * lat_local, blocks, after)
+
+    def exchange(spectra):
+        spectra = spectra.reshape(wide_count, -1, spectra.shape[1])
         return lax.all_to_all(spectra, "wide", split_axis=0, concat_axis=0, tiled=True)
 
-    def finish(segments, received, after):
+    def finish(job, after):
+        part, first, last, _ = sent[job[0]]
         *sends, picks = digest(
             lag_days,
             me,
-            received,
+            [received[index] for index in job],
             lat_table,
-            rows_of(all_weights, segments),
-            days_local,
+            rows_of(all_weights, part, first, last),
             narrow_count,
             after,
         )
-        total = combine(lag_days, me, rows_of(own_weights, segments), swap(sends, "narrow"))
-        at = 0
+        total = combine(
+            lag_days, me, rows_of(own_weights, part, first, last), swap(sends, "narrow")
+        )
         for parity in range(2):
-            for part, first, last in segments:
-                rows = slice(at, at + last - first)
-                spreads[part, parity, first] = total[rows]
-                if part == 0:
-                    picked[parity, first] = picks[:, rows]
-                at += last - first
+            rows = slice(parity * (last - first), (parity + 1) * (last - first))
+            spreads[part, parity, first] = total[rows]
+            if part == 0:
+                picked[parity, first] = picks[:, rows]
         return total
 
     def panel_of():
@@ -320,9 +400,10 @@
             axis=2,
         )
         series = series.reshape(days_local, slot_local, narrow_count * (ROW_DEG + 1))
-        series = jnp.transpose(series, (1, 2, 0))
-        series = by_source(swap([series] * narrow_count, "narrow"), "narrow")
-        series = jnp.moveaxis(series, 0, 2).reshape(
+        series = jnp.transpose(series, (1, 2, 0)).reshape(slot_local, -1)
+        series = gather(series, "narrow")
+        series = series.reshape(narrow_count, slot_local, narrow_count, ROW_DEG + 1, days_local)
+        series = jnp.moveaxis(series, 0, 3).reshape(
             slot_local, narrow_count, ROW_DEG + 1, days_local * narrow_count
         )
         weights = all_weights[0].reshape(2, 3, pair_local, narrow_count, deg_local)
@@ -336,20 +417,26 @@
         rounded = residual.astype(jnp.bfloat16)
         rows = rounded[:, :, :ROW_DEG].reshape(slot_local, narrow_count * ROW_DEG, kept_days)
         column = lax.dynamic_index_in_dim(rounded[:, :, ROW_DEG], me[0], 1, False)
-        columns = by_source(swap([column] * wide_count, "wide"), "wide")
-        columns = columns.reshape(order_count, kept_days)
+        columns = gather(column, "wide").reshape(order_count, kept_days)
         product = lax.dot_general(
             rows, columns, (((2,), (1,)), ((), ())), preferred_element_type=jnp.float32
         )
         return product / math.sqrt(kept_days)
 
-    for index, segments in enumerate(plan):
-        if index >= 2:
-            results.append(finish(plan[index - 2], received[index - 2], results[-1:]))
-        received.append(exchange(segments, results[-1:]))
-    results.append(finish(plan[-2], received[-2], results[-1:]))
+    spectra = {0: product(0, [])}
+    spectra[1] = before = product(1, [spectra[0]])
+    for index in reversed(range(2, len(sent))):
+        before = spectra[index] = product(index, [before, all_weights])
+    received = [exchange(spectra[index]) for index in range(len(sent) - 1)]
+    if len(sent) == 2:
+        received.append(exchange(spectra[1]))
+    done = [finish(jobs[0], [])]
     panel = panel_of()
-    finish(plan[-1], received[-1], results[-1:] + [panel])
+    done.append(panel)
+    if len(sent) > 2:
+        received.append(exchange(tie(spectra[len(sent) - 1], done)))
+    for job in jobs[1:]:
+        done = [finish(job, done)]
 
     spread = jnp.stack(
         [

time: 275 us -> 246 us (0.89)
  local copies, waits for them, and re-layouts: 29.1 us -> 15.1 us
  Pallas kernels: 54.8 us -> 63.1 us
  other arithmetic: 10.5 us -> 2.79 us
  matrix products: 6.95 us -> 0.34 us
  starting transfers between devices: 41 us -> 35.4 us
  waiting for transfers between devices: 127 us -> 123 us
    ppermute x0 -> x7, waiting for transfers between devices: none -> 47.2 us  [gather(): other = lax.ppermute(held, axis, [(i, i ^ reach) for i in range(count)])]
    all_to_all x3 -> x4, waiting for transfers between devices: 95 us -> 65.9 us  [exchange(): lax.all_to_all(spectra, 'wide', split_axis=0, concat_axis=0, tiled=True)]
    ppermute x22 -> x9, waiting for transfers between devices: 31.9 us -> 10.1 us  [swap(): lax.ppermute(sends[hop], axis, [(i, peer(i, hop, count)[0]) for i in rang...]
    ppermute x22 -> x9, starting transfers between devices: 25.2 us -> 5.8 us  [swap(): lax.ppermute(sends[hop], axis, [(i, peer(i, hop, count)[0]) for i in rang...]
    ppermute x0 -> x7, starting transfers between devices: none -> 9.09 us  [gather(): other = lax.ppermute(held, axis, [(i, i ^ reach) for i in range(count)])]
    pallas_call x6 -> x8, Pallas kernels: 52 us -> 60.7 us  [the longest x3 32.3 us: spectra_of(): pl.pallas_call(functools.partial(spectra_kernel, owned), grid=(last - fir...]
    dot_general x4 -> x0, matrix products: 6.61 us -> none  [table_of(): jnp.dot(parts[part], (every_order == chosen).astype(jnp.bfloat16), prefer...]
    all_to_all x3 -> x4, starting transfers between devices: 15.7 us -> 20.6 us  [exchange(): lax.all_to_all(spectra, 'wide', split_axis=0, concat_axis=0, tiled=True)]
  transfers between devices with their start and end apart: 25 -> 20, of which waited for: 11 -> 14; matrix products, arithmetic and copies ran while one was open for 13% -> 4% of each run, Pallas kernels for 11% -> 21%
where the time goes in v3:
time: 246 us; the launch traced here: 245 us
  waiting for transfers between devices  123 us (50%)
  Pallas kernels  63.1 us (26%)
  starting transfers between devices  35.4 us (14%)
  local copies, waits for them, and re-layouts  15.1 us (6%)
  between operations  5.21 us (2%)
  other arithmetic  2.79 us (1%)
    all_to_all x4, waiting for transfers between devices, exchange(): lax.all_to_all(spectra, 'wide', split_axis=0, concat_axis=0, tiled=True)  65.9 us
    ppermute x7, waiting for transfers between devices, gather(): other = lax.ppermute(held, axis, [(i, i ^ reach) for i in range(count)])  47.2 us
    pallas_call x3, Pallas kernels, spectra_of(): pl.pallas_call(functools.partial(spectra_kernel, owned), grid=(last - fir...  32.3 us
    pallas_call x3, Pallas kernels, digest(): pl.pallas_call(functools.partial(digest_kernel, (len(received), narrow_co...  23 us
    all_to_all x4, starting transfers between devices, exchange(): lax.all_to_all(spectra, 'wide', split_axis=0, concat_axis=0, tiled=True)  20.6 us
    ppermute x9, waiting for transfers between devices, swap(): lax.ppermute(sends[hop], axis, [(i, peer(i, hop, count)[0]) for i in rang...  10.1 us
    unnamed x38, local copies, waits for them, and re-layouts  10.1 us
    ppermute x7, starting transfers between devices, gather(): other = lax.ppermute(held, axis, [(i, i ^ reach) for i in range(count)])  9.09 us
  transfers between devices with their start and end apart: 20, of which 14 were waited for; matrix products, arithmetic and copies ran while one was open for 4% of the time, Pallas kernels for 21%

profile of v3, /device:TPU:0, one launch (start us, length us, event | category | flops | bytes accessed | tf_op | source)
XLA Modules:
  0.0 245.2 jit_solution(7014909620594673251)
XLA Ops:
  2.6 5.4 %shard_map.86.refs_0_ = bf16[384,1408]{1,0:T(8,128)(2,1)} custom-call(s32[1,384]{1,0:T(1,128)S(1)} %reshape.79.order_ref, bf16[1440,384]{1,0:T(8,128)(2,1)S(1)} %copy-done.4, bf16[5632,1440]{1,0:T(8,128)(2,1)} %bitcast.93), custom_call_target="tpu_custom_call" | custom-call | flops 1557135360 | bytes 6242304 | tf_op jit(solution)/shard_map/pallas_call | solution.py:108
  8.0 7.4 %all-to-all-start = ((bf16[8,48,1408]{2,1,0:T(8,128)(2,1)}), bf16[8,48,1408]{2,1,0:T(8,128)(2,1)S(1)}, u32[]{:S(2)}, u32[]{:S(2)}) async-start(bf16[8,48,1408]{2,1,0:T(8,128)(2,1)} %bitcast.11), calls=%async_computation | async-start | bytes 2162688 | tf_op jit(solution)/shard_map/all_to_all | solution.py:371
  15.5 12.2 %shard_map.87.refs_0_ = bf16[384,4224]{1,0:T(8,128)(2,1)} custom-call(s32[1,384]{1,0:T(1,128)S(1)} %reshape.79.order_ref, bf16[1440,384]{1,0:T(8,128)(2,1)S(1)} %copy-done.5, bf16[5632,1440]{1,0:T(8,128)(2,1)} %bitcast.94, bf16[384,1408]{1,0:T(8,128)(2,1)} %shard_map.86.refs_0_), custom_call_target="tpu_custom_call" | custom-call | flops 4671406080 | bytes 16515072 | tf_op jit(solution)/shard_map/pallas_call | solution.py:121
  27.7 14.3 %all-to-all-done.refs_0_ = bf16[8,48,1408]{2,1,0:T(8,128)(2,1)S(1)} async-done(((bf16[8,48,1408]{2,1,0:T(8,128)(2,1)}), bf16[8,48,1408]{2,1,0:T(8,128)(2,1)S(1)}, u32[]{:S(2)}, u32[]{:S(2)}) %all-to-all-start) | async-done | bytes 1081376 | tf_op jit(solution)/shard_map/all_to_all | solution.py:371
  42.9 4.5 %all-to-all-start.1 = ((bf16[8,48,4224]{2,1,0:T(8,128)(2,1)}), bf16[8,48,4224]{2,1,0:T(8,128)(2,1)}, u32[]{:S(2)}, u32[]{:S(2)}) async-start(bf16[8,48,4224]{2,1,0:T(8,128)(2,1)} %bitcast.12), calls=%async_computation.1 | async-start | bytes 6488064 | tf_op jit(solution)/shard_map/all_to_all | solution.py:371
  50.5 7.6 %collective-permute-done.1 = f32[2,2,2,3,24,96]{5,4,3,2,1,0:T(8,128)S(1)} collective-permute-done((f32[2,2,2,3,24,96]{5,4,3,2,1,0:T(8,128)S(1)}, f32[2,2,2,3,24,96]{5,4,3,2,1,0:T(8,128)S(1)}, u32[]{:S(2)}, u32[]{:S(2)}) %collective-permute-start.1) | collective-permute-done | bytes 221216 | tf_op jit(solution)/shard_map/ppermute | solution.py:314
  60.2 9.6 %shard_map.90.refs_0_ = bf16[128,5632]{1,0:T(8,128)(2,1)S(1)} custom-call(s32[1,384]{1,0:T(1,128)S(1)} %reshape.79.order_ref, bf16[1440,384]{1,0:T(8,128)(2,1)S(1)} %copy-done.3, bf16[5632,1440]{1,0:T(8,128)(2,1)} %bitcast.95, bf16[384,4224]{1,0:T(8,128)(2,1)} %shard_map.87.refs_0_, f32[2,2,3,24,384]{4,3,2,1,0:T(8,128)S(1)} %reshape.78.refs_1_), custom_call_target="tpu_custom_call" | custom-call | flops 2076180480 | bytes 18030592 | tf_op jit(solution)/shard_map/pallas_call | solution.py:121
  69.8 10.5 %shard_map.91 = bf16[256,5632]{1,0:T(8,128)(2,1)S(1)} custom-call(s32[1,384]{1,0:T(1,128)S(1)} %reshape.79.order_ref, bf16[1440,384]{1,0:T(8,128)(2,1)S(1)} %copy-done.3, bf16[5632,1440]{1,0:T(8,128)(2,1)} %bitcast.96, bf16[128,5632]{1,0:T(8,128)(2,1)S(1)} %shard_map.90.refs_0_, f32[2,2,3,24,384]{4,3,2,1,0:T(8,128)S(1)} %reshape.78.refs_1_), custom_call_target="tpu_custom_call" | custom-call | flops 4152360960 | bytes 19841024 | tf_op jit(solution)/shard_map/pallas_call | solution.py:121
  82.0 37.6 %all-to-all-done.1.refs_1_ = bf16[8,48,4224]{2,1,0:T(8,128)(2,1)} async-done(((bf16[8,48,4224]{2,1,0:T(8,128)(2,1)}), bf16[8,48,4224]{2,1,0:T(8,128)(2,1)}, u32[]{:S(2)}, u32[]{:S(2)}) %all-to-all-start.1) | async-done | bytes 3244064 | tf_op jit(solution)/shard_map/all_to_all | solution.py:371
  119.6 4.7 %all-to-all-start.2 = ((bf16[8,32,5632]{2,1,0:T(8,128)(2,1)}), bf16[8,32,5632]{2,1,0:T(8,128)(2,1)}, u32[]{:S(2)}, u32[]{:S(2)}) async-start(bf16[8,32,5632]{2,1,0:T(8,128)(2,1)} %bitcast.92), calls=%async_computation.2 | async-start | bytes 5767168 | tf_op jit(solution)/shard_map/all_to_all | solution.py:371
  130.3 9.2 %shard_map.88 = (bf16[18,48,96]{2,1,0:T(8,128)(2,1)S(1)}, bf16[18,48,96]{2,1,0:T(8,128)(2,1)S(1)}, bf16[18,48,96]{2,1,0:T(8,128)(2,1)S(1)}, bf16[18,48,96]{2,1,0:T(8,128)(2,1)S(1)}, bf16[64,48,16]{2,1,0:T(8,128)(2,1)S(1)}) custom-call(s32[3]{0:T(128)S(1)} %copy-done.10, s32[1]{0:T(128)} %bitcast.me_ref, f32[3,48,384]{2,1,0:T(8,128)S(1)} %pad_maximum_fusion.2.weight_ref, ...), custom_call_target="tpu_custom_call" | custom-call | flops 3321888768 | bytes 6684672 | tf_op jit(solution)/shard_map/pallas_call | solution.py:222
  143.8 5.0 %collective-permute-done.6 = bf16[2,48,1024]{2,1,0:T(8,128)(2,1)S(1)} collective-permute-done((bf16[2,48,1024]{2,1,0:T(8,128)(2,1)S(1)}, bf16[2,48,1024]{2,1,0:T(8,128)(2,1)S(1)}, u32[]{:S(2)}, u32[]{:S(2)}) %collective-permute-start.6) | collective-permute-done | bytes 196640 | tf_op jit(solution)/shard_map/ppermute | solution.py:314
  151.4 1.8 collective-permute-start.7
  153.2 5.3 %collective-permute-done.7 = bf16[1,48,248]{2,1,0:T(8,128)(2,1)S(1)} collective-permute-done((bf16[1,48,248]{2,1,0:T(8,128)(2,1)S(1)}, bf16[1,48,248]{2,1,0:T(8,128)(2,1)S(1)}, u32[]{:S(2)}, u32[]{:S(2)}) %collective-permute-start.7) | collective-permute-done | bytes 23840 | tf_op jit(solution)/shard_map/ppermute | solution.py:314
  160.6 11.4 %collective-permute-done.8 = bf16[2,48,248]{2,1,0:T(8,128)(2,1)S(1)} collective-permute-done((bf16[2,48,248]{2,1,0:T(8,128)(2,1)S(1)}, bf16[2,48,248]{2,1,0:T(8,128)(2,1)S(1)}, u32[]{:S(2)}, u32[]{:S(2)}) %collective-permute-start.8) | collective-permute-done | bytes 47648 | tf_op jit(solution)/shard_map/ppermute | solution.py:314
  172.0 4.0 %collective-permute-start.9 = (bf16[4,48,248]{2,1,0:T(8,128)(2,1)S(1)}, bf16[4,48,248]{2,1,0:T(8,128)(2,1)S(1)}, u32[]{:S(2)}, u32[]{:S(2)}) collective-permute-start(bf16[4,48,248]{2,1,0:T(8,128)(2,1)S(1)} %pad_maximum_fusion.7), channel_id=1, source_target_pairs={{0,16},{4,20},{8,24},{12,28},{16,0},{20,4},{24,8},{28,12},{1,17},{... | collective-permute-start | bytes 285704 | tf_op jit(solution)/shard_map/ppermute | solution.py:314
  177.0 16.0 %collective-permute-done.9 = bf16[4,48,248]{2,1,0:T(8,128)(2,1)S(1)} collective-permute-done((bf16[4,48,248]{2,1,0:T(8,128)(2,1)S(1)}, bf16[4,48,248]{2,1,0:T(8,128)(2,1)S(1)}, u32[]{:S(2)}, u32[]{:S(2)}) %collective-permute-start.9) | collective-permute-done | bytes 95264 | tf_op jit(solution)/shard_map/ppermute | solution.py:314
  194.8 3.9 %all-to-all-start.3 = ((bf16[8,16,5632]{2,1,0:T(8,128)(2,1)}), bf16[8,16,5632]{2,1,0:T(8,128)(2,1)S(1)}, u32[]{:S(2)}, u32[]{:S(2)}) async-start(bf16[8,16,5632]{2,1,0:T(8,128)(2,1)} %bitcast.91), calls=%async_computation.3 | async-start | bytes 2883584 | tf_op jit(solution)/shard_map/all_to_all | solution.py:371
  200.0 9.1 %shard_map.92 = (bf16[18,32,96]{2,1,0:T(8,128)(2,1)S(1)}, bf16[18,32,96]{2,1,0:T(8,128)(2,1)S(1)}, bf16[18,32,96]{2,1,0:T(8,128)(2,1)S(1)}, bf16[18,32,96]{2,1,0:T(8,128)(2,1)S(1)}, bf16[64,32,16]{2,1,0:T(8,128)(2,1)}) custom-call(s32[3]{0:T(128)S(1)} %copy-done.10, s32[1]{0:T(128)} %bitcast.me_ref, f32[3,32,384]{2,1,0:T(8,128)S(1)} %pad_maximum_fusion.6.weight_ref, ...), custom_call_target="tpu_custom_call" | custom-call | flops 2214592512 | bytes 4456448 | tf_op jit(solution)/shard_map/pallas_call | solution.py:222
  212.2 3.7 %collective-permute-done.11.refs_2_ = bf16[18,32,96]{2,1,0:T(8,128)(2,1)S(1)} collective-permute-done((bf16[18,32,96]{2,1,0:T(8,128)(2,1)S(1)}, bf16[18,32,96]{2,1,0:T(8,128)(2,1)S(1)}, u32[]{:S(2)}, u32[]{:S(2)}) %collective-permute-start.11) | collective-permute-done | bytes 110624 | tf_op jit(solution)/shard_map/ppermute | solution.py:301
  215.9 2.3 collective-permute-done.12.refs_3_
  219.0 14.0 %all-to-all-done.3.refs_0_ = bf16[8,16,5632]{2,1,0:T(8,128)(2,1)S(1)} async-done(((bf16[8,16,5632]{2,1,0:T(8,128)(2,1)}), bf16[8,16,5632]{2,1,0:T(8,128)(2,1)S(1)}, u32[]{:S(2)}, u32[]{:S(2)}) %all-to-all-start.3) | async-done | bytes 1441824 | tf_op jit(solution)/shard_map/all_to_all | solution.py:371
  233.0 4.6 %shard_map.95 = (bf16[18,16,96]{2,1,0:T(8,128)(2,1)S(1)}, bf16[18,16,96]{2,1,0:T(8,128)(2,1)S(1)}, bf16[18,16,96]{2,1,0:T(8,128)(2,1)S(1)}, bf16[18,16,96]{2,1,0:T(8,128)(2,1)S(1)}, bf16[64,16,16]{2,1,0:T(8,128)(2,1)}) custom-call(s32[3]{0:T(128)S(1)} %copy-done.10, s32[1]{0:T(128)} %bitcast.me_ref, f32[3,16,384]{2,1,0:T(8,128)S(1)} %pad_maximum_fusion.9.weight_ref, ...), custom_call_target="tpu_custom_call" | custom-call | flops 1107296256 | bytes 2228224 | tf_op jit(solution)/shard_map/pallas_call | solution.py:222
  239.6 3.0 %collective-permute-done.14.refs_2_ = bf16[18,16,96]{2,1,0:T(8,128)(2,1)S(1)} collective-permute-done((bf16[18,16,96]{2,1,0:T(8,128)(2,1)S(1)}, bf16[18,16,96]{2,1,0:T(8,128)(2,1)S(1)}, u32[]{:S(2)}, u32[]{:S(2)}) %collective-permute-start.14) | collective-permute-done | bytes 55328 | tf_op jit(solution)/shard_map/ppermute | solution.py:301
  (127 shorter events, 33.0 us)
Async XLA Ops:
  8.0 33.9 %all-to-all-start = ((bf16[8,48,1408]{2,1,0:T(8,128)(2,1)}), bf16[8,48,1408]{2,1,0:T(8,128)(2,1)S(1)}, u32[]{:S(2)}, u32[]{:S(2)}) async-start(bf16[8,48,1408]{2,1,0:T(8,128)(2,1)} %bitcast.11), calls=%async_computation | async-start | bytes 2162688 | tf_op jit(solution)/shard_map/all_to_all | solution.py:371
  42.9 76.7 %all-to-all-start.1 = ((bf16[8,48,4224]{2,1,0:T(8,128)(2,1)}), bf16[8,48,4224]{2,1,0:T(8,128)(2,1)}, u32[]{:S(2)}, u32[]{:S(2)}) async-start(bf16[8,48,4224]{2,1,0:T(8,128)(2,1)} %bitcast.12), calls=%async_computation.1 | async-start | bytes 6488064 | tf_op jit(solution)/shard_map/all_to_all | solution.py:371
  47.4 1.4 collective-permute-start
  48.9 9.1 %collective-permute-start.1 = (f32[2,2,2,3,24,96]{5,4,3,2,1,0:T(8,128)S(1)}, f32[2,2,2,3,24,96]{5,4,3,2,1,0:T(8,128)S(1)}, u32[]{:S(2)}, u32[]{:S(2)}) collective-permute-start(f32[2,2,2,3,24,96]{5,4,3,2,1,0:T(8,128)S(1)} %pad_maximum_fusion.1), channel_id=1, source_target_pairs={{0,2},{1,3},{2,0},{3,1},{4,6},{5,7},{6,4},{7,5},{8,10},{9,11},{10,... | collective-permute-start | bytes 663560 | tf_op jit(solution)/shard_map/ppermute | solution.py:314
  69.8 10.5 %copy-start = (bf16[128,5632]{1,0:T(8,128)(2,1)}, bf16[128,5632]{1,0:T(8,128)(2,1)S(1)}, u32[]{:S(2)}) copy-start(bf16[128,5632]{1,0:T(8,128)(2,1)S(1)} %shard_map.90.refs_0_) | copy-start | bytes 4325380
  119.6 9.3 %copy-start.14 = (f32[2,2,3,24,4,96]{5,3,2,1,0,4:T(8,128)S(1)}, f32[2,2,3,24,4,96]{5,3,2,1,0,4:T(8,128)}, u32[]{:S(2)}) copy-start(f32[2,2,3,24,4,96]{5,3,2,1,0,4:T(8,128)} %copy-done.13) | copy-start | bytes 1327108
  119.6 75.2 %all-to-all-start.2 = ((bf16[8,32,5632]{2,1,0:T(8,128)(2,1)}), bf16[8,32,5632]{2,1,0:T(8,128)(2,1)}, u32[]{:S(2)}, u32[]{:S(2)}) async-start(bf16[8,32,5632]{2,1,0:T(8,128)(2,1)} %bitcast.92), calls=%async_computation.2 | async-start | bytes 5767168 | tf_op jit(solution)/shard_map/all_to_all | solution.py:371
  140.4 1.4 collective-permute-start.5
  141.8 7.0 %collective-permute-start.6 = (bf16[2,48,1024]{2,1,0:T(8,128)(2,1)S(1)}, bf16[2,48,1024]{2,1,0:T(8,128)(2,1)S(1)}, u32[]{:S(2)}, u32[]{:S(2)}) collective-permute-start(bf16[2,48,1024]{2,1,0:T(8,128)(2,1)S(1)} %pad_maximum_fusion.4), channel_id=1, source_target_pairs={{0,2},{1,3},{2,0},{3,1},{4,6},{5,7},{6,4},{7,5},{8,10},{9,11},{10,... | collective-permute-start | bytes 589832 | tf_op jit(solution)/shard_map/ppermute | solution.py:314
  150.5 8.1 %copy-start.16 = (f32[3,96,24,2,2]{1,2,0,3,4:T(8,128)S(1)}, f32[3,96,24,2,2]{1,2,0,3,4:T(8,128)}, u32[]{:S(2)}) copy-start(f32[3,96,24,2,2]{1,2,0,3,4:T(8,128)} %copy-done.15) | copy-start | bytes 331780
  151.4 7.0 %collective-permute-start.7 = (bf16[1,48,248]{2,1,0:T(8,128)(2,1)S(1)}, bf16[1,48,248]{2,1,0:T(8,128)(2,1)S(1)}, u32[]{:S(2)}, u32[]{:S(2)}) collective-permute-start(bf16[1,48,248]{2,1,0:T(8,128)(2,1)S(1)} %dynamic-slice_bitcast_fusion), channel_id=1, source_target_pairs={{0,4},{4,0},{8,12},{12,8},{16,20},{20,16},{24,28},{28,24},{1,5},{5... | collective-permute-start | bytes 71432 | tf_op jit(solution)/shard_map/ppermute | solution.py:314
  158.5 13.5 %collective-permute-start.8 = (bf16[2,48,248]{2,1,0:T(8,128)(2,1)S(1)}, bf16[2,48,248]{2,1,0:T(8,128)(2,1)S(1)}, u32[]{:S(2)}, u32[]{:S(2)}) collective-permute-start(bf16[2,48,248]{2,1,0:T(8,128)(2,1)S(1)} %pad_maximum_fusion.11), channel_id=1, source_target_pairs={{0,8},{4,12},{8,0},{12,4},{16,24},{20,28},{24,16},{28,20},{1,9},{5... | collective-permute-start | bytes 142856 | tf_op jit(solution)/shard_map/ppermute | solution.py:314
  158.6 17.4 %collective-permute-start.2 = (bf16[18,48,96]{2,1,0:T(8,128)(2,1)S(1)}, bf16[18,48,96]{2,1,0:T(8,128)(2,1)S(1)}, u32[]{:S(2)}, u32[]{:S(2)}) collective-permute-start(bf16[18,48,96]{2,1,0:T(8,128)(2,1)S(1)} %get-tuple-element.16), channel_id=1, source_target_pairs={{0,1},{1,0},{2,3},{3,2},{4,5},{5,4},{6,7},{7,6},{8,9},{9,8},{10,11... | collective-permute-start | bytes 497672 | tf_op jit(solution)/shard_map/ppermute | solution.py:301
  158.7 17.3 %collective-permute-start.3 = (bf16[18,48,96]{2,1,0:T(8,128)(2,1)S(1)}, bf16[18,48,96]{2,1,0:T(8,128)(2,1)S(1)}, u32[]{:S(2)}, u32[]{:S(2)}) collective-permute-start(bf16[18,48,96]{2,1,0:T(8,128)(2,1)S(1)} %get-tuple-element.17), channel_id=1, source_target_pairs={{0,2},{1,3},{2,0},{3,1},{4,6},{5,7},{6,4},{7,5},{8,10},{9,11},{10,... | collective-permute-start | bytes 497672 | tf_op jit(solution)/shard_map/ppermute | solution.py:301
  160.2 15.8 %collective-permute-start.4 = (bf16[18,48,96]{2,1,0:T(8,128)(2,1)S(1)}, bf16[18,48,96]{2,1,0:T(8,128)(2,1)S(1)}, u32[]{:S(2)}, u32[]{:S(2)}) collective-permute-start(bf16[18,48,96]{2,1,0:T(8,128)(2,1)S(1)} %get-tuple-element.18), channel_id=1, source_target_pairs={{0,3},{1,2},{2,1},{3,0},{4,7},{5,6},{6,5},{7,4},{8,11},{9,10},{10,... | collective-permute-start | bytes 497672 | tf_op jit(solution)/shard_map/ppermute | solution.py:301
  172.0 21.0 %collective-permute-start.9 = (bf16[4,48,248]{2,1,0:T(8,128)(2,1)S(1)}, bf16[4,48,248]{2,1,0:T(8,128)(2,1)S(1)}, u32[]{:S(2)}, u32[]{:S(2)}) collective-permute-start(bf16[4,48,248]{2,1,0:T(8,128)(2,1)S(1)} %pad_maximum_fusion.7), channel_id=1, source_target_pairs={{0,16},{4,20},{8,24},{12,28},{16,0},{20,4},{24,8},{28,12},{1,17},{... | collective-permute-start | bytes 285704 | tf_op jit(solution)/shard_map/ppermute | solution.py:314
  177.0 16.4 %copy-start.8 = (f32[48,96]{1,0:T(8,128)}, f32[48,96]{1,0:T(8,128)S(1)}, u32[]{:S(2)}) copy-start(f32[48,96]{1,0:T(8,128)S(1)} %shard_map.89.refs_1_) | copy-start | bytes 55300
  194.8 38.2 %all-to-all-start.3 = ((bf16[8,16,5632]{2,1,0:T(8,128)(2,1)}), bf16[8,16,5632]{2,1,0:T(8,128)(2,1)S(1)}, u32[]{:S(2)}, u32[]{:S(2)}) async-start(bf16[8,16,5632]{2,1,0:T(8,128)(2,1)} %bitcast.91), calls=%async_computation.3 | async-start | bytes 2883584 | tf_op jit(solution)/shard_map/all_to_all | solution.py:371
  209.1 3.1 %collective-permute-start.10 = (bf16[18,32,96]{2,1,0:T(8,128)(2,1)S(1)}, bf16[18,32,96]{2,1,0:T(8,128)(2,1)S(1)}, u32[]{:S(2)}, u32[]{:S(2)}) collective-permute-start(bf16[18,32,96]{2,1,0:T(8,128)(2,1)S(1)} %get-tuple-element.21), channel_id=1, source_target_pairs={{0,1},{1,0},{2,3},{3,2},{4,5},{5,4},{6,7},{7,6},{8,9},{9,8},{10,11... | collective-permute-start | bytes 331784 | tf_op jit(solution)/shard_map/ppermute | solution.py:301
  209.2 6.7 %collective-permute-start.11 = (bf16[18,32,96]{2,1,0:T(8,128)(2,1)S(1)}, bf16[18,32,96]{2,1,0:T(8,128)(2,1)S(1)}, u32[]{:S(2)}, u32[]{:S(2)}) collective-permute-start(bf16[18,32,96]{2,1,0:T(8,128)(2,1)S(1)} %get-tuple-element.22), channel_id=1, source_target_pairs={{0,2},{1,3},{2,0},{3,1},{4,6},{5,7},{6,4},{7,5},{8,10},{9,11},{10,... | collective-permute-start | bytes 331784 | tf_op jit(solution)/shard_map/ppermute | solution.py:301
  210.7 7.4 %collective-permute-start.12 = (bf16[18,32,96]{2,1,0:T(8,128)(2,1)S(1)}, bf16[18,32,96]{2,1,0:T(8,128)(2,1)S(1)}, u32[]{:S(2)}, u32[]{:S(2)}) collective-permute-start(bf16[18,32,96]{2,1,0:T(8,128)(2,1)S(1)} %get-tuple-element.23), channel_id=1, source_target_pairs={{0,3},{1,2},{2,1},{3,0},{4,7},{5,6},{6,5},{7,4},{8,11},{9,10},{10,... | collective-permute-start | bytes 331784 | tf_op jit(solution)/shard_map/ppermute | solution.py:301
  237.6 1.9 collective-permute-start.13
  237.7 4.8 %collective-permute-start.14 = (bf16[18,16,96]{2,1,0:T(8,128)(2,1)S(1)}, bf16[18,16,96]{2,1,0:T(8,128)(2,1)S(1)}, u32[]{:S(2)}, u32[]{:S(2)}) collective-permute-start(bf16[18,16,96]{2,1,0:T(8,128)(2,1)S(1)} %get-tuple-element.26), channel_id=1, source_target_pairs={{0,2},{1,3},{2,0},{3,1},{4,6},{5,7},{6,4},{7,5},{8,10},{9,11},{10,... | collective-permute-start | bytes 165896 | tf_op jit(solution)/shard_map/ppermute | solution.py:301
  239.3 4.5 %collective-permute-start.15 = (bf16[18,16,96]{2,1,0:T(8,128)(2,1)S(1)}, bf16[18,16,96]{2,1,0:T(8,128)(2,1)S(1)}, u32[]{:S(2)}, u32[]{:S(2)}) collective-permute-start(bf16[18,16,96]{2,1,0:T(8,128)(2,1)S(1)} %get-tuple-element.27), channel_id=1, source_target_pairs={{0,3},{1,2},{2,1},{3,0},{4,7},{5,6},{6,5},{7,4},{8,11},{9,10},{10,... | collective-permute-start | bytes 165896 | tf_op jit(solution)/shard_map/ppermute | solution.py:301
  (14 other events, 39.6 us)

commit v4 on v3

--- a/solution.py
+++ b/solution.py
@@ -11,14 +11,15 @@
 
 LAGMAX = 8
 ROW_DEG = 3
-VMEM = 48 * 2**20
+VMEM = 40 * 2**20
+FULL_VMEM = 63 * 2**20
 
 
 def dft_columns(orders, longitudes):
     turns = np.arange(longitudes)[:, None] * np.arange(orders)[None, :] % longitudes
     angle = turns * (2.0 * np.pi / longitudes)
     scale = 1.0 / math.sqrt(longitudes)
-    return [(np.cos(angle) * scale).astype(jnp.bfloat16), (-np.sin(angle) * scale).astype(jnp.bfloat16)]
+    return np.stack([np.cos(angle) * scale, -np.sin(angle) * scale]).astype(jnp.bfloat16)
 
 
 def lat_columns(degrees, latitudes):
@@ -38,9 +39,9 @@
 IN_SMEM = pl.BlockSpec(memory_space=pltpu.SMEM)
 
 
-def table_from(owned, order_ref, part):
+def picks_of(owned, order_ref):
     slot_local, first, last = owned
-    slots = order_ref.shape[1]
+    slots = order_ref.shape[0]
     held = last - first
     rows = slots // slot_local * 2 * held
     column = lax.broadcasted_iota(jnp.int32, (1, rows), 1)
@@ -48,15 +49,14 @@
     odd = (place >= held).astype(jnp.int32)
     slot = owner * slot_local + 2 * (first + place - held * odd) + odd
     here = lax.broadcasted_iota(jnp.int32, (slots, rows), 0)
-    orders = jnp.broadcast_to(order_ref[...].astype(jnp.float32), (8, slots))
+    orders = jnp.broadcast_to(order_ref[...].astype(jnp.float32).reshape(1, slots), (8, slots))
     chosen = jnp.dot(
         orders,
         (here == slot).astype(jnp.float32),
         precision=lax.Precision.HIGHEST,
         preferred_element_type=jnp.float32,
     )
-    picks = (here.astype(jnp.float32) == chosen[:1]).astype(jnp.bfloat16)
-    return jnp.dot(part, picks, preferred_element_type=jnp.float32).astype(jnp.bfloat16)
+    return (here.astype(jnp.float32) == chosen[:1]).astype(jnp.bfloat16)
 
 
 def spectra_kernel(owned, order_ref, part_ref, field_ref, *refs):
@@ -64,66 +64,72 @@
 
     @pl.when(pl.program_id(0) == 0)
     def _():
-        table_ref[...] = table_from(owned, order_ref, part_ref[...])
+        table_ref[...] = jnp.dot(
+            part_ref[...], picks_of(owned, order_ref), preferred_element_type=jnp.float32
+        ).astype(jnp.bfloat16)
 
     cells = jnp.dot(field_ref[...], table_ref[...], preferred_element_type=jnp.float32)
     out_ref[...] = cells.T.astype(jnp.bfloat16)
 
 
-def first_spectra_kernel(owned, order_ref, part_hbm, field_hbm, out_ref, part_ref, field_ref, sems):
+def first_spectra_kernel(owned, part, order_ref, part_hbm, field_hbm, out_ref, part_ref, field_ref, sems):
     block = out_ref.shape[1]
-    cut = block // 256 * 128
-    pieces = [(0, cut), (cut, block)]
-    copies = [pltpu.make_async_copy(part_hbm, part_ref, sems.at[0])]
-    for index, (start, stop) in enumerate(pieces):
-        rows = pl.ds(start, stop - start)
+    tiles = block // 128
+    cuts = [128 * (tiles * i // 3) for i in range(4)]
+    part_copy = pltpu.make_async_copy(part_hbm.at[part], part_ref, sems.at[0])
+    copies = []
+    for index in range(3):
+        rows = pl.ds(cuts[index], cuts[index + 1] - cuts[index])
         copies.append(
             pltpu.make_async_copy(field_hbm.at[rows], field_ref.at[rows], sems.at[index + 1])
         )
-    for copy in copies:
+    part_copy.start()
+    copies[0].start()
+    picks = picks_of(owned, order_ref)
+    part_copy.wait()
+    for copy in copies[1:]:
         copy.start()
-    copies[0].wait()
-    table = table_from(owned, order_ref, part_ref[...])
-    for (start, stop), copy in zip(pieces, copies[1:]):
+    table = jnp.dot(part_ref[...], picks, preferred_element_type=jnp.float32).astype(jnp.bfloat16)
+    for start, stop, copy in zip(cuts, cuts[1:], copies):
         copy.wait()
         cells = jnp.dot(field_ref[start:stop], table, preferred_element_type=jnp.float32)
         out_ref[:, start:stop] = cells.T.astype(jnp.bfloat16)
 
 
-def spectra_of(order_row, owned, part, fields, block, blocks, after):
+def spectra_of(order_table, owned, parts, part, fields, block, blocks, after):
     lon_count = fields.shape[1]
     first, last = blocks
     slot_local, first_pair, last_pair = owned
-    rows = order_row.shape[1] // slot_local * 2 * (last_pair - first_pair)
+    rows = order_table.shape[0] // slot_local * 2 * (last_pair - first_pair)
     cells = (last - first) * block
-    alone = blocks == (0, 1) and block % 128 == 0 and block > 128 and not after
+    alone = blocks == (0, 1) and block % 128 == 0 and block > 256 and not after
     cost = pl.CostEstimate(
         flops=2 * rows * cells * lon_count,
         bytes_accessed=2 * (cells * lon_count + rows * (cells + lon_count)),
         transcendentals=0,
     )
     out_shape = jax.ShapeDtypeStruct((rows, cells), jnp.bfloat16)
-    params = pltpu.CompilerParams(vmem_limit_bytes=VMEM)
+    params = pltpu.CompilerParams(vmem_limit_bytes=FULL_VMEM)
     if alone:
         return pl.pallas_call(
-            functools.partial(first_spectra_kernel, owned),
+            functools.partial(first_spectra_kernel, owned, part),
             in_specs=[IN_VMEM, IN_HBM, IN_HBM],
             out_specs=IN_VMEM,
             out_shape=out_shape,
             scratch_shapes=[
-                pltpu.VMEM(part.shape, jnp.bfloat16),
+                pltpu.VMEM(parts.shape[1:], jnp.bfloat16),
                 pltpu.VMEM((block, lon_count), jnp.bfloat16),
-                pltpu.SemaphoreType.DMA((3,)),
+                pltpu.SemaphoreType.DMA((4,)),
             ],
             compiler_params=params,
             cost_estimate=cost,
-        )(order_row, part, fields)
+        )(order_table, parts, fields)
     return pl.pallas_call(
         functools.partial(spectra_kernel, owned),
         grid=(last - first,),
         in_specs=[
-            pl.BlockSpec(order_row.shape, lambda i: (0, 0)),
-            pl.BlockSpec(part.shape, lambda i: (0, 0)),
+            pl.BlockSpec(order_table.shape, lambda i: (0,)),
+            pl.BlockSpec((None,) + parts.shape[1:], lambda i: (part, 0, 0)),
             pl.BlockSpec((block, lon_count), lambda i: (i + first, 0)),
         ]
         + [ANY] * len(after),
@@ -132,7 +138,7 @@
         scratch_shapes=[pltpu.VMEM((lon_count, rows), jnp.bfloat16)],
         compiler_params=params,
         cost_estimate=cost,
-    )(order_row, part, fields, *after)
+    )(order_table, parts, fields, *after)
 
 
 def peer(me, hop, count):
@@ -148,8 +154,8 @@
     refs = refs[:-2]
     lat_copy = pltpu.make_async_copy(lat_hbm, lat_ref, lat_sem)
     lat_copy.start()
-    sends, pick_ref = refs[:narrow_count], refs[narrow_count]
-    line_ref, series_ref, block_ref = refs[narrow_count + 1 :]
+    sends, pick_refs = refs[:narrow_count], refs[narrow_count:-3]
+    line_ref, series_ref, block_ref = refs[-3:]
     days, slots, degrees = series_ref.shape
     half, padded = slots // 2, line_ref.shape[1] // 2
     start = 0
@@ -201,16 +207,17 @@
             block_ref[owner, LAGMAX : 2 * LAGMAX, rows, :] = series_ref[days - LAGMAX :, rows, own]
             block_ref[owner, 2 * LAGMAX, rows, :] = coarse[:, own]
             block_ref[owner, 2 * LAGMAX + 1, rows, :] = fine[:, own]
-    for owner in range(narrow_count):
-        kept = slice(owner * (ROW_DEG + 1), (owner + 1) * (ROW_DEG + 1))
-        first = owner * deg_local
-        pick_ref[:, :, kept] = series_ref[:, :, first : first + ROW_DEG + 1]
+    for pick_ref in pick_refs:
+        for owner in range(narrow_count):
+            kept = slice(owner * (ROW_DEG + 1), (owner + 1) * (ROW_DEG + 1))
+            first = owner * deg_local
+            pick_ref[:, :, kept] = series_ref[:, :, first : first + ROW_DEG + 1]
     me = me_ref[0]
     for hop, send in enumerate(sends):
         send[...] = block_ref[peer(me, hop, narrow_count)[0]]
 
 
-def digest(lag_days, me, received, lat_table, weights, narrow_count, after):
+def digest(lag_days, me, received, lat_table, weights, narrow_count, wants_picks, after):
     sources, slots, _ = received[0].shape
     latitudes, degrees = lat_table.shape[0], lat_table.shape[1] // 2
     lat_local = latitudes // sources
@@ -222,9 +229,9 @@
     return pl.pallas_call(
         functools.partial(digest_kernel, (len(received), narrow_count, lat_local, len(after))),
         in_specs=[IN_SMEM, IN_SMEM, IN_VMEM, IN_HBM] + [IN_VMEM] * len(received) + [ANY] * len(after),
-        out_specs=[IN_VMEM] * (narrow_count + 1),
+        out_specs=[IN_VMEM] * (narrow_count + wants_picks),
         out_shape=[jax.ShapeDtypeStruct(message, jnp.bfloat16)] * narrow_count
-        + [jax.ShapeDtypeStruct(picked, jnp.bfloat16)],
+        + [jax.ShapeDtypeStruct(picked, jnp.bfloat16)] * wants_picks,
         scratch_shapes=[
             pltpu.VMEM((days_local, padded, latitudes), jnp.bfloat16),
             pltpu.VMEM((days_local, slots, degrees), jnp.bfloat16),
@@ -232,7 +239,7 @@
             pltpu.VMEM(lat_table.shape, jnp.bfloat16),
             pltpu.SemaphoreType.DMA(()),
         ],
-        compiler_params=pltpu.CompilerParams(vmem_limit_bytes=VMEM),
+        compiler_params=pltpu.CompilerParams(vmem_limit_bytes=VMEM if slots > 32 else VMEM // 2),
         cost_estimate=pl.CostEstimate(
             flops=4 * slots * days_local * latitudes * degrees,
             bytes_accessed=2 * slots * days_local * (latitudes + degrees),
@@ -286,7 +293,7 @@
             pltpu.VMEM((count + 1, 2 * LAGMAX, slots, degrees), jnp.bfloat16),
             pltpu.VMEM((count, slots, degrees), jnp.float32),
         ],
-        compiler_params=pltpu.CompilerParams(vmem_limit_bytes=VMEM),
+        compiler_params=pltpu.CompilerParams(vmem_limit_bytes=VMEM // 2),
         cost_estimate=pl.CostEstimate(
             flops=8 * count * LAGMAX * slots * degrees,
             bytes_accessed=2 * count * days * slots * degrees,
@@ -303,21 +310,23 @@
     ]
 
 
-def gather(block, axis):
+def gather_step(held, depth, axis):
+    count = lax.axis_size(axis)
+    reach = count >> (depth + 1)
+    other = lax.ppermute(held, axis, [(i, i ^ reach) for i in range(count)])
+    upper = (lax.axis_index(axis) & reach) != 0
+    return jnp.stack([jnp.where(upper, other, held), jnp.where(upper, held, other)], axis=depth)
+
+
+def gather(block, axis, held=None):
     count = lax.axis_size(axis)
     if count & (count - 1):
         return lax.all_gather(block, axis)
-    me = lax.axis_index(axis)
-    held = block[None]
-    reach = 1
-    while reach < count:
-        other = lax.ppermute(held, axis, [(i, i ^ reach) for i in range(count)])
-        upper = (me & reach) != 0
-        held = jnp.concatenate(
-            [jnp.where(upper, other, held), jnp.where(upper, held, other)], axis=0
-        )
-        reach *= 2
-    return held
+    depth = 0 if held is None else 1
+    held = block if held is None else held
+    while count >> (depth + 1):
+        held, depth = gather_step(held, depth, axis), depth + 1
+    return held.reshape((count,) + block.shape)
 
 
 def plan_of(slot_local, days_local, day_block):
@@ -344,10 +353,8 @@
     me = lax.axis_index("narrow").astype(jnp.int32).reshape(1)
 
     fields = daily_fields.reshape(days_local * lat_local, lon_count)
-    parts = [jnp.asarray(p) for p in dft_columns(order_count, lon_count)]
+    parts = jnp.asarray(dft_columns(order_count, lon_count))
     lat_table = jnp.asarray(lat_columns(deg_count, lat_local * wide_count))
-    order_row = order_table.reshape(1, order_count)
-
     own_weights = jnp.transpose(
         lag_weights.reshape(3, deg_local, pair_local, 2, 2), (4, 3, 0, 2, 1)
     )
@@ -364,7 +371,7 @@
     def product(index, after):
         part, first, last, blocks = sent[index]
         owned = (slot_local, first, last)
-        return spectra_of(order_row, owned, parts[part], fields, day_block * lat_local, blocks, after)
+        return spectra_of(order_table, owned, parts, part, fields, day_block * lat_local, blocks, after)
 
     def exchange(spectra):
         spectra = spectra.reshape(wide_count, -1, spectra.shape[1])
@@ -372,26 +379,28 @@
 
     def finish(job, after):
         part, first, last, _ = sent[job[0]]
-        *sends, picks = digest(
+        out = digest(
             lag_days,
             me,
             [received[index] for index in job],
             lat_table,
             rows_of(all_weights, part, first, last),
             narrow_count,
+            part == 0,
             after,
         )
+        sends, picks = out[:narrow_count], out[narrow_count:]
         total = combine(
             lag_days, me, rows_of(own_weights, part, first, last), swap(sends, "narrow")
         )
         for parity in range(2):
             rows = slice(parity * (last - first), (parity + 1) * (last - first))
             spreads[part, parity, first] = total[rows]
-            if part == 0:
-                picked[parity, first] = picks[:, rows]
+            if picks:
+                picked[parity, first] = picks[0][:, rows]
         return total
 
-    def panel_of():
+    def panel_rows():
         series = jnp.stack(
             [
                 jnp.concatenate([picked[k] for k in sorted(picked) if k[0] == parity], axis=1)
@@ -417,7 +426,11 @@
         rounded = residual.astype(jnp.bfloat16)
         rows = rounded[:, :, :ROW_DEG].reshape(slot_local, narrow_count * ROW_DEG, kept_days)
         column = lax.dynamic_index_in_dim(rounded[:, :, ROW_DEG], me[0], 1, False)
-        columns = gather(column, "wide").reshape(order_count, kept_days)
+        held = column if wide_count & (wide_count - 1) else gather_step(column, 0, "wide")
+        return rows, column, held
+
+    def panel_of(rows, column, held):
+        columns = gather(column, "wide", held).reshape(order_count, kept_days)
         product = lax.dot_general(
             rows, columns, (((2,), (1,)), ((), ())), preferred_element_type=jnp.float32
         )
@@ -431,12 +444,13 @@
     if len(sent) == 2:
         received.append(exchange(spectra[1]))
     done = [finish(jobs[0], [])]
-    panel = panel_of()
-    done.append(panel)
+    rows, column, held = panel_rows()
     if len(sent) > 2:
-        received.append(exchange(tie(spectra[len(sent) - 1], done)))
-    for job in jobs[1:]:
-        done = [finish(job, done)]
+        received.append(exchange(tie(spectra[len(sent) - 1], done + [held])))
+    panel = panel_of(rows, column, held)
+    for job in jobs[1:-1]:
+        done.append(finish(job, []))
+    finish(jobs[-1], done + [panel])
 
     spread = jnp.stack(
         [

time: 246 us -> 241 us (0.980)
  waiting for transfers between devices: 123 us -> 91.6 us
  local copies, waits for them, and re-layouts: 15.1 us -> 32.9 us
  other arithmetic: 2.79 us -> 9.49 us
    ppermute x7, waiting for transfers between devices: 47.2 us -> 24.7 us  [gather_step(): other = lax.ppermute(held, axis, [(i, i ^ reach) for i in range(count)])]
    another operation x5 -> x7, local copies, waits for them, and re-layouts: 0.82 us -> 8.82 us  [the longest x3 4.14 us: panel_rows(): jnp.stack([jnp.concatenate([picked[k] for k in sorted(picked) if k[0] ==...]
    all_to_all x4, waiting for transfers between devices: 65.9 us -> 58.5 us  [exchange(): lax.all_to_all(spectra, 'wide', split_axis=0, concat_axis=0, tiled=True)]
    another operation x1 -> x15, other arithmetic: 0.04 us -> 6.64 us  [the longest x14 5.03 us: gather_step(): jnp.stack([jnp.where(upper, other, held), jnp.where(upper, held, other)],...]
    unnamed x38 -> x48, local copies, waits for them, and re-layouts: 10.1 us -> 4.55 us
    slice x7 -> x8, local copies, waits for them, and re-layouts: 0.87 us -> 5.24 us  [the longest x4 4.56 us: panel_rows(): residual = residual - weights[position] * shifted.astype(jnp.float32)]
    transpose x2, local copies, waits for them, and re-layouts: 0.63 us -> 3.64 us  [the longest x1 2.66 us: panel_rows(): jnp.moveaxis(series, 0, 3)]
    pallas_call x3, Pallas kernels: 23 us -> 20.2 us  [digest(): pl.pallas_call(functools.partial(digest_kernel, (len(received), narrow_co...]
  transfers between devices with their start and end apart: 20 -> 20, of which waited for: 14 -> 13; matrix products, arithmetic and copies ran while one was open for 4% -> 16% of each run, Pallas kernels for 21% -> 22%
where the time goes in v4:
time: 241 us; the launch traced here: 240 us
  waiting for transfers between devices  91.6 us (38%)
  Pallas kernels  65 us (27%)
  starting transfers between devices  35.8 us (15%)
  local copies, waits for them, and re-layouts  32.9 us (14%)
  other arithmetic  9.49 us (4%)
  between operations  5.05 us (2%)
    all_to_all x4, waiting for transfers between devices, exchange(): lax.all_to_all(spectra, 'wide', split_axis=0, concat_axis=0, tiled=True)  58.5 us
    pallas_call x3, Pallas kernels, spectra_of(): pl.pallas_call(functools.partial(spectra_kernel, owned), grid=(last - fir...  35.1 us
    ppermute x7, waiting for transfers between devices, gather_step(): other = lax.ppermute(held, axis, [(i, i ^ reach) for i in range(count)])  24.7 us
    all_to_all x4, starting transfers between devices, exchange(): lax.all_to_all(spectra, 'wide', split_axis=0, concat_axis=0, tiled=True)  20.5 us
    pallas_call x3, Pallas kernels, digest(): pl.pallas_call(functools.partial(digest_kernel, (len(received), narrow_co...  20.2 us
    ppermute x7, starting transfers between devices, gather_step(): other = lax.ppermute(held, axis, [(i, i ^ reach) for i in range(count)])  9.39 us
    ppermute x9, waiting for transfers between devices, swap(): lax.ppermute(sends[hop], axis, [(i, peer(i, hop, count)[0]) for i in rang...  8.42 us
    pallas_call x1, Pallas kernels, spectra_of(): pl.pallas_call(functools.partial(first_spectra_kernel, owned, part), in_s...  6.8 us
  transfers between devices with their start and end apart: 20, of which 13 were waited for; matrix products, arithmetic and copies ran while one was open for 16% of the time, Pallas kernels for 22%

profile of v4, /device:TPU:0, one launch (start us, length us, event | category | flops | bytes accessed | tf_op | source)
XLA Modules:
  0.0 240.1 jit_solution(11529500893671433039)
XLA Ops:
  0.6 6.8 %shard_map.77.refs_0_ = bf16[384,1408]{1,0:T(8,128)(2,1)} custom-call(s32[384]{0:T(512)} %order_ref.7, bf16[2,1440,384]{2,1,0:T(8,128)(2,1)} %constant.45.clone.part_hbm.part_ref, bf16[5632,1440]{1,0:T(8,128)(2,1)} %bitcast.121), custom_call_target="tpu_custom_call" | custom-call | flops 1557135360 | bytes 6242304 | tf_op jit(solution)/shard_map/pallas_call | solution.py:114
  7.4 7.3 %all-to-all-start = ((bf16[8,48,1408]{2,1,0:T(8,128)(2,1)}), bf16[8,48,1408]{2,1,0:T(8,128)(2,1)}, u32[]{:S(2)}, u32[]{:S(2)}) async-start(bf16[8,48,1408]{2,1,0:T(8,128)(2,1)} %bitcast.128), calls=%async_computation | async-start | bytes 2162688 | tf_op jit(solution)/shard_map/all_to_all | solution.py:378
  14.7 12.5 %shard_map.78.refs_0_ = bf16[384,4224]{1,0:T(8,128)(2,1)} custom-call(s32[384]{0:T(512)} %order_ref.7, bf16[2,1440,384]{2,1,0:T(8,128)(2,1)} %constant.45.clone.part_hbm.part_ref, bf16[5632,1440]{1,0:T(8,128)(2,1)} %bitcast.122, bf16[384,1408]{1,0:T(8,128)(2,1)} %shard_map.77.refs_0_), custom_call_target="tpu_custom_call" | custom-call | flops 4671406080 | bytes 16515072 | tf_op jit(solution)/shard_map/pallas_call | solution.py:127
  27.3 14.0 %all-to-all-done.refs_0_ = bf16[8,48,1408]{2,1,0:T(8,128)(2,1)} async-done(((bf16[8,48,1408]{2,1,0:T(8,128)(2,1)}), bf16[8,48,1408]{2,1,0:T(8,128)(2,1)}, u32[]{:S(2)}, u32[]{:S(2)}) %all-to-all-start) | async-done | bytes 1081376 | tf_op jit(solution)/shard_map/all_to_all | solution.py:378
  41.3 4.6 %all-to-all-start.1 = ((bf16[8,48,4224]{2,1,0:T(8,128)(2,1)}), bf16[8,48,4224]{2,1,0:T(8,128)(2,1)}, u32[]{:S(2)}, u32[]{:S(2)}) async-start(bf16[8,48,4224]{2,1,0:T(8,128)(2,1)} %bitcast.125), calls=%async_computation.1 | async-start | bytes 6488064 | tf_op jit(solution)/shard_map/all_to_all | solution.py:378
  47.5 3.6 %collective-permute-done = f32[2,2,3,24,96]{4,3,2,1,0:T(8,128)S(1)} collective-permute-done((f32[2,2,3,24,96]{4,3,2,1,0:T(8,128)S(1)}, f32[2,2,3,24,96]{4,3,2,1,0:T(8,128)S(1)}, u32[]{:S(2)}, u32[]{:S(2)}) %collective-permute-start) | collective-permute-done | bytes 110624 | tf_op jit(solution)/shard_map/ppermute | solution.py:316
  55.3 10.9 %shard_map.81.refs_0_ = bf16[128,5632]{1,0:T(8,128)(2,1)} custom-call(s32[384]{0:T(512)} %order_ref.7, bf16[2,1440,384]{2,1,0:T(8,128)(2,1)} %constant.45.clone.part_hbm.part_ref, bf16[5632,1440]{1,0:T(8,128)(2,1)} %bitcast.123, bf16[384,4224]{1,0:T(8,128)(2,1)} %shard_map.78.refs_0_, f32[2,2,3,24,384]{4,3,2,1,0:T(8,128)} %reshape.75.refs_1_), custom_call_target="tpu_custom_call" | custom-call | flops 2076180480 | bytes 18030592 | tf_op jit(solution)/shard_map/pallas_call | solution.py:127
  66.2 11.6 %shard_map.82 = bf16[256,5632]{1,0:T(8,128)(2,1)} custom-call(s32[384]{0:T(512)} %order_ref.7, bf16[2,1440,384]{2,1,0:T(8,128)(2,1)} %constant.45.clone.part_hbm.part_ref, bf16[5632,1440]{1,0:T(8,128)(2,1)} %bitcast.124, bf16[128,5632]{1,0:T(8,128)(2,1)} %shard_map.81.refs_0_, f32[2,2,3,24,384]{4,3,2,1,0:T(8,128)} %reshape.75.refs_1_), custom_call_target="tpu_custom_call" | custom-call | flops 4152360960 | bytes 19841024 | tf_op jit(solution)/shard_map/pallas_call | solution.py:127
  77.9 40.3 %all-to-all-done.1.refs_1_ = bf16[8,48,4224]{2,1,0:T(8,128)(2,1)} async-done(((bf16[8,48,4224]{2,1,0:T(8,128)(2,1)}), bf16[8,48,4224]{2,1,0:T(8,128)(2,1)}, u32[]{:S(2)}, u32[]{:S(2)}) %all-to-all-start.1) | async-done | bytes 3244064 | tf_op jit(solution)/shard_map/all_to_all | solution.py:378
  118.2 4.0 %all-to-all-start.2 = ((bf16[8,32,5632]{2,1,0:T(8,128)(2,1)}), bf16[8,32,5632]{2,1,0:T(8,128)(2,1)S(1)}, u32[]{:S(2)}, u32[]{:S(2)}) async-start(bf16[8,32,5632]{2,1,0:T(8,128)(2,1)} %bitcast.127), calls=%async_computation.2 | async-start | bytes 5767168 | tf_op jit(solution)/shard_map/all_to_all | solution.py:378
  130.2 9.6 %shard_map.79 = (bf16[18,48,96]{2,1,0:T(8,128)(2,1)S(1)}, bf16[18,48,96]{2,1,0:T(8,128)(2,1)S(1)}, bf16[18,48,96]{2,1,0:T(8,128)(2,1)S(1)}, bf16[18,48,96]{2,1,0:T(8,128)(2,1)S(1)}, bf16[64,48,16]{2,1,0:T(8,128)(2,1)S(1)}) custom-call(s32[3]{0:T(128)S(1)} %copy-done.2, s32[1]{0:T(128)} %bitcast.me_ref, f32[3,48,384]{2,1,0:T(8,128)S(1)} %pad_maximum_fusion.3.weight_ref, ...), custom_call_target="tpu_custom_call" | custom-call | flops 3321888768 | bytes 6684672 | tf_op jit(solution)/shard_map/pallas_call | solution.py:229
  164.4 2.9 %reshape_reshape.6 = bf16[4,48,4,4,64]{4,3,2,1,0:T(4,128)(2,1)} reshape(bf16[2,2,48,1024]{3,2,1,0:T(8,128)(2,1)} %pad_maximum_fusion.1) | data formatting | bytes 786432 | tf_op jit(solution)/shard_map/reshape;reshape | solution.py:414
  167.4 2.7 %copy.55 = bf16[48,4,4,4,64]{4,3,0,2,1:T(4,128)(2,1)} copy(bf16[48,4,4,4,64]{4,2,1,0,3:T(4,128)(2,1)} %bitcast.131) | data formatting | bytes 786432 | tf_op jit(solution)/shard_map/transpose | solution.py:415
  170.0 2.5 %reshape.82 = bf16[48,4,4,256]{3,0,2,1:T(8,128)(2,1)} reshape(bf16[48,4,4,4,64]{4,3,0,2,1:T(4,128)(2,1)} %copy.55) | data formatting | bytes 786432 | tf_op jit(solution)/shard_map/reshape | solution.py:415
  172.5 2.4 %subtract_convert_fusion = bf16[48,4,4,248]{3,0,2,1:T(8,128)(2,1)S(1)} fusion(bf16[48,4,4,256]{3,0,2,1:T(8,128)(2,1)} %reshape.82, s32[]{:T(128)S(6)} %select_n.112, f32[48,4,4]{0,2,1:T(4,128)S(1)} %copy.61, s32[]{:T(128)S(6)} %select_n.111, f32[48,4,4]{0,2,1:T(4,128)S(1)} %copy.59, s32[]{:T(128)S(6)} %select_n.110, f32[48,4,4]{0,2,1:T(4,128)S(1)} %copy.57), kind=kLoop, calls=%fused_computation.1 | loop fusion | flops 2095104 | bytes 1913868 | tf_op jit(solution)/shard_map/convert_element_type | solution.py:426
  175.7 2.7 %collective-permute-start.10 = (bf16[48,248]{1,0:T(8,128)(2,1)}, bf16[48,248]{1,0:T(8,128)(2,1)}, u32[]{:S(2)}, u32[]{:S(2)}) collective-permute-start(bf16[48,248]{1,0:T(8,128)(2,1)} %dynamic-slice_bitcast_fusion), channel_id=1, source_target_pairs={{0,16},{4,20},{8,24},{12,28},{16,0},{20,4},{24,8},{28,12},{1,17},{... | collective-permute-start | bytes 71432 | tf_op jit(solution)/shard_map/ppermute | solution.py:316
  180.5 7.9 %collective-permute-done.10 = bf16[48,248]{1,0:T(8,128)(2,1)} collective-permute-done((bf16[48,248]{1,0:T(8,128)(2,1)}, bf16[48,248]{1,0:T(8,128)(2,1)}, u32[]{:S(2)}, u32[]{:S(2)}) %collective-permute-start.10) | collective-permute-done | bytes 23840 | tf_op jit(solution)/shard_map/ppermute | solution.py:316
  189.8 4.6 %all-to-all-start.3 = ((bf16[8,16,5632]{2,1,0:T(8,128)(2,1)}), bf16[8,16,5632]{2,1,0:T(8,128)(2,1)}, u32[]{:S(2)}, u32[]{:S(2)}) async-start(bf16[8,16,5632]{2,1,0:T(8,128)(2,1)} %bitcast.126), calls=%async_computation.3 | async-start | bytes 2883584 | tf_op jit(solution)/shard_map/all_to_all | solution.py:378
  195.9 6.2 %shard_map.83 = (bf16[18,32,96]{2,1,0:T(8,128)(2,1)S(1)}, bf16[18,32,96]{2,1,0:T(8,128)(2,1)S(1)}, bf16[18,32,96]{2,1,0:T(8,128)(2,1)S(1)}, bf16[18,32,96]{2,1,0:T(8,128)(2,1)S(1)}) custom-call(s32[3]{0:T(128)S(1)} %copy-done.2, s32[1]{0:T(128)} %bitcast.me_ref, f32[3,32,384]{2,1,0:T(8,128)S(1)} %pad_maximum_fusion.7.weight_ref, ...), custom_call_target="tpu_custom_call" | custom-call | flops 2214592512 | bytes 4456448 | tf_op jit(solution)/shard_map/pallas_call | solution.py:229
  205.7 3.2 %collective-permute-done.6.refs_2_ = bf16[18,32,96]{2,1,0:T(8,128)(2,1)S(1)} collective-permute-done((bf16[18,32,96]{2,1,0:T(8,128)(2,1)S(1)}, bf16[18,32,96]{2,1,0:T(8,128)(2,1)S(1)}, u32[]{:S(2)}, u32[]{:S(2)}) %collective-permute-start.6) | collective-permute-done | bytes 110624 | tf_op jit(solution)/shard_map/ppermute | solution.py:308
  211.9 6.2 %collective-permute-done.11 = bf16[2,48,248]{2,1,0:T(8,128)(2,1)S(1)} collective-permute-done((bf16[2,48,248]{2,1,0:T(8,128)(2,1)S(1)}, bf16[2,48,248]{2,1,0:T(8,128)(2,1)S(1)}, u32[]{:S(2)}, u32[]{:S(2)}) %collective-permute-start.11) | collective-permute-done | bytes 47648 | tf_op jit(solution)/shard_map/ppermute | solution.py:316
  220.0 3.2 %collective-permute-done.12 = bf16[2,2,48,248]{3,2,0,1:T(8,128)(2,1)S(1)} collective-permute-done((bf16[2,2,48,248]{3,2,0,1:T(8,128)(2,1)S(1)}, bf16[2,2,48,248]{3,2,0,1:T(8,128)(2,1)S(1)}, u32[]{:S(2)}, u32[]{:S(2)}) %collective-permute-start.12) | collective-permute-done | bytes 95264 | tf_op jit(solution)/shard_map/ppermute | solution.py:316
  224.0 4.1 %all-to-all-done.3.refs_0_ = bf16[8,16,5632]{2,1,0:T(8,128)(2,1)} async-done(((bf16[8,16,5632]{2,1,0:T(8,128)(2,1)}), bf16[8,16,5632]{2,1,0:T(8,128)(2,1)}, u32[]{:S(2)}, u32[]{:S(2)}) %all-to-all-start.3) | async-done | bytes 1441824 | tf_op jit(solution)/shard_map/all_to_all | solution.py:378
  228.2 4.4 %shard_map.86 = (bf16[18,16,96]{2,1,0:T(8,128)(2,1)S(1)}, bf16[18,16,96]{2,1,0:T(8,128)(2,1)S(1)}, bf16[18,16,96]{2,1,0:T(8,128)(2,1)S(1)}, bf16[18,16,96]{2,1,0:T(8,128)(2,1)S(1)}) custom-call(s32[3]{0:T(128)S(1)} %copy-done.2, s32[1]{0:T(128)} %bitcast.me_ref, f32[3,16,384]{2,1,0:T(8,128)S(1)} %pad_maximum_fusion.10.weight_ref, ...), custom_call_target="tpu_custom_call" | custom-call | flops 1107296256 | bytes 2228224 | tf_op jit(solution)/shard_map/pallas_call | solution.py:229
  (139 shorter events, 56.7 us)
Async XLA Ops:
  7.4 33.9 %all-to-all-start = ((bf16[8,48,1408]{2,1,0:T(8,128)(2,1)}), bf16[8,48,1408]{2,1,0:T(8,128)(2,1)}, u32[]{:S(2)}, u32[]{:S(2)}) async-start(bf16[8,48,1408]{2,1,0:T(8,128)(2,1)} %bitcast.128), calls=%async_computation | async-start | bytes 2162688 | tf_op jit(solution)/shard_map/all_to_all | solution.py:378
  41.3 76.8 %all-to-all-start.1 = ((bf16[8,48,4224]{2,1,0:T(8,128)(2,1)}), bf16[8,48,4224]{2,1,0:T(8,128)(2,1)}, u32[]{:S(2)}, u32[]{:S(2)}) async-start(bf16[8,48,4224]{2,1,0:T(8,128)(2,1)} %bitcast.125), calls=%async_computation.1 | async-start | bytes 6488064 | tf_op jit(solution)/shard_map/all_to_all | solution.py:378
  46.0 5.2 %collective-permute-start = (f32[2,2,3,24,96]{4,3,2,1,0:T(8,128)S(1)}, f32[2,2,3,24,96]{4,3,2,1,0:T(8,128)S(1)}, u32[]{:S(2)}, u32[]{:S(2)}) collective-permute-start(f32[2,2,3,24,96]{4,3,2,1,0:T(8,128)S(1)} %bitcast.135), channel_id=1, source_target_pairs={{0,2},{1,3},{2,0},{3,1},{4,6},{5,7},{6,4},{7,5},{8,10},{9,11},{10,... | collective-permute-start | bytes 331784 | tf_op jit(solution)/shard_map/ppermute | solution.py:316
  51.2 1.6 collective-permute-start.1
  118.2 10.3 %copy-start.9 = (f32[2,2,3,24,384]{4,3,2,1,0:T(8,128)S(1)}, f32[2,2,3,24,384]{4,3,2,1,0:T(8,128)}, u32[]{:S(2)}) copy-start(f32[2,2,3,24,384]{4,3,2,1,0:T(8,128)} %reshape.75.refs_1_) | copy-start | bytes 1327108
  118.2 71.6 %all-to-all-start.2 = ((bf16[8,32,5632]{2,1,0:T(8,128)(2,1)}), bf16[8,32,5632]{2,1,0:T(8,128)(2,1)S(1)}, u32[]{:S(2)}, u32[]{:S(2)}) async-start(bf16[8,32,5632]{2,1,0:T(8,128)(2,1)} %bitcast.127), calls=%async_computation.2 | async-start | bytes 5767168 | tf_op jit(solution)/shard_map/all_to_all | solution.py:378
  139.9 20.7 %copy-start.4 = (bf16[18,48,96]{2,1,0:T(8,128)(2,1)}, bf16[18,48,96]{2,1,0:T(8,128)(2,1)S(1)}, u32[]{:S(2)}) copy-start(bf16[18,48,96]{2,1,0:T(8,128)(2,1)S(1)} %get-tuple-element.17) | copy-start | bytes 497668
  146.7 4.7 %collective-permute-start.8 = (bf16[48,1024]{1,0:T(8,128)(2,1)S(1)}, bf16[48,1024]{1,0:T(8,128)(2,1)S(1)}, u32[]{:S(2)}, u32[]{:S(2)}) collective-permute-start(bf16[48,1024]{1,0:T(8,128)(2,1)S(1)} %reshape.81), channel_id=1, source_target_pairs={{0,2},{1,3},{2,0},{3,1},{4,6},{5,7},{6,4},{7,5},{8,10},{9,11},{10,... | collective-permute-start | bytes 294920 | tf_op jit(solution)/shard_map/ppermute | solution.py:316
  153.1 9.6 %collective-permute-start.9 = (bf16[2,48,1024]{2,1,0:T(8,128)(2,1)}, bf16[2,48,1024]{2,1,0:T(8,128)(2,1)}, u32[]{:S(2)}, u32[]{:S(2)}) collective-permute-start(bf16[2,48,1024]{2,1,0:T(8,128)(2,1)} %pad_maximum_fusion.5), channel_id=1, source_target_pairs={{0,1},{1,0},{2,3},{3,2},{4,5},{5,4},{6,7},{7,6},{8,9},{9,8},{10,11... | collective-permute-start | bytes 589832 | tf_op jit(solution)/shard_map/ppermute | solution.py:316
  160.6 17.9 %collective-permute-start.2 = (bf16[18,48,96]{2,1,0:T(8,128)(2,1)}, bf16[18,48,96]{2,1,0:T(8,128)(2,1)S(1)}, u32[]{:S(2)}, u32[]{:S(2)}) collective-permute-start(bf16[18,48,96]{2,1,0:T(8,128)(2,1)} %copy-done.5), channel_id=1, source_target_pairs={{0,1},{1,0},{2,3},{3,2},{4,5},{5,4},{6,7},{7,6},{8,9},{9,8},{10,11... | collective-permute-start | bytes 497672 | tf_op jit(solution)/shard_map/ppermute | solution.py:308
  161.1 17.3 %collective-permute-start.3 = (bf16[18,48,96]{2,1,0:T(8,128)(2,1)}, bf16[18,48,96]{2,1,0:T(8,128)(2,1)}, u32[]{:S(2)}, u32[]{:S(2)}) collective-permute-start(bf16[18,48,96]{2,1,0:T(8,128)(2,1)} %copy-done.4), channel_id=1, source_target_pairs={{0,2},{1,3},{2,0},{3,1},{4,6},{5,7},{6,4},{7,5},{8,10},{9,11},{10,... | collective-permute-start | bytes 497672 | tf_op jit(solution)/shard_map/ppermute | solution.py:308
  162.6 15.8 %collective-permute-start.4 = (bf16[18,48,96]{2,1,0:T(8,128)(2,1)}, bf16[18,48,96]{2,1,0:T(8,128)(2,1)}, u32[]{:S(2)}, u32[]{:S(2)}) collective-permute-start(bf16[18,48,96]{2,1,0:T(8,128)(2,1)} %copy-done.3), channel_id=1, source_target_pairs={{0,3},{1,2},{2,1},{3,0},{4,7},{5,6},{6,5},{7,4},{8,11},{9,10},{10,... | collective-permute-start | bytes 497672 | tf_op jit(solution)/shard_map/ppermute | solution.py:308
  170.0 8.4 %copy-start.17 = (f32[3,24,96]{2,1,0:T(8,128)S(1)}, f32[3,24,96]{2,1,0:T(8,128)}, u32[]{:S(2)}) copy-start(f32[3,24,96]{2,1,0:T(8,128)} %get-tuple-element.59) | copy-start | bytes 82948
  175.7 12.7 %collective-permute-start.10 = (bf16[48,248]{1,0:T(8,128)(2,1)}, bf16[48,248]{1,0:T(8,128)(2,1)}, u32[]{:S(2)}, u32[]{:S(2)}) collective-permute-start(bf16[48,248]{1,0:T(8,128)(2,1)} %dynamic-slice_bitcast_fusion), channel_id=1, source_target_pairs={{0,16},{4,20},{8,24},{12,28},{16,0},{20,4},{24,8},{28,12},{1,17},{... | collective-permute-start | bytes 71432 | tf_op jit(solution)/shard_map/ppermute | solution.py:316
  189.8 38.3 %all-to-all-start.3 = ((bf16[8,16,5632]{2,1,0:T(8,128)(2,1)}), bf16[8,16,5632]{2,1,0:T(8,128)(2,1)}, u32[]{:S(2)}, u32[]{:S(2)}) async-start(bf16[8,16,5632]{2,1,0:T(8,128)(2,1)} %bitcast.126), calls=%async_computation.3 | async-start | bytes 2883584 | tf_op jit(solution)/shard_map/all_to_all | solution.py:378
  202.1 3.6 %collective-permute-start.5 = (bf16[18,32,96]{2,1,0:T(8,128)(2,1)S(1)}, bf16[18,32,96]{2,1,0:T(8,128)(2,1)S(1)}, u32[]{:S(2)}, u32[]{:S(2)}) collective-permute-start(bf16[18,32,96]{2,1,0:T(8,128)(2,1)S(1)} %get-tuple-element.20), channel_id=1, source_target_pairs={{0,1},{1,0},{2,3},{3,2},{4,5},{5,4},{6,7},{7,6},{8,9},{9,8},{10,11... | collective-permute-start | bytes 331784 | tf_op jit(solution)/shard_map/ppermute | solution.py:308
  202.1 6.7 %collective-permute-start.6 = (bf16[18,32,96]{2,1,0:T(8,128)(2,1)S(1)}, bf16[18,32,96]{2,1,0:T(8,128)(2,1)S(1)}, u32[]{:S(2)}, u32[]{:S(2)}) collective-permute-start(bf16[18,32,96]{2,1,0:T(8,128)(2,1)S(1)} %get-tuple-element.21), channel_id=1, source_target_pairs={{0,2},{1,3},{2,0},{3,1},{4,6},{5,7},{6,4},{7,5},{8,10},{9,11},{10,... | collective-permute-start | bytes 331784 | tf_op jit(solution)/shard_map/ppermute | solution.py:308
  203.7 7.4 %collective-permute-start.7 = (bf16[18,32,96]{2,1,0:T(8,128)(2,1)S(1)}, bf16[18,32,96]{2,1,0:T(8,128)(2,1)S(1)}, u32[]{:S(2)}, u32[]{:S(2)}) collective-permute-start(bf16[18,32,96]{2,1,0:T(8,128)(2,1)S(1)} %get-tuple-element.22), channel_id=1, source_target_pairs={{0,3},{1,2},{2,1},{3,0},{4,7},{5,6},{6,5},{7,4},{8,11},{9,10},{10,... | collective-permute-start | bytes 331784 | tf_op jit(solution)/shard_map/ppermute | solution.py:308
  204.0 14.1 %collective-permute-start.11 = (bf16[2,48,248]{2,1,0:T(8,128)(2,1)S(1)}, bf16[2,48,248]{2,1,0:T(8,128)(2,1)S(1)}, u32[]{:S(2)}, u32[]{:S(2)}) collective-permute-start(bf16[2,48,248]{2,1,0:T(8,128)(2,1)S(1)} %copy-done.16), channel_id=1, source_target_pairs={{0,8},{4,12},{8,0},{12,4},{16,24},{20,28},{24,16},{28,20},{1,9},{5... | collective-permute-start | bytes 142856 | tf_op jit(solution)/shard_map/ppermute | solution.py:316
  205.7 17.6 %slice-start = ((bf16[48,4,4,248]{3,0,2,1:T(8,128)(2,1)}), bf16[48,4,3,248]{3,0,2,1:T(8,128)(2,1)S(1)}, s32[]{:S(2)}) async-start(bf16[48,4,4,248]{3,0,2,1:T(8,128)(2,1)} %copy-done.12), calls=%async_computation.4 | async-start | bytes 589824 | tf_op jit(solution)/shard_map/slice | solution.py:427
  218.2 5.0 %collective-permute-start.12 = (bf16[2,2,48,248]{3,2,0,1:T(8,128)(2,1)S(1)}, bf16[2,2,48,248]{3,2,0,1:T(8,128)(2,1)S(1)}, u32[]{:S(2)}, u32[]{:S(2)}) collective-permute-start(bf16[2,2,48,248]{3,2,0,1:T(8,128)(2,1)S(1)} %pad_maximum_fusion.8), channel_id=1, source_target_pairs={{0,4},{4,0},{8,12},{12,8},{16,20},{20,16},{24,28},{28,24},{1,5},{5... | collective-permute-start | bytes 285704 | tf_op jit(solution)/shard_map/ppermute | solution.py:316
  232.6 3.1 %collective-permute-start.13 = (bf16[18,16,96]{2,1,0:T(8,128)(2,1)S(1)}, bf16[18,16,96]{2,1,0:T(8,128)(2,1)S(1)}, u32[]{:S(2)}, u32[]{:S(2)}) collective-permute-start(bf16[18,16,96]{2,1,0:T(8,128)(2,1)S(1)} %get-tuple-element.25), channel_id=1, source_target_pairs={{0,1},{1,0},{2,3},{3,2},{4,5},{5,4},{6,7},{7,6},{8,9},{9,8},{10,11... | collective-permute-start | bytes 165896 | tf_op jit(solution)/shard_map/ppermute | solution.py:308
  232.6 4.8 %collective-permute-start.14 = (bf16[18,16,96]{2,1,0:T(8,128)(2,1)S(1)}, bf16[18,16,96]{2,1,0:T(8,128)(2,1)S(1)}, u32[]{:S(2)}, u32[]{:S(2)}) collective-permute-start(bf16[18,16,96]{2,1,0:T(8,128)(2,1)S(1)} %get-tuple-element.26), channel_id=1, source_target_pairs={{0,2},{1,3},{2,0},{3,1},{4,6},{5,7},{6,4},{7,5},{8,10},{9,11},{10,... | collective-permute-start | bytes 165896 | tf_op jit(solution)/shard_map/ppermute | solution.py:308
  234.2 4.5 %collective-permute-start.15 = (bf16[18,16,96]{2,1,0:T(8,128)(2,1)S(1)}, bf16[18,16,96]{2,1,0:T(8,128)(2,1)S(1)}, u32[]{:S(2)}, u32[]{:S(2)}) collective-permute-start(bf16[18,16,96]{2,1,0:T(8,128)(2,1)S(1)} %get-tuple-element.27), channel_id=1, source_target_pairs={{0,3},{1,2},{2,1},{3,0},{4,7},{5,6},{6,5},{7,4},{8,11},{9,10},{10,... | collective-permute-start | bytes 165896 | tf_op jit(solution)/shard_map/ppermute | solution.py:308
  (20 other events, 71.7 us)

commit v5 on v4

--- a/solution.py
+++ b/solution.py
@@ -39,13 +39,13 @@
 IN_SMEM = pl.BlockSpec(memory_space=pltpu.SMEM)
 
 
-def picks_of(owned, order_ref):
+def picks_of(owned, order_ref, swapped=0):
     slot_local, first, last = owned
     slots = order_ref.shape[0]
     held = last - first
     rows = slots // slot_local * 2 * held
     column = lax.broadcasted_iota(jnp.int32, (1, rows), 1)
-    owner, place = lax.div(column, 2 * held), lax.rem(column, 2 * held)
+    owner, place = lax.div(column, 2 * held) ^ swapped, lax.rem(column, 2 * held)
     odd = (place >= held).astype(jnp.int32)
     slot = owner * slot_local + 2 * (first + place - held * odd) + odd
     here = lax.broadcasted_iota(jnp.int32, (slots, rows), 0)
@@ -72,20 +72,21 @@
     out_ref[...] = cells.T.astype(jnp.bfloat16)
 
 
-def first_spectra_kernel(owned, part, order_ref, part_hbm, field_hbm, out_ref, part_ref, field_ref, sems):
-    block = out_ref.shape[1]
+def first_spectra_kernel(owned, part, order_ref, part_hbm, field_hbm, *refs):
+    outs, (part_ref, field_ref, sems) = refs[:-3], refs[-3:]
+    rows, block = outs[0].shape
     tiles = block // 128
     cuts = [128 * (tiles * i // 3) for i in range(4)]
     part_copy = pltpu.make_async_copy(part_hbm.at[part], part_ref, sems.at[0])
     copies = []
     for index in range(3):
-        rows = pl.ds(cuts[index], cuts[index + 1] - cuts[index])
+        cells = pl.ds(cuts[index], cuts[index + 1] - cuts[index])
         copies.append(
-            pltpu.make_async_copy(field_hbm.at[rows], field_ref.at[rows], sems.at[index + 1])
+            pltpu.make_async_copy(field_hbm.at[cells], field_ref.at[cells], sems.at[index + 1])
         )
     part_copy.start()
     copies[0].start()
-    picks = picks_of(owned, order_ref)
+    picks = picks_of(owned, order_ref, lax.axis_index("wide"))
     part_copy.wait()
     for copy in copies[1:]:
         copy.start()
@@ -93,7 +94,33 @@
     for start, stop, copy in zip(cuts, cuts[1:], copies):
         copy.wait()
         cells = jnp.dot(field_ref[start:stop], table, preferred_element_type=jnp.float32)
-        out_ref[:, start:stop] = cells.T.astype(jnp.bfloat16)
+        cells = cells.T.astype(jnp.bfloat16)
+        for hop, out_ref in enumerate(outs):
+            out_ref[:, start:stop] = cells[hop * rows : (hop + 1) * rows]
+
+
+def first_spectra_of(order_table, owned, parts, part, fields, block):
+    lon_count = fields.shape[1]
+    slot_local, first_pair, last_pair = owned
+    hops = order_table.shape[0] // slot_local
+    rows = 2 * (last_pair - first_pair)
+    return pl.pallas_call(
+        functools.partial(first_spectra_kernel, owned, part),
+        in_specs=[IN_VMEM, IN_HBM, IN_HBM],
+        out_specs=[IN_VMEM] * hops,
+        out_shape=[jax.ShapeDtypeStruct((rows, block), jnp.bfloat16)] * hops,
+        scratch_shapes=[
+            pltpu.VMEM(parts.shape[1:], jnp.bfloat16),
+            pltpu.VMEM((block, lon_count), jnp.bfloat16),
+            pltpu.SemaphoreType.DMA((4,)),
+        ],
+        compiler_params=pltpu.CompilerParams(vmem_limit_bytes=FULL_VMEM),
+        cost_estimate=pl.CostEstimate(
+            flops=2 * hops * rows * block * lon_count,
+            bytes_accessed=2 * (block * lon_count + hops * rows * (block + lon_count)),
+            transcendentals=0,
+        ),
+    )(order_table, parts, fields)
 
 
 def spectra_of(order_table, owned, parts, part, fields, block, blocks, after):
@@ -102,7 +129,6 @@
     slot_local, first_pair, last_pair = owned
     rows = order_table.shape[0] // slot_local * 2 * (last_pair - first_pair)
     cells = (last - first) * block
-    alone = blocks == (0, 1) and block % 128 == 0 and block > 256 and not after
     cost = pl.CostEstimate(
         flops=2 * rows * cells * lon_count,
         bytes_accessed=2 * (cells * lon_count + rows * (cells + lon_count)),
@@ -110,20 +136,6 @@
     )
     out_shape = jax.ShapeDtypeStruct((rows, cells), jnp.bfloat16)
     params = pltpu.CompilerParams(vmem_limit_bytes=FULL_VMEM)
-    if alone:
-        return pl.pallas_call(
-            functools.partial(first_spectra_kernel, owned, part),
-            in_specs=[IN_VMEM, IN_HBM, IN_HBM],
-            out_specs=IN_VMEM,
-            out_shape=out_shape,
-            scratch_shapes=[
-                pltpu.VMEM(parts.shape[1:], jnp.bfloat16),
-                pltpu.VMEM((block, lon_count), jnp.bfloat16),
-                pltpu.SemaphoreType.DMA((4,)),
-            ],
-            compiler_params=params,
-            cost_estimate=cost,
-        )(order_table, parts, fields)
     return pl.pallas_call(
         functools.partial(spectra_kernel, owned),
         grid=(last - first,),
@@ -148,12 +160,20 @@
 
 
 def digest_kernel(shape, lag_ref, me_ref, weight_ref, lat_hbm, *refs):
-    groups, narrow_count, lat_local, n_after = shape
-    blocks, refs = refs[:groups], refs[groups + n_after :]
-    lat_ref, lat_sem = refs[-2:]
-    refs = refs[:-2]
-    lat_copy = pltpu.make_async_copy(lat_hbm, lat_ref, lat_sem)
-    lat_copy.start()
+    groups, hops, narrow_count, lat_local, n_after = shape
+    by_hop, blocks, refs = refs[:hops], list(refs[hops : hops + groups]), refs[hops + groups + n_after :]
+    lat_ref, stage_ref, sems = refs[-3:]
+    refs = refs[:-3]
+    copies = [pltpu.make_async_copy(lat_hbm, lat_ref, sems.at[hops])]
+    for hop, ref in enumerate(by_hop):
+        source = me_ref[1] ^ hop
+        copies.append(pltpu.make_async_copy(ref, stage_ref.at[source], sems.at[hop]))
+    for copy in copies:
+        copy.start()
+    if hops:
+        blocks.insert(0, stage_ref)
+        for copy in copies[1:]:
+            copy.wait()
     sends, pick_refs = refs[:narrow_count], refs[narrow_count:-3]
     line_ref, series_ref, block_ref = refs[-3:]
     days, slots, degrees = series_ref.shape
@@ -171,7 +191,7 @@
                     line_ref[day, :half, lats] = block[source, :half, cells]
                     line_ref[day, padded : padded + half, lats] = block[source, half:, cells]
         if start == 0:
-            lat_copy.wait()
+            copies[0].wait()
         for parity in range(2):
             lines = line_ref[start:stop, parity * padded : (parity + 1) * padded, :]
             coeffs = jnp.dot(
@@ -218,17 +238,24 @@
 
 
 def digest(lag_days, me, received, lat_table, weights, narrow_count, wants_picks, after):
+    by_hop = received[0] if isinstance(received[0], list) else []
+    received = received[1:] if by_hop else received
     sources, slots, _ = received[0].shape
     latitudes, degrees = lat_table.shape[0], lat_table.shape[1] // 2
     lat_local = latitudes // sources
-    days_local = sum(block.shape[2] for block in received) // lat_local
+    days_local = sum(block.shape[-1] for block in by_hop[:1] + received) // lat_local
     deg_local = degrees // narrow_count
     padded = 2 * (-(-(slots // 2) // 8) * 8)
     message = (2 * LAGMAX + 2, slots, deg_local)
     picked = (days_local, slots, narrow_count * (ROW_DEG + 1))
     return pl.pallas_call(
-        functools.partial(digest_kernel, (len(received), narrow_count, lat_local, len(after))),
-        in_specs=[IN_SMEM, IN_SMEM, IN_VMEM, IN_HBM] + [IN_VMEM] * len(received) + [ANY] * len(after),
+        functools.partial(
+            digest_kernel, (len(received), len(by_hop), narrow_count, lat_local, len(after))
+        ),
+        in_specs=[IN_SMEM, IN_SMEM, IN_VMEM, IN_HBM]
+        + [ANY] * len(by_hop)
+        + [IN_VMEM] * len(received)
+        + [ANY] * len(after),
         out_specs=[IN_VMEM] * (narrow_count + wants_picks),
         out_shape=[jax.ShapeDtypeStruct(message, jnp.bfloat16)] * narrow_count
         + [jax.ShapeDtypeStruct(picked, jnp.bfloat16)] * wants_picks,
@@ -237,15 +264,16 @@
             pltpu.VMEM((days_local, slots, degrees), jnp.bfloat16),
             pltpu.VMEM((narrow_count,) + message, jnp.bfloat16),
             pltpu.VMEM(lat_table.shape, jnp.bfloat16),
-            pltpu.SemaphoreType.DMA(()),
+            pltpu.VMEM((sources,) + by_hop[0].shape if by_hop else (8, 128), jnp.bfloat16),
+            pltpu.SemaphoreType.DMA((len(by_hop) + 1,)),
         ],
-        compiler_params=pltpu.CompilerParams(vmem_limit_bytes=VMEM if slots > 32 else VMEM // 2),
+        compiler_params=pltpu.CompilerParams(vmem_limit_bytes=VMEM if slots > 32 else VMEM // 2 if slots > 16 else FULL_VMEM - 2**20),
         cost_estimate=pl.CostEstimate(
             flops=4 * slots * days_local * latitudes * degrees,
             bytes_accessed=2 * slots * days_local * (latitudes + degrees),
             transcendentals=0,
         ),
-    )(lag_days, me, weights, lat_table, *received, *after)
+    )(lag_days, me, weights, lat_table, *by_hop, *received, *after)
 
 
 def tie(array, after):
@@ -258,10 +286,10 @@
     )(array, *after)
 
 
-def combine_kernel(count, lag_ref, me_ref, weight_ref, *refs):
-    got, out_ref, seam_ref, sum_ref = refs[:count], refs[count], refs[count + 1], refs[count + 2]
+def combine_kernel(count, final, lag_ref, me_ref, weight_ref, *refs):
+    got, others, (out_ref, seam_ref, sum_ref) = refs[:count], refs[count:-3], refs[-3:]
     me = me_ref[0]
-    total = jnp.zeros(out_ref.shape, jnp.float32)
+    total = jnp.zeros(sum_ref.shape[1:], jnp.float32)
     for hop in range(count):
         source = peer(me, hop, count)[1]
         seam_ref[source, LAGMAX:] = got[hop][:LAGMAX]
@@ -278,17 +306,32 @@
             for lag, weight in zip(lags, weights):
                 residual = residual - weight * seam_ref[block, day - lag].astype(jnp.float32)
             total = total + residual * residual
-    out_ref[...] = total
-
-
-def combine(lag_days, me, weights, got):
+    if final is None:
+        out_ref[...] = total
+        return
+    sum_ref[0] = total
+    kept_days, places = final
+    for source, (part, first, last) in zip([*others, sum_ref.at[0]], places):
+        held = last - first
+        for parity in range(2):
+            for pair in range(first, last):
+                row = parity * held + pair - first
+                out_ref[2 * pair + parity, part : part + 1, :] = (
+                    source[row : row + 1, :] / kept_days
+                )
+
+
+def combine(lag_days, me, weights, got, others=(), final=None):
     count = len(got)
     days, slots, degrees = got[0].shape
+    shape = (slots, degrees)
+    if final is not None:
+        shape = (2 * max(last for _, _, last in final[1]), 2, degrees)
     return pl.pallas_call(
-        functools.partial(combine_kernel, count),
-        in_specs=[IN_SMEM, IN_SMEM] + [IN_VMEM] * (count + 1),
+        functools.partial(combine_kernel, count, final),
+        in_specs=[IN_SMEM, IN_SMEM] + [IN_VMEM] * (count + 1 + len(others)),
         out_specs=IN_VMEM,
-        out_shape=jax.ShapeDtypeStruct((slots, degrees), jnp.float32),
+        out_shape=jax.ShapeDtypeStruct(shape, jnp.float32),
         scratch_shapes=[
             pltpu.VMEM((count + 1, 2 * LAGMAX, slots, degrees), jnp.bfloat16),
             pltpu.VMEM((count, slots, degrees), jnp.float32),
@@ -299,7 +342,7 @@
             bytes_accessed=2 * count * days * slots * degrees,
             transcendentals=0,
         ),
-    )(lag_days, me, weights, *got)
+    )(lag_days, me, weights, *got, *others)
 
 
 def swap(sends, axis):
@@ -310,29 +353,30 @@
     ]
 
 
-def gather_step(held, depth, axis):
+def gather_swap(held, depth, axis):
     count = lax.axis_size(axis)
     reach = count >> (depth + 1)
-    other = lax.ppermute(held, axis, [(i, i ^ reach) for i in range(count)])
-    upper = (lax.axis_index(axis) & reach) != 0
-    return jnp.stack([jnp.where(upper, other, held), jnp.where(upper, held, other)], axis=depth)
-
-
-def gather(block, axis, held=None):
+    return lax.ppermute(held, axis, [(i, i ^ reach) for i in range(count)])
+
+
+def gather(block, axis, other=None):
     count = lax.axis_size(axis)
     if count & (count - 1):
         return lax.all_gather(block, axis)
-    depth = 0 if held is None else 1
-    held = block if held is None else held
+    held, depth = block, 0
     while count >> (depth + 1):
-        held, depth = gather_step(held, depth, axis), depth + 1
+        if depth or other is None:
+            other = gather_swap(held, depth, axis)
+        upper = (lax.axis_index(axis) & (count >> (depth + 1))) != 0
+        pair = [jnp.where(upper, other, held), jnp.where(upper, held, other)]
+        held, depth = jnp.stack(pair, axis=depth), depth + 1
     return held.reshape((count,) + block.shape)
 
 
-def plan_of(slot_local, days_local, day_block):
+def plan_of(slot_local, days_local, day_block, wide_count):
     pairs, blocks = slot_local // 2, days_local // day_block
     every = (0, blocks)
-    if slot_local % 48 == 0 and blocks > 1:
+    if slot_local % 48 == 0 and blocks > 1 and wide_count & (wide_count - 1) == 0:
         cut = pairs * 2 // 3
         sent = [(0, 0, pairs, (0, 1)), (0, 0, pairs, (1, blocks)), (1, 0, cut, every), (1, cut, pairs, every)]
         return sent, [(0, 1), (2,), (3,)]
@@ -350,7 +394,7 @@
     deg_count = deg_local * narrow_count
     kept_days = days_local * narrow_count - LAGMAX
     day_block = math.gcd(128 // math.gcd(128, lat_local), days_local)
-    me = lax.axis_index("narrow").astype(jnp.int32).reshape(1)
+    me = jnp.stack([lax.axis_index("narrow"), lax.axis_index("wide")]).astype(jnp.int32)
 
     fields = daily_fields.reshape(days_local * lat_local, lon_count)
     parts = jnp.asarray(dft_columns(order_count, lon_count))
@@ -364,8 +408,7 @@
     def rows_of(weights, part, first, last):
         return jnp.concatenate([weights[part, parity, :, first:last] for parity in range(2)], axis=1)
 
-    sent, jobs = plan_of(slot_local, days_local, day_block)
-    spreads = {}
+    sent, jobs = plan_of(slot_local, days_local, day_block, wide_count)
     picked = {}
 
     def product(index, after):
@@ -373,11 +416,19 @@
         owned = (slot_local, first, last)
         return spectra_of(order_table, owned, parts, part, fields, day_block * lat_local, blocks, after)
 
+    def first_exchange():
+        part, first, last, _ = sent[0]
+        owned = (slot_local, first, last)
+        spectra = first_spectra_of(
+            order_table, owned, parts, part, fields, day_block * lat_local
+        )
+        return spectra[0], swap(spectra, "wide")
+
     def exchange(spectra):
         spectra = spectra.reshape(wide_count, -1, spectra.shape[1])
         return lax.all_to_all(spectra, "wide", split_axis=0, concat_axis=0, tiled=True)
 
-    def finish(job, after):
+    def finish(job, after, others=(), final=None):
         part, first, last, _ = sent[job[0]]
         out = digest(
             lag_days,
@@ -391,11 +442,15 @@
         )
         sends, picks = out[:narrow_count], out[narrow_count:]
         total = combine(
-            lag_days, me, rows_of(own_weights, part, first, last), swap(sends, "narrow")
+            lag_days,
+            me,
+            rows_of(own_weights, part, first, last),
+            swap(sends, "narrow"),
+            others,
+            final,
         )
         for parity in range(2):
             rows = slice(parity * (last - first), (parity + 1) * (last - first))
-            spreads[part, parity, first] = total[rows]
             if picks:
                 picked[parity, first] = picks[0][:, rows]
         return total
@@ -426,46 +481,38 @@
         rounded = residual.astype(jnp.bfloat16)
         rows = rounded[:, :, :ROW_DEG].reshape(slot_local, narrow_count * ROW_DEG, kept_days)
         column = lax.dynamic_index_in_dim(rounded[:, :, ROW_DEG], me[0], 1, False)
-        held = column if wide_count & (wide_count - 1) else gather_step(column, 0, "wide")
-        return rows, column, held
-
-    def panel_of(rows, column, held):
-        columns = gather(column, "wide", held).reshape(order_count, kept_days)
+        far = None if wide_count & (wide_count - 1) else gather_swap(column, 0, "wide")
+        return rows, column, far
+
+    def panel_of(rows, column, far):
+        columns = gather(column, "wide", far).reshape(order_count, kept_days)
         product = lax.dot_general(
             rows, columns, (((2,), (1,)), ((), ())), preferred_element_type=jnp.float32
         )
         return product / math.sqrt(kept_days)
 
-    spectra = {0: product(0, [])}
-    spectra[1] = before = product(1, [spectra[0]])
-    for index in reversed(range(2, len(sent))):
-        before = spectra[index] = product(index, [before, all_weights])
-    received = [exchange(spectra[index]) for index in range(len(sent) - 1)]
-    if len(sent) == 2:
-        received.append(exchange(spectra[1]))
+    spectra, received = {}, []
+    if len(sent) > 2:
+        first, blocks = first_exchange()
+        received.append(blocks)
+        spectra[1] = product(1, [first])
+        spectra[1] = before = tie(spectra[1], blocks[1:])
+        for index in reversed(range(2, len(sent))):
+            before = spectra[index] = product(index, [before, all_weights])
+        received += [exchange(spectra[index]) for index in range(1, len(sent) - 1)]
+    else:
+        for index in range(len(sent)):
+            received.append(exchange(product(index, [])))
     done = [finish(jobs[0], [])]
-    rows, column, held = panel_rows()
+    rows, column, far = panel_rows()
     if len(sent) > 2:
-        received.append(exchange(tie(spectra[len(sent) - 1], done + [held])))
-    panel = panel_of(rows, column, held)
+        received.append(exchange(tie(spectra[len(sent) - 1], done + [far])))
+    panel = panel_of(rows, column, far)
     for job in jobs[1:-1]:
         done.append(finish(job, []))
-    finish(jobs[-1], done + [panel])
-
-    spread = jnp.stack(
-        [
-            jnp.stack(
-                [
-                    jnp.concatenate(
-                        [spreads[k] for k in sorted(spreads) if k[:2] == (part, parity)], axis=0
-                    )
-                    for part in range(2)
-                ]
-            )
-            for parity in range(2)
-        ]
-    )
-    noise_variance = jnp.transpose(spread / kept_days, (3, 2, 0, 1)).reshape(deg_local, slot_local, 2)
+    places = [sent[job[0]][:3] for job in jobs]
+    variances = finish(jobs[-1], done + [panel], done, (kept_days, places))
+    noise_variance = jnp.transpose(variances, (2, 0, 1))
     return (noise_variance, panel)
 
 

time: 241 us -> 238 us (0.988)
  waiting for transfers between devices: 91.6 us -> 75.1 us
  starting transfers between devices: 35.8 us -> 45.5 us
  Pallas kernels: 65 us -> 68 us
    all_to_all x4 -> x3, waiting for transfers between devices: 58.5 us -> 43.8 us  [exchange(): lax.all_to_all(spectra, 'wide', split_axis=0, concat_axis=0, tiled=True)]
    ppermute x9 -> x16, starting transfers between devices: 5.93 us -> 19.5 us  [swap(): lax.ppermute(sends[hop], axis, [(i, peer(i, hop, count)[0]) for i in rang...]
    all_to_all x4 -> x3, starting transfers between devices: 20.5 us -> 16.2 us  [exchange(): lax.all_to_all(spectra, 'wide', split_axis=0, concat_axis=0, tiled=True)]
    unnamed x48 -> x83, local copies, waits for them, and re-layouts: 4.55 us -> 8.29 us
    ppermute x9 -> x16, waiting for transfers between devices: 8.42 us -> 5.17 us  [swap(): lax.ppermute(sends[hop], axis, [(i, peer(i, hop, count)[0]) for i in rang...]
    pallas_call x7, Pallas kernels: 29.9 us -> 33 us  [the longest x3 22.8 us: digest(): pl.pallas_call(functools.partial(digest_kernel, (len(received), len(by_ho...]
    another operation x17 -> x15, other arithmetic: 5.05 us -> 4.57 us  [the longest x14 4.5 us: gather(): held, depth = (jnp.stack(pair, axis=depth), depth + 1)]
  transfers between devices with their start and end apart: 20 -> 26, of which waited for: 13 -> 12; matrix products, arithmetic and copies ran while one was open for 16% -> 15% of each run, Pallas kernels for 22% -> 23%
where the time goes in v5:
time: 238 us; the launch traced here: 237 us
  waiting for transfers between devices  75.1 us (32%)
  Pallas kernels  68 us (29%)
  starting transfers between devices  45.5 us (19%)
  local copies, waits for them, and re-layouts  32.5 us (14%)
  other arithmetic  10 us (4%)
  between operations  5.09 us (2%)
    all_to_all x3, waiting for transfers between devices, exchange(): lax.all_to_all(spectra, 'wide', split_axis=0, concat_axis=0, tiled=True)  43.8 us
    pallas_call x3, Pallas kernels, spectra_of(): pl.pallas_call(functools.partial(spectra_kernel, owned), grid=(last - fir...  35 us
    ppermute x7, waiting for transfers between devices, gather_swap(): return lax.ppermute(held, axis, [(i, i ^ reach) for i in range(count)])  26.1 us
    pallas_call x3, Pallas kernels, digest(): pl.pallas_call(functools.partial(digest_kernel, (len(received), len(by_ho...  22.8 us
    ppermute x16, starting transfers between devices, swap(): lax.ppermute(sends[hop], axis, [(i, peer(i, hop, count)[0]) for i in rang...  19.5 us
    all_to_all x3, starting transfers between devices, exchange(): lax.all_to_all(spectra, 'wide', split_axis=0, concat_axis=0, tiled=True)  16.2 us
    ppermute x7, starting transfers between devices, gather_swap(): return lax.ppermute(held, axis, [(i, i ^ reach) for i in range(count)])  9.75 us
    unnamed x83, local copies, waits for them, and re-layouts  8.29 us
  transfers between devices with their start and end apart: 26, of which 12 were waited for; matrix products, arithmetic and copies ran while one was open for 15% of the time, Pallas kernels for 23%

profile of v5, /device:TPU:0, one launch (start us, length us, event | category | flops | bytes accessed | tf_op | source)
XLA Modules:
  0.0 236.6 jit_solution(17955117929306153885)
XLA Ops:
  0.6 6.7 %shard_map.77 = (bf16[48,1408]{1,0:T(8,128)(2,1)}, bf16[48,1408]{1,0:T(8,128)(2,1)}, bf16[48,1408]{1,0:T(8,128)(2,1)}, bf16[48,1408]{1,0:T(8,128)(2,1)}, bf16[48...) custom-call(s32[384]{0:T(512)} %order_ref.7, ...), custom_call_target="tpu_custom_call" | custom-call | flops 1557135360 | bytes 6242304 | tf_op jit(solution)/shard_map/pallas_call | solution.py:107
  7.4 3.0 %collective-permute-start.2 = (bf16[48,1408]{1,0:T(8,128)(2,1)}, bf16[48,1408]{1,0:T(8,128)(2,1)S(1)}, u32[]{:S(2)}, u32[]{:S(2)}) collective-permute-start(bf16[48,1408]{1,0:T(8,128)(2,1)} %get-tuple-element.24), channel_id=1, source_target_pairs={{0,4},{4,0},{8,12},{12,8},{16,20},{20,16},{24,28},{28,24},{1,5},{5... | collective-permute-start | bytes 405512 | tf_op jit(solution)/shard_map/ppermute | solution.py:351
  12.0 3.0 %collective-permute-start.5 = (bf16[48,1408]{1,0:T(8,128)(2,1)}, bf16[48,1408]{1,0:T(8,128)(2,1)S(1)}, u32[]{:S(2)}, u32[]{:S(2)}) collective-permute-start(bf16[48,1408]{1,0:T(8,128)(2,1)} %get-tuple-element.27), channel_id=1, source_target_pairs={{0,16},{4,20},{8,24},{12,28},{16,0},{20,4},{24,8},{28,12},{1,17},{... | collective-permute-start | bytes 405512 | tf_op jit(solution)/shard_map/ppermute | solution.py:351
  16.2 3.6 %collective-permute-start.7 = (bf16[48,1408]{1,0:T(8,128)(2,1)}, bf16[48,1408]{1,0:T(8,128)(2,1)S(1)}, u32[]{:S(2)}, u32[]{:S(2)}) collective-permute-start(bf16[48,1408]{1,0:T(8,128)(2,1)} %get-tuple-element.29), channel_id=1, source_target_pairs={{0,24},{4,28},{8,16},{12,20},{16,8},{20,12},{24,0},{28,4},{1,25},{... | collective-permute-start | bytes 405512 | tf_op jit(solution)/shard_map/ppermute | solution.py:351
  22.4 12.5 %shard_map.78.refs_0_ = bf16[384,4224]{1,0:T(8,128)(2,1)} custom-call(s32[384]{0:T(512)} %order_ref.7, bf16[2,1440,384]{2,1,0:T(8,128)(2,1)} %constant.42.clone.part_hbm.part_ref, bf16[5632,1440]{1,0:T(8,128)(2,1)} %bitcast.108, bf16[48,1408]{1,0:T(8,128)(2,1)} %get-tuple-element.23.refs_0_), custom_call_target="tpu_custom_call" | custom-call | flops 4671406080 | bytes 16515072 | tf_op jit(solution)/shard_map/pallas_call | solution.py:139
  35.8 7.6 %all-to-all-start = ((bf16[8,48,4224]{2,1,0:T(8,128)(2,1)}), bf16[8,48,4224]{2,1,0:T(8,128)(2,1)}, u32[]{:S(2)}, u32[]{:S(2)}) async-start(bf16[8,48,4224]{2,1,0:T(8,128)(2,1)} %bitcast.111), calls=%async_computation | async-start | bytes 6488064 | tf_op jit(solution)/shard_map/all_to_all | solution.py:429
  45.0 3.6 %collective-permute-done = f32[2,2,3,24,96]{4,3,2,1,0:T(8,128)S(1)} collective-permute-done((f32[2,2,3,24,96]{4,3,2,1,0:T(8,128)S(1)}, f32[2,2,3,24,96]{4,3,2,1,0:T(8,128)S(1)}, u32[]{:S(2)}, u32[]{:S(2)}) %collective-permute-start) | collective-permute-done | bytes 110624 | tf_op jit(solution)/shard_map/ppermute | solution.py:359
  52.8 10.9 %shard_map.80.refs_0_ = bf16[128,5632]{1,0:T(8,128)(2,1)} custom-call(s32[384]{0:T(512)} %order_ref.7, bf16[2,1440,384]{2,1,0:T(8,128)(2,1)} %constant.42.clone.part_hbm.part_ref, bf16[5632,1440]{1,0:T(8,128)(2,1)} %bitcast.109, bf16[384,4224]{1,0:T(8,128)(2,1)} %shard_map.79.refs_0_, f32[2,2,3,24,384]{4,3,2,1,0:T(8,128)} %reshape.65.refs_1_), custom_call_target="tpu_custom_call" | custom-call | flops 2076180480 | bytes 18030592 | tf_op jit(solution)/shard_map/pallas_call | solution.py:139
  63.7 11.6 %shard_map.84 = bf16[256,5632]{1,0:T(8,128)(2,1)} custom-call(s32[384]{0:T(512)} %order_ref.7, bf16[2,1440,384]{2,1,0:T(8,128)(2,1)} %constant.42.clone.part_hbm.part_ref, bf16[5632,1440]{1,0:T(8,128)(2,1)} %bitcast.110, bf16[128,5632]{1,0:T(8,128)(2,1)} %shard_map.80.refs_0_, f32[2,2,3,24,384]{4,3,2,1,0:T(8,128)} %reshape.65.refs_1_), custom_call_target="tpu_custom_call" | custom-call | flops 4152360960 | bytes 19841024 | tf_op jit(solution)/shard_map/pallas_call | solution.py:139
  75.3 40.7 %all-to-all-done.refs_8_ = bf16[8,48,4224]{2,1,0:T(8,128)(2,1)} async-done(((bf16[8,48,4224]{2,1,0:T(8,128)(2,1)}), bf16[8,48,4224]{2,1,0:T(8,128)(2,1)}, u32[]{:S(2)}, u32[]{:S(2)}) %all-to-all-start) | async-done | bytes 3244064 | tf_op jit(solution)/shard_map/all_to_all | solution.py:429
  115.9 4.0 %all-to-all-start.2 = ((bf16[8,32,5632]{2,1,0:T(8,128)(2,1)}), bf16[8,32,5632]{2,1,0:T(8,128)(2,1)S(1)}, u32[]{:S(2)}, u32[]{:S(2)}) async-start(bf16[8,32,5632]{2,1,0:T(8,128)(2,1)} %bitcast.113), calls=%async_computation.2 | async-start | bytes 5767168 | tf_op jit(solution)/shard_map/all_to_all | solution.py:429
  132.7 11.4 %shard_map.81 = (bf16[18,48,96]{2,1,0:T(8,128)(2,1)S(1)}, bf16[18,48,96]{2,1,0:T(8,128)(2,1)}, bf16[18,48,96]{2,1,0:T(8,128)(2,1)S(1)}, bf16[18,48,96]{2,1,0:T(8,128)(2,1)S(1)}, bf16[64,48,16]{2,1,0:T(8,128)(2,1)S(1)}) custom-call(s32[3]{0:T(128)S(1)} %copy-done.18, s32[2]{0:T(128)S(1)} %pad_add_fusion.me_ref, ...), custom_call_target="tpu_custom_call" | custom-call | flops 3321888768 | bytes 6684672 | tf_op jit(solution)/shard_map/pallas_call | solution.py:251
  164.1 2.9 %reshape_reshape.6 = bf16[4,48,4,4,64]{4,3,2,1,0:T(4,128)(2,1)} reshape(bf16[2,2,48,1024]{3,2,1,0:T(8,128)(2,1)} %pad_maximum_fusion.1) | data formatting | bytes 786432 | tf_op jit(solution)/shard_map/reshape;reshape | solution.py:469
  167.0 2.6 %copy.52 = bf16[48,4,4,4,64]{4,3,0,2,1:T(4,128)(2,1)} copy(bf16[48,4,4,4,64]{4,2,1,0,3:T(4,128)(2,1)} %bitcast.116) | data formatting | bytes 786432 | tf_op jit(solution)/shard_map/transpose | solution.py:470
  169.7 2.5 %reshape.70 = bf16[48,4,4,256]{3,0,2,1:T(8,128)(2,1)} reshape(bf16[48,4,4,4,64]{4,3,0,2,1:T(4,128)(2,1)} %copy.52) | data formatting | bytes 786432 | tf_op jit(solution)/shard_map/reshape | solution.py:470
  172.2 2.4 %subtract_convert_fusion = bf16[48,4,4,248]{3,0,2,1:T(8,128)(2,1)S(1)} fusion(bf16[48,4,4,256]{3,0,2,1:T(8,128)(2,1)} %reshape.70, s32[]{:T(128)S(6)} %select_n.111, f32[48,4,4]{0,2,1:T(4,128)} %copy.58, s32[]{:T(128)S(6)} %select_n.110, f32[48,4,4]{0,2,1:T(4,128)} %copy.56, s32[]{:T(128)S(6)} %select_n.109, f32[48,4,4]{0,2,1:T(4,128)} %copy.54), kind=kLoop, calls=%fused_computation.1 | loop fusion | flops 2095104 | bytes 1913868 | tf_op jit(solution)/shard_map/convert_element_type | solution.py:481
  174.7 2.7 %collective-permute-start.14 = (bf16[48,248]{1,0:T(8,128)(2,1)S(1)}, bf16[48,248]{1,0:T(8,128)(2,1)}, u32[]{:S(2)}, u32[]{:S(2)}) collective-permute-start(bf16[48,248]{1,0:T(8,128)(2,1)S(1)} %dynamic-slice_bitcast_fusion), channel_id=1, source_target_pairs={{0,16},{4,20},{8,24},{12,28},{16,0},{20,4},{24,8},{28,12},{1,17},{... | collective-permute-start | bytes 71432 | tf_op jit(solution)/shard_map/ppermute | solution.py:359
  179.4 5.8 %collective-permute-done.14.refs_2_ = bf16[48,248]{1,0:T(8,128)(2,1)} collective-permute-done((bf16[48,248]{1,0:T(8,128)(2,1)S(1)}, bf16[48,248]{1,0:T(8,128)(2,1)}, u32[]{:S(2)}, u32[]{:S(2)}) %collective-permute-start.14) | collective-permute-done | bytes 23840 | tf_op jit(solution)/shard_map/ppermute | solution.py:359
  185.2 4.6 %all-to-all-start.1 = ((bf16[8,16,5632]{2,1,0:T(8,128)(2,1)}), bf16[8,16,5632]{2,1,0:T(8,128)(2,1)}, u32[]{:S(2)}, u32[]{:S(2)}) async-start(bf16[8,16,5632]{2,1,0:T(8,128)(2,1)} %bitcast.112), calls=%async_computation.1 | async-start | bytes 2883584 | tf_op jit(solution)/shard_map/all_to_all | solution.py:429
  193.7 6.2 %shard_map.85 = (bf16[18,32,96]{2,1,0:T(8,128)(2,1)S(1)}, bf16[18,32,96]{2,1,0:T(8,128)(2,1)S(1)}, bf16[18,32,96]{2,1,0:T(8,128)(2,1)S(1)}, bf16[18,32,96]{2,1,0:T(8,128)(2,1)S(1)}) custom-call(s32[3]{0:T(128)S(1)} %copy-done.18, s32[2]{0:T(128)S(1)} %pad_add_fusion.me_ref, f32[3,32,384]{2,1,0:T(8,128)S(1)} %pad_maximum_fusion.7.weight_ref, ...), custom_call_target="tpu_custom_call" | custom-call | flops 2214592512 | bytes 4456448 | tf_op jit(solution)/shard_map/pallas_call | solution.py:251
  200.0 1.9 collective-permute-start.16
  202.0 11.5 %collective-permute-done.18 = bf16[2,48,248]{2,1,0:T(8,128)(2,1)S(1)} collective-permute-done((bf16[2,48,248]{2,1,0:T(8,128)(2,1)S(1)}, bf16[2,48,248]{2,1,0:T(8,128)(2,1)S(1)}, u32[]{:S(2)}, u32[]{:S(2)}) %collective-permute-start.18) | collective-permute-done | bytes 47648 | tf_op jit(solution)/shard_map/ppermute | solution.py:359
  220.4 3.1 %all-to-all-done.1.refs_0_ = bf16[8,16,5632]{2,1,0:T(8,128)(2,1)} async-done(((bf16[8,16,5632]{2,1,0:T(8,128)(2,1)}), bf16[8,16,5632]{2,1,0:T(8,128)(2,1)}, u32[]{:S(2)}, u32[]{:S(2)}) %all-to-all-start.1) | async-done | bytes 1441824 | tf_op jit(solution)/shard_map/all_to_all | solution.py:429
  223.5 5.2 %shard_map.87 = (bf16[18,16,96]{2,1,0:T(8,128)(2,1)}, bf16[18,16,96]{2,1,0:T(8,128)(2,1)}, bf16[18,16,96]{2,1,0:T(8,128)(2,1)}, bf16[18,16,96]{2,1,0:T(8,128)(2,1)}) custom-call(s32[3]{0:T(128)} %lag_ref.11, s32[2]{0:T(128)} %copy-done.20, f32[3,16,384]{2,1,0:T(8,128)} %pad_maximum_fusion.9.weight_ref, bf16[704,768]{1,0:T(8,128)(2,1)} %constant.43.clone.lat_hbm, ...), custom_call_target="tpu_custom_call" | custom-call | flops 1107296256 | bytes 2228224 | tf_op jit(solution)/shard_map/pallas_call | solution.py:251
  (180 shorter events, 61.3 us)
Async XLA Ops:
  7.4 8.9 %collective-permute-start.2 = (bf16[48,1408]{1,0:T(8,128)(2,1)}, bf16[48,1408]{1,0:T(8,128)(2,1)S(1)}, u32[]{:S(2)}, u32[]{:S(2)}) collective-permute-start(bf16[48,1408]{1,0:T(8,128)(2,1)} %get-tuple-element.24), channel_id=1, source_target_pairs={{0,4},{4,0},{8,12},{12,8},{16,20},{20,16},{24,28},{28,24},{1,5},{5... | collective-permute-start | bytes 405512 | tf_op jit(solution)/shard_map/ppermute | solution.py:351
  10.4 11.3 %collective-permute-start.3 = (bf16[48,1408]{1,0:T(8,128)(2,1)}, bf16[48,1408]{1,0:T(8,128)(2,1)S(1)}, u32[]{:S(2)}, u32[]{:S(2)}) collective-permute-start(bf16[48,1408]{1,0:T(8,128)(2,1)} %get-tuple-element.25), channel_id=1, source_target_pairs={{0,8},{4,12},{8,0},{12,4},{16,24},{20,28},{24,16},{28,20},{1,9},{5... | collective-permute-start | bytes 405512 | tf_op jit(solution)/shard_map/ppermute | solution.py:351
  12.0 23.0 %collective-permute-start.4 = (bf16[48,1408]{1,0:T(8,128)(2,1)}, bf16[48,1408]{1,0:T(8,128)(2,1)S(1)}, u32[]{:S(2)}, u32[]{:S(2)}) collective-permute-start(bf16[48,1408]{1,0:T(8,128)(2,1)} %get-tuple-element.26), channel_id=1, source_target_pairs={{0,12},{4,8},{8,4},{12,0},{16,28},{20,24},{24,20},{28,16},{1,13},{... | collective-permute-start | bytes 405512 | tf_op jit(solution)/shard_map/ppermute | solution.py:351
  12.0 23.0 %collective-permute-start.5 = (bf16[48,1408]{1,0:T(8,128)(2,1)}, bf16[48,1408]{1,0:T(8,128)(2,1)S(1)}, u32[]{:S(2)}, u32[]{:S(2)}) collective-permute-start(bf16[48,1408]{1,0:T(8,128)(2,1)} %get-tuple-element.27), channel_id=1, source_target_pairs={{0,16},{4,20},{8,24},{12,28},{16,0},{20,4},{24,8},{28,12},{1,17},{... | collective-permute-start | bytes 405512 | tf_op jit(solution)/shard_map/ppermute | solution.py:351
  14.9 20.1 %collective-permute-start.6 = (bf16[48,1408]{1,0:T(8,128)(2,1)}, bf16[48,1408]{1,0:T(8,128)(2,1)S(1)}, u32[]{:S(2)}, u32[]{:S(2)}) collective-permute-start(bf16[48,1408]{1,0:T(8,128)(2,1)} %get-tuple-element.28), channel_id=1, source_target_pairs={{0,20},{4,16},{8,28},{12,24},{16,4},{20,0},{24,12},{28,8},{1,21},{... | collective-permute-start | bytes 405512 | tf_op jit(solution)/shard_map/ppermute | solution.py:351
  16.2 18.8 %collective-permute-start.7 = (bf16[48,1408]{1,0:T(8,128)(2,1)}, bf16[48,1408]{1,0:T(8,128)(2,1)S(1)}, u32[]{:S(2)}, u32[]{:S(2)}) collective-permute-start(bf16[48,1408]{1,0:T(8,128)(2,1)} %get-tuple-element.29), channel_id=1, source_target_pairs={{0,24},{4,28},{8,16},{12,20},{16,8},{20,12},{24,0},{28,4},{1,25},{... | collective-permute-start | bytes 405512 | tf_op jit(solution)/shard_map/ppermute | solution.py:351
  21.7 13.4 %collective-permute-start.8 = (bf16[48,1408]{1,0:T(8,128)(2,1)}, bf16[48,1408]{1,0:T(8,128)(2,1)}, u32[]{:S(2)}, u32[]{:S(2)}) collective-permute-start(bf16[48,1408]{1,0:T(8,128)(2,1)} %get-tuple-element.30), channel_id=1, source_target_pairs={{0,28},{4,24},{8,20},{12,16},{16,12},{20,8},{24,4},{28,0},{1,29},{... | collective-permute-start | bytes 405512 | tf_op jit(solution)/shard_map/ppermute | solution.py:351
  35.8 80.1 %all-to-all-start = ((bf16[8,48,4224]{2,1,0:T(8,128)(2,1)}), bf16[8,48,4224]{2,1,0:T(8,128)(2,1)}, u32[]{:S(2)}, u32[]{:S(2)}) async-start(bf16[8,48,4224]{2,1,0:T(8,128)(2,1)} %bitcast.111), calls=%async_computation | async-start | bytes 6488064 | tf_op jit(solution)/shard_map/all_to_all | solution.py:429
  43.5 5.2 %collective-permute-start = (f32[2,2,3,24,96]{4,3,2,1,0:T(8,128)S(1)}, f32[2,2,3,24,96]{4,3,2,1,0:T(8,128)S(1)}, u32[]{:S(2)}, u32[]{:S(2)}) collective-permute-start(f32[2,2,3,24,96]{4,3,2,1,0:T(8,128)S(1)} %bitcast.120), channel_id=1, source_target_pairs={{0,2},{1,3},{2,0},{3,1},{4,6},{5,7},{6,4},{7,5},{8,10},{9,11},{10,... | collective-permute-start | bytes 331784 | tf_op jit(solution)/shard_map/ppermute | solution.py:359
  115.9 69.3 %all-to-all-start.2 = ((bf16[8,32,5632]{2,1,0:T(8,128)(2,1)}), bf16[8,32,5632]{2,1,0:T(8,128)(2,1)S(1)}, u32[]{:S(2)}, u32[]{:S(2)}) async-start(bf16[8,32,5632]{2,1,0:T(8,128)(2,1)} %bitcast.113), calls=%async_computation.2 | async-start | bytes 5767168 | tf_op jit(solution)/shard_map/all_to_all | solution.py:429
  148.9 4.7 %collective-permute-start.12 = (bf16[48,1024]{1,0:T(8,128)(2,1)S(1)}, bf16[48,1024]{1,0:T(8,128)(2,1)S(1)}, u32[]{:S(2)}, u32[]{:S(2)}) collective-permute-start(bf16[48,1024]{1,0:T(8,128)(2,1)S(1)} %reshape.69), channel_id=1, source_target_pairs={{0,2},{1,3},{2,0},{3,1},{4,6},{5,7},{6,4},{7,5},{8,10},{9,11},{10,... | collective-permute-start | bytes 294920 | tf_op jit(solution)/shard_map/ppermute | solution.py:359
  155.3 7.0 %collective-permute-start.13 = (bf16[2,48,1024]{2,1,0:T(8,128)(2,1)}, bf16[2,48,1024]{2,1,0:T(8,128)(2,1)}, u32[]{:S(2)}, u32[]{:S(2)}) collective-permute-start(bf16[2,48,1024]{2,1,0:T(8,128)(2,1)} %pad_maximum_fusion.5), channel_id=1, source_target_pairs={{0,1},{1,0},{2,3},{3,2},{4,5},{5,4},{6,7},{7,6},{8,9},{9,8},{10,11... | collective-permute-start | bytes 589832 | tf_op jit(solution)/shard_map/ppermute | solution.py:359
  160.0 17.4 %collective-permute-start.9 = (bf16[18,48,96]{2,1,0:T(8,128)(2,1)}, bf16[18,48,96]{2,1,0:T(8,128)(2,1)S(1)}, u32[]{:S(2)}, u32[]{:S(2)}) collective-permute-start(bf16[18,48,96]{2,1,0:T(8,128)(2,1)} %get-tuple-element.32), channel_id=1, source_target_pairs={{0,1},{1,0},{2,3},{3,2},{4,5},{5,4},{6,7},{7,6},{8,9},{9,8},{10,11... | collective-permute-start | bytes 497672 | tf_op jit(solution)/shard_map/ppermute | solution.py:351
  160.5 16.9 %collective-permute-start.10 = (bf16[18,48,96]{2,1,0:T(8,128)(2,1)}, bf16[18,48,96]{2,1,0:T(8,128)(2,1)S(1)}, u32[]{:S(2)}, u32[]{:S(2)}) collective-permute-start(bf16[18,48,96]{2,1,0:T(8,128)(2,1)} %copy-done.23), channel_id=1, source_target_pairs={{0,2},{1,3},{2,0},{3,1},{4,6},{5,7},{6,4},{7,5},{8,10},{9,11},{10,... | collective-permute-start | bytes 497672 | tf_op jit(solution)/shard_map/ppermute | solution.py:351
  162.3 15.2 %collective-permute-start.11 = (bf16[18,48,96]{2,1,0:T(8,128)(2,1)}, bf16[18,48,96]{2,1,0:T(8,128)(2,1)}, u32[]{:S(2)}, u32[]{:S(2)}) collective-permute-start(bf16[18,48,96]{2,1,0:T(8,128)(2,1)} %copy-done.22), channel_id=1, source_target_pairs={{0,3},{1,2},{2,1},{3,0},{4,7},{5,6},{6,5},{7,4},{8,11},{9,10},{10,... | collective-permute-start | bytes 497672 | tf_op jit(solution)/shard_map/ppermute | solution.py:351
  174.7 10.5 %collective-permute-start.14 = (bf16[48,248]{1,0:T(8,128)(2,1)S(1)}, bf16[48,248]{1,0:T(8,128)(2,1)}, u32[]{:S(2)}, u32[]{:S(2)}) collective-permute-start(bf16[48,248]{1,0:T(8,128)(2,1)S(1)} %dynamic-slice_bitcast_fusion), channel_id=1, source_target_pairs={{0,16},{4,20},{8,24},{12,28},{16,0},{20,4},{24,8},{28,12},{1,17},{... | collective-permute-start | bytes 71432 | tf_op jit(solution)/shard_map/ppermute | solution.py:359
  185.2 38.3 %all-to-all-start.1 = ((bf16[8,16,5632]{2,1,0:T(8,128)(2,1)}), bf16[8,16,5632]{2,1,0:T(8,128)(2,1)}, u32[]{:S(2)}, u32[]{:S(2)}) async-start(bf16[8,16,5632]{2,1,0:T(8,128)(2,1)} %bitcast.112), calls=%async_computation.1 | async-start | bytes 2883584 | tf_op jit(solution)/shard_map/all_to_all | solution.py:429
  190.8 22.7 %collective-permute-start.18 = (bf16[2,48,248]{2,1,0:T(8,128)(2,1)S(1)}, bf16[2,48,248]{2,1,0:T(8,128)(2,1)S(1)}, u32[]{:S(2)}, u32[]{:S(2)}) collective-permute-start(bf16[2,48,248]{2,1,0:T(8,128)(2,1)S(1)} %pad_maximum_fusion.12), channel_id=1, source_target_pairs={{0,8},{4,12},{8,0},{12,4},{16,24},{20,28},{24,16},{28,20},{1,9},{5... | collective-permute-start | bytes 142856 | tf_op jit(solution)/shard_map/ppermute | solution.py:359
  199.9 16.1 %collective-permute-start.15 = (bf16[18,32,96]{2,1,0:T(8,128)(2,1)S(1)}, bf16[18,32,96]{2,1,0:T(8,128)(2,1)S(1)}, u32[]{:S(2)}, u32[]{:S(2)}) collective-permute-start(bf16[18,32,96]{2,1,0:T(8,128)(2,1)S(1)} %get-tuple-element.37), channel_id=1, source_target_pairs={{0,1},{1,0},{2,3},{3,2},{4,5},{5,4},{6,7},{7,6},{8,9},{9,8},{10,11... | collective-permute-start | bytes 331784 | tf_op jit(solution)/shard_map/ppermute | solution.py:351
  200.0 16.0 %collective-permute-start.16 = (bf16[18,32,96]{2,1,0:T(8,128)(2,1)S(1)}, bf16[18,32,96]{2,1,0:T(8,128)(2,1)S(1)}, u32[]{:S(2)}, u32[]{:S(2)}) collective-permute-start(bf16[18,32,96]{2,1,0:T(8,128)(2,1)S(1)} %get-tuple-element.38), channel_id=1, source_target_pairs={{0,2},{1,3},{2,0},{3,1},{4,6},{5,7},{6,4},{7,5},{8,10},{9,11},{10,... | collective-permute-start | bytes 331784 | tf_op jit(solution)/shard_map/ppermute | solution.py:351
  201.9 14.1 %collective-permute-start.17 = (bf16[18,32,96]{2,1,0:T(8,128)(2,1)S(1)}, bf16[18,32,96]{2,1,0:T(8,128)(2,1)S(1)}, u32[]{:S(2)}, u32[]{:S(2)}) collective-permute-start(bf16[18,32,96]{2,1,0:T(8,128)(2,1)S(1)} %get-tuple-element.39), channel_id=1, source_target_pairs={{0,3},{1,2},{2,1},{3,0},{4,7},{5,6},{6,5},{7,4},{8,11},{9,10},{10,... | collective-permute-start | bytes 331784 | tf_op jit(solution)/shard_map/ppermute | solution.py:351
  213.6 5.0 %collective-permute-start.19 = (bf16[2,2,48,248]{3,2,0,1:T(8,128)(2,1)S(1)}, bf16[2,2,48,248]{3,2,0,1:T(8,128)(2,1)S(1)}, u32[]{:S(2)}, u32[]{:S(2)}) collective-permute-start(bf16[2,2,48,248]{3,2,0,1:T(8,128)(2,1)S(1)} %pad_maximum_fusion.8), channel_id=1, source_target_pairs={{0,4},{4,0},{8,12},{12,8},{16,20},{20,16},{24,28},{28,24},{1,5},{5... | collective-permute-start | bytes 285704 | tf_op jit(solution)/shard_map/ppermute | solution.py:359
  228.8 4.9 %collective-permute-start.21 = (bf16[18,16,96]{2,1,0:T(8,128)(2,1)}, bf16[18,16,96]{2,1,0:T(8,128)(2,1)S(1)}, u32[]{:S(2)}, u32[]{:S(2)}) collective-permute-start(bf16[18,16,96]{2,1,0:T(8,128)(2,1)} %get-tuple-element.42), channel_id=1, source_target_pairs={{0,2},{1,3},{2,0},{3,1},{4,6},{5,7},{6,4},{7,5},{8,10},{9,11},{10,... | collective-permute-start | bytes 165896 | tf_op jit(solution)/shard_map/ppermute | solution.py:351
  230.7 4.5 %collective-permute-start.22 = (bf16[18,16,96]{2,1,0:T(8,128)(2,1)}, bf16[18,16,96]{2,1,0:T(8,128)(2,1)S(1)}, u32[]{:S(2)}, u32[]{:S(2)}) collective-permute-start(bf16[18,16,96]{2,1,0:T(8,128)(2,1)} %get-tuple-element.43), channel_id=1, source_target_pairs={{0,3},{1,2},{2,1},{3,0},{4,7},{5,6},{6,5},{7,4},{8,11},{9,10},{10,... | collective-permute-start | bytes 165896 | tf_op jit(solution)/shard_map/ppermute | solution.py:351
  (44 other events, 294.3 us)

commit v6 on v5

--- a/solution.py
+++ b/solution.py
@@ -12,7 +12,7 @@
 LAGMAX = 8
 ROW_DEG = 3
 VMEM = 40 * 2**20
-FULL_VMEM = 63 * 2**20
+FULL_VMEM = 64 * 2**20 - 2**17
 
 
 def dft_columns(orders, longitudes):
@@ -30,7 +30,8 @@
     scale = math.sqrt(2.0 / latitudes)
     cosines = np.cos(degree * odd_lat % period * unit) * scale
     sines = np.sin((degree + 1) * odd_lat % period * unit) * scale
-    return np.concatenate([cosines, sines], axis=1).astype(jnp.bfloat16)
+    table = np.concatenate([cosines, sines], axis=1).astype(jnp.bfloat16)
+    return np.stack([table, np.zeros_like(table)])
 
 
 ANY = pl.BlockSpec(memory_space=pl.ANY)
@@ -164,7 +165,11 @@
     by_hop, blocks, refs = refs[:hops], list(refs[hops : hops + groups]), refs[hops + groups + n_after :]
     lat_ref, stage_ref, sems = refs[-3:]
     refs = refs[:-3]
-    copies = [pltpu.make_async_copy(lat_hbm, lat_ref, sems.at[hops])]
+    copies = []
+    if len(lat_hbm.shape) == 3:
+        copies.append(pltpu.make_async_copy(lat_hbm.at[0], lat_ref, sems.at[hops]))
+    else:
+        lat_ref = lat_hbm
     for hop, ref in enumerate(by_hop):
         source = me_ref[1] ^ hop
         copies.append(pltpu.make_async_copy(ref, stage_ref.at[source], sems.at[hop]))
@@ -172,7 +177,7 @@
         copy.start()
     if hops:
         blocks.insert(0, stage_ref)
-        for copy in copies[1:]:
+        for copy in copies[-hops:]:
             copy.wait()
     sends, pick_refs = refs[:narrow_count], refs[narrow_count:-3]
     line_ref, series_ref, block_ref = refs[-3:]
@@ -190,7 +195,7 @@
                 else:
                     line_ref[day, :half, lats] = block[source, :half, cells]
                     line_ref[day, padded : padded + half, lats] = block[source, half:, cells]
-        if start == 0:
+        if start == 0 and lat_ref is not lat_hbm:
             copies[0].wait()
         for parity in range(2):
             lines = line_ref[start:stop, parity * padded : (parity + 1) * padded, :]
@@ -241,7 +246,7 @@
     by_hop = received[0] if isinstance(received[0], list) else []
     received = received[1:] if by_hop else received
     sources, slots, _ = received[0].shape
-    latitudes, degrees = lat_table.shape[0], lat_table.shape[1] // 2
+    latitudes, degrees = lat_table.shape[-2], lat_table.shape[-1] // 2
     lat_local = latitudes // sources
     days_local = sum(block.shape[-1] for block in by_hop[:1] + received) // lat_local
     deg_local = degrees // narrow_count
@@ -252,7 +257,7 @@
         functools.partial(
             digest_kernel, (len(received), len(by_hop), narrow_count, lat_local, len(after))
         ),
-        in_specs=[IN_SMEM, IN_SMEM, IN_VMEM, IN_HBM]
+        in_specs=[IN_SMEM, IN_SMEM, IN_VMEM, IN_HBM if lat_table.ndim == 3 else IN_VMEM]
         + [ANY] * len(by_hop)
         + [IN_VMEM] * len(received)
         + [ANY] * len(after),
@@ -263,11 +268,11 @@
             pltpu.VMEM((days_local, padded, latitudes), jnp.bfloat16),
             pltpu.VMEM((days_local, slots, degrees), jnp.bfloat16),
             pltpu.VMEM((narrow_count,) + message, jnp.bfloat16),
-            pltpu.VMEM(lat_table.shape, jnp.bfloat16),
+            pltpu.VMEM(lat_table.shape[-2:] if lat_table.ndim == 3 else (16, 128), jnp.bfloat16),
             pltpu.VMEM((sources,) + by_hop[0].shape if by_hop else (8, 128), jnp.bfloat16),
             pltpu.SemaphoreType.DMA((len(by_hop) + 1,)),
         ],
-        compiler_params=pltpu.CompilerParams(vmem_limit_bytes=VMEM if slots > 32 else VMEM // 2 if slots > 16 else FULL_VMEM - 2**20),
+        compiler_params=pltpu.CompilerParams(vmem_limit_bytes=FULL_VMEM if slots > 32 else VMEM // 2),
         cost_estimate=pl.CostEstimate(
             flops=4 * slots * days_local * latitudes * degrees,
             bytes_accessed=2 * slots * days_local * (latitudes + degrees),
@@ -284,6 +289,24 @@
         out_shape=jax.ShapeDtypeStruct(array.shape, array.dtype),
         input_output_aliases={0: 0},
     )(array, *after)
+
+
+def hold_kernel(table_ref, *refs):
+    out_ref, sem = refs[-2:]
+    copy = pltpu.make_async_copy(table_ref.at[0], out_ref, sem)
+    copy.start()
+    copy.wait()
+
+
+def hold(table, after):
+    return pl.pallas_call(
+        hold_kernel,
+        in_specs=[ANY] * (1 + len(after)),
+        out_specs=IN_VMEM,
+        out_shape=jax.ShapeDtypeStruct(table.shape[1:], table.dtype),
+        scratch_shapes=[pltpu.SemaphoreType.DMA(())],
+        compiler_params=pltpu.CompilerParams(vmem_limit_bytes=VMEM // 2),
+    )(table, *after)
 
 
 def combine_kernel(count, final, lag_ref, me_ref, weight_ref, *refs):
@@ -428,13 +451,13 @@
         spectra = spectra.reshape(wide_count, -1, spectra.shape[1])
         return lax.all_to_all(spectra, "wide", split_axis=0, concat_axis=0, tiled=True)
 
-    def finish(job, after, others=(), final=None):
+    def finish(job, after, table, others=(), final=None):
         part, first, last, _ = sent[job[0]]
         out = digest(
             lag_days,
             me,
             [received[index] for index in job],
-            lat_table,
+            table,
             rows_of(all_weights, part, first, last),
             narrow_count,
             part == 0,
@@ -453,7 +476,7 @@
             rows = slice(parity * (last - first), (parity + 1) * (last - first))
             if picks:
                 picked[parity, first] = picks[0][:, rows]
-        return total
+        return total, sends[0]
 
     def panel_rows():
         series = jnp.stack(
@@ -503,15 +526,18 @@
     else:
         for index in range(len(sent)):
             received.append(exchange(product(index, [])))
-    done = [finish(jobs[0], [])]
+    done = [finish(jobs[0], [], lat_table)[0]]
+    table = lat_table
     rows, column, far = panel_rows()
     if len(sent) > 2:
         received.append(exchange(tie(spectra[len(sent) - 1], done + [far])))
     panel = panel_of(rows, column, far)
     for job in jobs[1:-1]:
-        done.append(finish(job, []))
+        total, message = finish(job, [], lat_table)
+        table = hold(lat_table, [message])
+        done.append(total)
     places = [sent[job[0]][:3] for job in jobs]
-    variances = finish(jobs[-1], done + [panel], done, (kept_days, places))
+    variances, _ = finish(jobs[-1], done + [panel], table, done, (kept_days, places))
     noise_variance = jnp.transpose(variances, (2, 0, 1))
     return (noise_variance, panel)
 

time: 238 us -> 236 us (level)
  waiting for transfers between devices: 75.1 us -> 100 us
  local copies, waits for them, and re-layouts: 32.5 us -> 12.1 us
  other arithmetic: 10 us -> 2.99 us
    ppermute x7, waiting for transfers between devices: 26.1 us -> 45.8 us  [gather_swap(): return lax.ppermute(held, axis, [(i, i ^ reach) for i in range(count)])]
    unnamed x83 -> x51, local copies, waits for them, and re-layouts: 8.29 us -> 3.29 us
    another operation x14, other arithmetic: 4.5 us -> 0.38 us  [gather(): held, depth = (jnp.stack(pair, axis=depth), depth + 1)]
    ppermute x16, waiting for transfers between devices: 5.17 us -> 9.27 us  [swap(): lax.ppermute(sends[hop], axis, [(i, peer(i, hop, count)[0]) for i in rang...]
    slice x4, local copies, waits for them, and re-layouts: 2.65 us -> 0.2 us  [panel_rows(): residual = residual - weights[position] * shifted.astype(jnp.float32)]
    another operation x1, local copies, waits for them, and re-layouts: 2.92 us -> 0.49 us  [panel_rows(): series.reshape(narrow_count, slot_local, narrow_count, ROW_DEG + 1, days_...]
  transfers between devices with their start and end apart: 26 -> 26, of which waited for: 12 -> 14; matrix products, arithmetic and copies ran while one was open for 15% -> 6% of each run, Pallas kernels for 23% -> 24%
where the time goes in v6:
time: 236 us; the launch traced here: 235 us
  waiting for transfers between devices  100 us (42%)
  Pallas kernels  67.8 us (29%)
  starting transfers between devices  47.1 us (20%)
  local copies, waits for them, and re-layouts  12.1 us (5%)
  between operations  5.11 us (2%)
  other arithmetic  2.99 us (1%)
    ppermute x7, waiting for transfers between devices, gather_swap(): return lax.ppermute(held, axis, [(i, i ^ reach) for i in range(count)])  45.8 us
    all_to_all x3, waiting for transfers between devices, exchange(): lax.all_to_all(spectra, 'wide', split_axis=0, concat_axis=0, tiled=True)  44.8 us
    pallas_call x3, Pallas kernels, spectra_of(): pl.pallas_call(functools.partial(spectra_kernel, owned), grid=(last - fir...  35 us
    pallas_call x3, Pallas kernels, digest(): pl.pallas_call(functools.partial(digest_kernel, (len(received), len(by_ho...  22.9 us
    ppermute x16, starting transfers between devices, swap(): lax.ppermute(sends[hop], axis, [(i, peer(i, hop, count)[0]) for i in rang...  19.6 us
    all_to_all x3, starting transfers between devices, exchange(): lax.all_to_all(spectra, 'wide', split_axis=0, concat_axis=0, tiled=True)  17.7 us
    ppermute x7, starting transfers between devices, gather_swap(): return lax.ppermute(held, axis, [(i, i ^ reach) for i in range(count)])  9.81 us
    ppermute x16, waiting for transfers between devices, swap(): lax.ppermute(sends[hop], axis, [(i, peer(i, hop, count)[0]) for i in rang...  9.27 us
  transfers between devices with their start and end apart: 26, of which 14 were waited for; matrix products, arithmetic and copies ran while one was open for 6% of the time, Pallas kernels for 24%

profile of v6, /device:TPU:0, one launch (start us, length us, event | category | flops | bytes accessed | tf_op | source)
XLA Modules:
  0.0 235.4 jit_solution(7161615221977319779)
XLA Ops:
  0.6 6.7 %shard_map.77 = (bf16[48,1408]{1,0:T(8,128)(2,1)}, bf16[48,1408]{1,0:T(8,128)(2,1)}, bf16[48,1408]{1,0:T(8,128)(2,1)}, bf16[48,1408]{1,0:T(8,128)(2,1)}, bf16[48...) custom-call(s32[384]{0:T(512)} %order_ref.7, ...), custom_call_target="tpu_custom_call" | custom-call | flops 1557135360 | bytes 6242304 | tf_op jit(solution)/shard_map/pallas_call | solution.py:108
  7.4 3.0 %collective-permute-start.2 = (bf16[48,1408]{1,0:T(8,128)(2,1)}, bf16[48,1408]{1,0:T(8,128)(2,1)}, u32[]{:S(2)}, u32[]{:S(2)}) collective-permute-start(bf16[48,1408]{1,0:T(8,128)(2,1)} %get-tuple-element.24), channel_id=1, source_target_pairs={{0,4},{4,0},{8,12},{12,8},{16,20},{20,16},{24,28},{28,24},{1,5},{5... | collective-permute-start | bytes 405512 | tf_op jit(solution)/shard_map/ppermute | solution.py:374
  12.0 3.0 %collective-permute-start.5 = (bf16[48,1408]{1,0:T(8,128)(2,1)}, bf16[48,1408]{1,0:T(8,128)(2,1)}, u32[]{:S(2)}, u32[]{:S(2)}) collective-permute-start(bf16[48,1408]{1,0:T(8,128)(2,1)} %get-tuple-element.27), channel_id=1, source_target_pairs={{0,16},{4,20},{8,24},{12,28},{16,0},{20,4},{24,8},{28,12},{1,17},{... | collective-permute-start | bytes 405512 | tf_op jit(solution)/shard_map/ppermute | solution.py:374
  16.2 3.6 %collective-permute-start.7 = (bf16[48,1408]{1,0:T(8,128)(2,1)}, bf16[48,1408]{1,0:T(8,128)(2,1)}, u32[]{:S(2)}, u32[]{:S(2)}) collective-permute-start(bf16[48,1408]{1,0:T(8,128)(2,1)} %get-tuple-element.29), channel_id=1, source_target_pairs={{0,24},{4,28},{8,16},{12,20},{16,8},{20,12},{24,0},{28,4},{1,25},{... | collective-permute-start | bytes 405512 | tf_op jit(solution)/shard_map/ppermute | solution.py:374
  19.8 1.9 collective-permute-done.3.refs_2_
  22.5 12.5 %shard_map.78.refs_0_ = bf16[384,4224]{1,0:T(8,128)(2,1)} custom-call(s32[384]{0:T(512)} %order_ref.7, bf16[2,1440,384]{2,1,0:T(8,128)(2,1)} %constant.42.clone.part_hbm.part_ref, bf16[5632,1440]{1,0:T(8,128)(2,1)} %bitcast.108, bf16[48,1408]{1,0:T(8,128)(2,1)} %get-tuple-element.23.refs_0_), custom_call_target="tpu_custom_call" | custom-call | flops 4671406080 | bytes 16515072 | tf_op jit(solution)/shard_map/pallas_call | solution.py:140
  35.2 8.2 %all-to-all-start.1 = ((bf16[8,48,4224]{2,1,0:T(8,128)(2,1)}), bf16[8,48,4224]{2,1,0:T(8,128)(2,1)}, u32[]{:S(2)}, u32[]{:S(2)}) async-start(bf16[8,48,4224]{2,1,0:T(8,128)(2,1)} %bitcast.111), calls=%async_computation.1 | async-start | bytes 6488064 | tf_op jit(solution)/shard_map/all_to_all | solution.py:452
  45.0 3.6 %collective-permute-done = f32[2,2,3,24,96]{4,3,2,1,0:T(8,128)S(1)} collective-permute-done((f32[2,2,3,24,96]{4,3,2,1,0:T(8,128)S(1)}, f32[2,2,3,24,96]{4,3,2,1,0:T(8,128)S(1)}, u32[]{:S(2)}, u32[]{:S(2)}) %collective-permute-start) | collective-permute-done | bytes 110624 | tf_op jit(solution)/shard_map/ppermute | solution.py:382
  52.7 10.9 %shard_map.80.refs_0_ = bf16[128,5632]{1,0:T(8,128)(2,1)} custom-call(s32[384]{0:T(512)} %order_ref.7, bf16[2,1440,384]{2,1,0:T(8,128)(2,1)} %constant.42.clone.part_hbm.part_ref, bf16[5632,1440]{1,0:T(8,128)(2,1)} %bitcast.109, bf16[384,4224]{1,0:T(8,128)(2,1)} %shard_map.79.refs_0_, f32[2,2,3,24,384]{4,3,2,1,0:T(8,128)} %reshape.65.refs_1_), custom_call_target="tpu_custom_call" | custom-call | flops 2076180480 | bytes 18030592 | tf_op jit(solution)/shard_map/pallas_call | solution.py:140
  63.7 11.6 %shard_map.81 = bf16[256,5632]{1,0:T(8,128)(2,1)} custom-call(s32[384]{0:T(512)} %order_ref.7, bf16[2,1440,384]{2,1,0:T(8,128)(2,1)} %constant.42.clone.part_hbm.part_ref, bf16[5632,1440]{1,0:T(8,128)(2,1)} %bitcast.110, bf16[128,5632]{1,0:T(8,128)(2,1)} %shard_map.80.refs_0_, f32[2,2,3,24,384]{4,3,2,1,0:T(8,128)} %reshape.65.refs_1_), custom_call_target="tpu_custom_call" | custom-call | flops 4152360960 | bytes 19841024 | tf_op jit(solution)/shard_map/pallas_call | solution.py:140
  75.2 40.7 %all-to-all-done.1.refs_8_ = bf16[8,48,4224]{2,1,0:T(8,128)(2,1)} async-done(((bf16[8,48,4224]{2,1,0:T(8,128)(2,1)}), bf16[8,48,4224]{2,1,0:T(8,128)(2,1)}, u32[]{:S(2)}, u32[]{:S(2)}) %all-to-all-start.1) | async-done | bytes 3244064 | tf_op jit(solution)/shard_map/all_to_all | solution.py:452
  115.9 4.8 %all-to-all-start = ((bf16[8,32,5632]{2,1,0:T(8,128)(2,1)}), bf16[8,32,5632]{2,1,0:T(8,128)(2,1)}, u32[]{:S(2)}, u32[]{:S(2)}) async-start(bf16[8,32,5632]{2,1,0:T(8,128)(2,1)} %bitcast.113), calls=%async_computation | async-start | bytes 5767168 | tf_op jit(solution)/shard_map/all_to_all | solution.py:452
  129.1 11.7 %shard_map.84 = (bf16[18,48,96]{2,1,0:T(8,128)(2,1)}, bf16[18,48,96]{2,1,0:T(8,128)(2,1)}, bf16[18,48,96]{2,1,0:T(8,128)(2,1)}, bf16[18,48,96]{2,1,0:T(8,128)(2,1)}, bf16[64,48,16]{2,1,0:T(8,128)(2,1)}) custom-call(s32[3]{0:T(128)} %lag_ref.11, s32[2]{0:T(128)} %pad_add_fusion.me_ref, f32[3,48,384]{2,1,0:T(8,128)} %pad_maximum_fusion.3.weight_ref, ...), custom_call_target="tpu_custom_call" | custom-call | flops 3321888768 | bytes 6684672 | tf_op jit(solution)/shard_map/pallas_call | solution.py:256
  144.7 2.8 %collective-permute-done.12 = bf16[48,1024]{1,0:T(8,128)(2,1)S(1)} collective-permute-done((bf16[48,1024]{1,0:T(8,128)(2,1)S(1)}, bf16[48,1024]{1,0:T(8,128)(2,1)S(1)}, u32[]{:S(2)}, u32[]{:S(2)}) %collective-permute-start.12) | collective-permute-done | bytes 98336 | tf_op jit(solution)/shard_map/ppermute | solution.py:382
  153.2 2.7 %collective-permute-start.14 = (bf16[48,248]{1,0:T(8,128)(2,1)S(1)}, bf16[48,248]{1,0:T(8,128)(2,1)S(1)}, u32[]{:S(2)}, u32[]{:S(2)}) collective-permute-start(bf16[48,248]{1,0:T(8,128)(2,1)S(1)} %dynamic-slice_bitcast_fusion), channel_id=1, source_target_pairs={{0,16},{4,20},{8,24},{12,28},{16,0},{20,4},{24,8},{28,12},{1,17},{... | collective-permute-start | bytes 71432 | tf_op jit(solution)/shard_map/ppermute | solution.py:382
  157.0 3.2 %collective-permute-done.11.refs_3_ = bf16[18,48,96]{2,1,0:T(8,128)(2,1)S(1)} collective-permute-done((bf16[18,48,96]{2,1,0:T(8,128)(2,1)S(1)}, bf16[18,48,96]{2,1,0:T(8,128)(2,1)S(1)}, u32[]{:S(2)}, u32[]{:S(2)}) %collective-permute-start.11) | collective-permute-done | bytes 165920 | tf_op jit(solution)/shard_map/ppermute | solution.py:374
  161.7 23.4 %collective-permute-done.14.refs_2_ = bf16[48,248]{1,0:T(8,128)(2,1)S(1)} collective-permute-done((bf16[48,248]{1,0:T(8,128)(2,1)S(1)}, bf16[48,248]{1,0:T(8,128)(2,1)S(1)}, u32[]{:S(2)}, u32[]{:S(2)}) %collective-permute-start.14) | collective-permute-done | bytes 23840 | tf_op jit(solution)/shard_map/ppermute | solution.py:382
  185.7 4.8 %all-to-all-start.2 = ((bf16[8,16,5632]{2,1,0:T(8,128)(2,1)}), bf16[8,16,5632]{2,1,0:T(8,128)(2,1)}, u32[]{:S(2)}, u32[]{:S(2)}) async-start(bf16[8,16,5632]{2,1,0:T(8,128)(2,1)} %bitcast.112), calls=%async_computation.2 | async-start | bytes 2883584 | tf_op jit(solution)/shard_map/all_to_all | solution.py:452
  192.4 7.5 %shard_map.82 = (bf16[18,32,96]{2,1,0:T(8,128)(2,1)S(1)}, bf16[18,32,96]{2,1,0:T(8,128)(2,1)S(1)}, bf16[18,32,96]{2,1,0:T(8,128)(2,1)S(1)}, bf16[18,32,96]{2,1,0:T(8,128)(2,1)S(1)}) custom-call(s32[3]{0:T(128)S(1)} %copy-done.5, s32[2]{0:T(128)S(1)} %copy-done.6, f32[3,32,384]{2,1,0:T(8,128)S(1)} %pad_maximum_fusion.7.weight_ref, ...), custom_call_target="tpu_custom_call" | custom-call | flops 2214592512 | bytes 4456448 | tf_op jit(solution)/shard_map/pallas_call | solution.py:256
  201.9 12.3 %collective-permute-done.18 = bf16[2,48,248]{2,1,0:T(8,128)(2,1)S(1)} collective-permute-done((bf16[2,48,248]{2,1,0:T(8,128)(2,1)S(1)}, bf16[2,48,248]{2,1,0:T(8,128)(2,1)S(1)}, u32[]{:S(2)}, u32[]{:S(2)}) %collective-permute-start.18) | collective-permute-done | bytes 47648 | tf_op jit(solution)/shard_map/ppermute | solution.py:382
  217.0 2.2 collective-permute-done.19
  220.0 4.1 %all-to-all-done.2.refs_0_ = bf16[8,16,5632]{2,1,0:T(8,128)(2,1)} async-done(((bf16[8,16,5632]{2,1,0:T(8,128)(2,1)}), bf16[8,16,5632]{2,1,0:T(8,128)(2,1)}, u32[]{:S(2)}, u32[]{:S(2)}) %all-to-all-start.2) | async-done | bytes 1441824 | tf_op jit(solution)/shard_map/all_to_all | solution.py:452
  224.1 3.7 %shard_map.88 = (bf16[18,16,96]{2,1,0:T(8,128)(2,1)S(1)}, bf16[18,16,96]{2,1,0:T(8,128)(2,1)S(1)}, bf16[18,16,96]{2,1,0:T(8,128)(2,1)S(1)}, bf16[18,16,96]{2,1,0:T(8,128)(2,1)S(1)}) custom-call(s32[3]{0:T(128)S(1)} %copy-done.5, s32[2]{0:T(128)S(1)} %copy-done.6, f32[3,16,384]{2,1,0:T(8,128)S(1)} %pad_maximum_fusion.9.weight_ref, ...), custom_call_target="tpu_custom_call" | custom-call | flops 1107296256 | bytes 2228224 | tf_op jit(solution)/shard_map/pallas_call | solution.py:256
  227.9 1.9 collective-permute-start.21
  (149 shorter events, 39.5 us)
Async XLA Ops:
  7.4 8.9 %collective-permute-start.2 = (bf16[48,1408]{1,0:T(8,128)(2,1)}, bf16[48,1408]{1,0:T(8,128)(2,1)}, u32[]{:S(2)}, u32[]{:S(2)}) collective-permute-start(bf16[48,1408]{1,0:T(8,128)(2,1)} %get-tuple-element.24), channel_id=1, source_target_pairs={{0,4},{4,0},{8,12},{12,8},{16,20},{20,16},{24,28},{28,24},{1,5},{5... | collective-permute-start | bytes 405512 | tf_op jit(solution)/shard_map/ppermute | solution.py:374
  10.4 11.4 %collective-permute-start.3 = (bf16[48,1408]{1,0:T(8,128)(2,1)}, bf16[48,1408]{1,0:T(8,128)(2,1)}, u32[]{:S(2)}, u32[]{:S(2)}) collective-permute-start(bf16[48,1408]{1,0:T(8,128)(2,1)} %get-tuple-element.25), channel_id=1, source_target_pairs={{0,8},{4,12},{8,0},{12,4},{16,24},{20,28},{24,16},{28,20},{1,9},{5... | collective-permute-start | bytes 405512 | tf_op jit(solution)/shard_map/ppermute | solution.py:374
  12.0 23.1 %collective-permute-start.4 = (bf16[48,1408]{1,0:T(8,128)(2,1)}, bf16[48,1408]{1,0:T(8,128)(2,1)}, u32[]{:S(2)}, u32[]{:S(2)}) collective-permute-start(bf16[48,1408]{1,0:T(8,128)(2,1)} %get-tuple-element.26), channel_id=1, source_target_pairs={{0,12},{4,8},{8,4},{12,0},{16,28},{20,24},{24,20},{28,16},{1,13},{... | collective-permute-start | bytes 405512 | tf_op jit(solution)/shard_map/ppermute | solution.py:374
  12.0 23.1 %collective-permute-start.5 = (bf16[48,1408]{1,0:T(8,128)(2,1)}, bf16[48,1408]{1,0:T(8,128)(2,1)}, u32[]{:S(2)}, u32[]{:S(2)}) collective-permute-start(bf16[48,1408]{1,0:T(8,128)(2,1)} %get-tuple-element.27), channel_id=1, source_target_pairs={{0,16},{4,20},{8,24},{12,28},{16,0},{20,4},{24,8},{28,12},{1,17},{... | collective-permute-start | bytes 405512 | tf_op jit(solution)/shard_map/ppermute | solution.py:374
  14.9 20.2 %collective-permute-start.6 = (bf16[48,1408]{1,0:T(8,128)(2,1)}, bf16[48,1408]{1,0:T(8,128)(2,1)}, u32[]{:S(2)}, u32[]{:S(2)}) collective-permute-start(bf16[48,1408]{1,0:T(8,128)(2,1)} %get-tuple-element.28), channel_id=1, source_target_pairs={{0,20},{4,16},{8,28},{12,24},{16,4},{20,0},{24,12},{28,8},{1,21},{... | collective-permute-start | bytes 405512 | tf_op jit(solution)/shard_map/ppermute | solution.py:374
  16.2 19.0 %collective-permute-start.7 = (bf16[48,1408]{1,0:T(8,128)(2,1)}, bf16[48,1408]{1,0:T(8,128)(2,1)}, u32[]{:S(2)}, u32[]{:S(2)}) collective-permute-start(bf16[48,1408]{1,0:T(8,128)(2,1)} %get-tuple-element.29), channel_id=1, source_target_pairs={{0,24},{4,28},{8,16},{12,20},{16,8},{20,12},{24,0},{28,4},{1,25},{... | collective-permute-start | bytes 405512 | tf_op jit(solution)/shard_map/ppermute | solution.py:374
  21.8 13.4 %collective-permute-start.8 = (bf16[48,1408]{1,0:T(8,128)(2,1)}, bf16[48,1408]{1,0:T(8,128)(2,1)}, u32[]{:S(2)}, u32[]{:S(2)}) collective-permute-start(bf16[48,1408]{1,0:T(8,128)(2,1)} %get-tuple-element.30), channel_id=1, source_target_pairs={{0,28},{4,24},{8,20},{12,16},{16,12},{20,8},{24,4},{28,0},{1,29},{... | collective-permute-start | bytes 405512 | tf_op jit(solution)/shard_map/ppermute | solution.py:374
  35.2 80.7 %all-to-all-start.1 = ((bf16[8,48,4224]{2,1,0:T(8,128)(2,1)}), bf16[8,48,4224]{2,1,0:T(8,128)(2,1)}, u32[]{:S(2)}, u32[]{:S(2)}) async-start(bf16[8,48,4224]{2,1,0:T(8,128)(2,1)} %bitcast.111), calls=%async_computation.1 | async-start | bytes 6488064 | tf_op jit(solution)/shard_map/all_to_all | solution.py:452
  43.4 5.2 %collective-permute-start = (f32[2,2,3,24,96]{4,3,2,1,0:T(8,128)S(1)}, f32[2,2,3,24,96]{4,3,2,1,0:T(8,128)S(1)}, u32[]{:S(2)}, u32[]{:S(2)}) collective-permute-start(f32[2,2,3,24,96]{4,3,2,1,0:T(8,128)S(1)} %bitcast.120), channel_id=1, source_target_pairs={{0,2},{1,3},{2,0},{3,1},{4,6},{5,7},{6,4},{7,5},{8,10},{9,11},{10,... | collective-permute-start | bytes 331784 | tf_op jit(solution)/shard_map/ppermute | solution.py:382
  115.9 69.7 %all-to-all-start = ((bf16[8,32,5632]{2,1,0:T(8,128)(2,1)}), bf16[8,32,5632]{2,1,0:T(8,128)(2,1)}, u32[]{:S(2)}, u32[]{:S(2)}) async-start(bf16[8,32,5632]{2,1,0:T(8,128)(2,1)} %bitcast.113), calls=%async_computation | async-start | bytes 5767168 | tf_op jit(solution)/shard_map/all_to_all | solution.py:452
  142.8 4.7 %collective-permute-start.12 = (bf16[48,1024]{1,0:T(8,128)(2,1)S(1)}, bf16[48,1024]{1,0:T(8,128)(2,1)S(1)}, u32[]{:S(2)}, u32[]{:S(2)}) collective-permute-start(bf16[48,1024]{1,0:T(8,128)(2,1)S(1)} %reshape.70), channel_id=1, source_target_pairs={{0,2},{1,3},{2,0},{3,1},{4,6},{5,7},{6,4},{7,5},{8,10},{9,11},{10,... | collective-permute-start | bytes 294920 | tf_op jit(solution)/shard_map/ppermute | solution.py:382
  148.1 7.7 %collective-permute-start.9 = (bf16[18,48,96]{2,1,0:T(8,128)(2,1)S(1)}, bf16[18,48,96]{2,1,0:T(8,128)(2,1)S(1)}, u32[]{:S(2)}, u32[]{:S(2)}) collective-permute-start(bf16[18,48,96]{2,1,0:T(8,128)(2,1)S(1)} %copy-done.24), channel_id=1, source_target_pairs={{0,1},{1,0},{2,3},{3,2},{4,5},{5,4},{6,7},{7,6},{8,9},{9,8},{10,11... | collective-permute-start | bytes 497672 | tf_op jit(solution)/shard_map/ppermute | solution.py:374
  148.7 8.3 %collective-permute-start.10 = (bf16[18,48,96]{2,1,0:T(8,128)(2,1)S(1)}, bf16[18,48,96]{2,1,0:T(8,128)(2,1)S(1)}, u32[]{:S(2)}, u32[]{:S(2)}) collective-permute-start(bf16[18,48,96]{2,1,0:T(8,128)(2,1)S(1)} %copy-done.23), channel_id=1, source_target_pairs={{0,2},{1,3},{2,0},{3,1},{4,6},{5,7},{6,4},{7,5},{8,10},{9,11},{10,... | collective-permute-start | bytes 497672 | tf_op jit(solution)/shard_map/ppermute | solution.py:374
  150.5 9.7 %collective-permute-start.11 = (bf16[18,48,96]{2,1,0:T(8,128)(2,1)S(1)}, bf16[18,48,96]{2,1,0:T(8,128)(2,1)S(1)}, u32[]{:S(2)}, u32[]{:S(2)}) collective-permute-start(bf16[18,48,96]{2,1,0:T(8,128)(2,1)S(1)} %copy-done.22), channel_id=1, source_target_pairs={{0,3},{1,2},{2,1},{3,0},{4,7},{5,6},{6,5},{7,4},{8,11},{9,10},{10,... | collective-permute-start | bytes 497672 | tf_op jit(solution)/shard_map/ppermute | solution.py:374
  153.2 31.9 %collective-permute-start.14 = (bf16[48,248]{1,0:T(8,128)(2,1)S(1)}, bf16[48,248]{1,0:T(8,128)(2,1)S(1)}, u32[]{:S(2)}, u32[]{:S(2)}) collective-permute-start(bf16[48,248]{1,0:T(8,128)(2,1)S(1)} %dynamic-slice_bitcast_fusion), channel_id=1, source_target_pairs={{0,16},{4,20},{8,24},{12,28},{16,0},{20,4},{24,8},{28,12},{1,17},{... | collective-permute-start | bytes 71432 | tf_op jit(solution)/shard_map/ppermute | solution.py:382
  185.7 38.5 %all-to-all-start.2 = ((bf16[8,16,5632]{2,1,0:T(8,128)(2,1)}), bf16[8,16,5632]{2,1,0:T(8,128)(2,1)}, u32[]{:S(2)}, u32[]{:S(2)}) async-start(bf16[8,16,5632]{2,1,0:T(8,128)(2,1)} %bitcast.112), calls=%async_computation.2 | async-start | bytes 2883584 | tf_op jit(solution)/shard_map/all_to_all | solution.py:452
  190.6 23.5 %collective-permute-start.18 = (bf16[2,48,248]{2,1,0:T(8,128)(2,1)S(1)}, bf16[2,48,248]{2,1,0:T(8,128)(2,1)S(1)}, u32[]{:S(2)}, u32[]{:S(2)}) collective-permute-start(bf16[2,48,248]{2,1,0:T(8,128)(2,1)S(1)} %pad_maximum_fusion.12), channel_id=1, source_target_pairs={{0,8},{4,12},{8,0},{12,4},{16,24},{20,28},{24,16},{28,20},{1,9},{5... | collective-permute-start | bytes 142856 | tf_op jit(solution)/shard_map/ppermute | solution.py:382
  199.8 16.3 %collective-permute-start.15 = (bf16[18,32,96]{2,1,0:T(8,128)(2,1)S(1)}, bf16[18,32,96]{2,1,0:T(8,128)(2,1)S(1)}, u32[]{:S(2)}, u32[]{:S(2)}) collective-permute-start(bf16[18,32,96]{2,1,0:T(8,128)(2,1)S(1)} %get-tuple-element.37), channel_id=1, source_target_pairs={{0,1},{1,0},{2,3},{3,2},{4,5},{5,4},{6,7},{7,6},{8,9},{9,8},{10,11... | collective-permute-start | bytes 331784 | tf_op jit(solution)/shard_map/ppermute | solution.py:374
  199.9 16.2 %collective-permute-start.16 = (bf16[18,32,96]{2,1,0:T(8,128)(2,1)S(1)}, bf16[18,32,96]{2,1,0:T(8,128)(2,1)S(1)}, u32[]{:S(2)}, u32[]{:S(2)}) collective-permute-start(bf16[18,32,96]{2,1,0:T(8,128)(2,1)S(1)} %get-tuple-element.38), channel_id=1, source_target_pairs={{0,2},{1,3},{2,0},{3,1},{4,6},{5,7},{6,4},{7,5},{8,10},{9,11},{10,... | collective-permute-start | bytes 331784 | tf_op jit(solution)/shard_map/ppermute | solution.py:374
  201.8 14.4 %collective-permute-start.17 = (bf16[18,32,96]{2,1,0:T(8,128)(2,1)S(1)}, bf16[18,32,96]{2,1,0:T(8,128)(2,1)S(1)}, u32[]{:S(2)}, u32[]{:S(2)}) collective-permute-start(bf16[18,32,96]{2,1,0:T(8,128)(2,1)S(1)} %get-tuple-element.39), channel_id=1, source_target_pairs={{0,3},{1,2},{2,1},{3,0},{4,7},{5,6},{6,5},{7,4},{8,11},{9,10},{10,... | collective-permute-start | bytes 331784 | tf_op jit(solution)/shard_map/ppermute | solution.py:374
  214.2 5.0 %collective-permute-start.19 = (bf16[2,2,48,248]{3,2,0,1:T(8,128)(2,1)S(1)}, bf16[2,2,48,248]{3,2,0,1:T(8,128)(2,1)S(1)}, u32[]{:S(2)}, u32[]{:S(2)}) collective-permute-start(bf16[2,2,48,248]{3,2,0,1:T(8,128)(2,1)S(1)} %pad_maximum_fusion.8), channel_id=1, source_target_pairs={{0,4},{4,0},{8,12},{12,8},{16,20},{20,16},{24,28},{28,24},{1,5},{5... | collective-permute-start | bytes 285704 | tf_op jit(solution)/shard_map/ppermute | solution.py:382
  227.8 3.3 %collective-permute-start.20 = (bf16[18,16,96]{2,1,0:T(8,128)(2,1)S(1)}, bf16[18,16,96]{2,1,0:T(8,128)(2,1)S(1)}, u32[]{:S(2)}, u32[]{:S(2)}) collective-permute-start(bf16[18,16,96]{2,1,0:T(8,128)(2,1)S(1)} %get-tuple-element.41), channel_id=1, source_target_pairs={{0,1},{1,0},{2,3},{3,2},{4,5},{5,4},{6,7},{7,6},{8,9},{9,8},{10,11... | collective-permute-start | bytes 165896 | tf_op jit(solution)/shard_map/ppermute | solution.py:374
  227.9 4.8 %collective-permute-start.21 = (bf16[18,16,96]{2,1,0:T(8,128)(2,1)S(1)}, bf16[18,16,96]{2,1,0:T(8,128)(2,1)S(1)}, u32[]{:S(2)}, u32[]{:S(2)}) collective-permute-start(bf16[18,16,96]{2,1,0:T(8,128)(2,1)S(1)} %get-tuple-element.42), channel_id=1, source_target_pairs={{0,2},{1,3},{2,0},{3,1},{4,6},{5,7},{6,4},{7,5},{8,10},{9,11},{10,... | collective-permute-start | bytes 165896 | tf_op jit(solution)/shard_map/ppermute | solution.py:374
  229.8 4.2 %collective-permute-start.22 = (bf16[18,16,96]{2,1,0:T(8,128)(2,1)S(1)}, bf16[18,16,96]{2,1,0:T(8,128)(2,1)S(1)}, u32[]{:S(2)}, u32[]{:S(2)}) collective-permute-start(bf16[18,16,96]{2,1,0:T(8,128)(2,1)S(1)} %get-tuple-element.43), channel_id=1, source_target_pairs={{0,3},{1,2},{2,1},{3,0},{4,7},{5,6},{6,5},{7,4},{8,11},{9,10},{10,... | collective-permute-start | bytes 165896 | tf_op jit(solution)/shard_map/ppermute | solution.py:374
  (28 other events, 166.5 us)

commit v7 on v6

--- a/solution.py
+++ b/solution.py
@@ -126,7 +126,8 @@
 
 def spectra_of(order_table, owned, parts, part, fields, block, blocks, after):
     lon_count = fields.shape[1]
-    first, last = blocks
+    first, last, skip = blocks
+    last = last - skip
     slot_local, first_pair, last_pair = owned
     rows = order_table.shape[0] // slot_local * 2 * (last_pair - first_pair)
     cells = (last - first) * block
@@ -143,7 +144,7 @@
         in_specs=[
             pl.BlockSpec(order_table.shape, lambda i: (0,)),
             pl.BlockSpec((None,) + parts.shape[1:], lambda i: (part, 0, 0)),
-            pl.BlockSpec((block, lon_count), lambda i: (i + first, 0)),
+            pl.BlockSpec((block, lon_count), lambda i: (i + first + (i > 0) * skip, 0)),
         ]
         + [ANY] * len(after),
         out_specs=pl.BlockSpec((rows, block), lambda i: (0, i)),
@@ -161,7 +162,8 @@
 
 
 def digest_kernel(shape, lag_ref, me_ref, weight_ref, lat_hbm, *refs):
-    groups, hops, narrow_count, lat_local, n_after = shape
+    groups, hops, narrow_count, lat_local, n_after, spans, ranges, kind = shape
+    edge_refs, refs = refs[: kind == "last"], refs[kind == "last" :]
     by_hop, blocks, refs = refs[:hops], list(refs[hops : hops + groups]), refs[hops + groups + n_after :]
     lat_ref, stage_ref, sems = refs[-3:]
     refs = refs[:-3]
@@ -180,14 +182,23 @@
         for copy in copies[-hops:]:
             copy.wait()
     sends, pick_refs = refs[:narrow_count], refs[narrow_count:-3]
+    made_refs, pick_refs = (pick_refs, []) if kind == "edges" else ([], pick_refs)
     line_ref, series_ref, block_ref = refs[-3:]
     days, slots, degrees = series_ref.shape
     half, padded = slots // 2, line_ref.shape[1] // 2
-    start = 0
+    for edge_ref in edge_refs:
+        for index, first in enumerate((spans[0][0] - LAGMAX, spans[0][1])):
+            series_ref[first : first + LAGMAX] = edge_ref[index * LAGMAX : (index + 1) * LAGMAX]
+    pieces = []
     for block in blocks:
-        stop = start + block.shape[2] // lat_local
+        used = 0
+        while used < block.shape[2] // lat_local:
+            start, stop = spans[len(pieces)]
+            pieces.append((block, used, start, stop))
+            used += stop - start
+    for block, used, start, stop in pieces:
         for day in range(start, stop):
-            cells = slice((day - start) * lat_local, (day - start + 1) * lat_local)
+            cells = slice((used + day - start) * lat_local, (used + day - start + 1) * lat_local)
             for source in range(block.shape[0]):
                 lats = slice(source * lat_local, (source + 1) * lat_local)
                 if half == padded:
@@ -195,7 +206,7 @@
                 else:
                     line_ref[day, :half, lats] = block[source, :half, cells]
                     line_ref[day, padded : padded + half, lats] = block[source, half:, cells]
-        if start == 0 and lat_ref is not lat_hbm:
+        if start == spans[0][0] and lat_ref is not lat_hbm:
             copies[0].wait()
         for parity in range(2):
             lines = line_ref[start:stop, parity * padded : (parity + 1) * padded, :]
@@ -206,7 +217,6 @@
             )
             coeffs = coeffs.astype(jnp.bfloat16).reshape(stop - start, padded, degrees)
             series_ref[start:stop, parity * half : (parity + 1) * half, :] = coeffs[:, :half]
-        start = stop
 
     step = 16 if slots % 16 == 0 else slots
     lags = [lag_ref[i] for i in range(3)]
@@ -221,17 +231,21 @@
                 residual = residual - weight * series_ref[day - lag, rows, :].astype(jnp.float32)
             return total + residual * residual
 
-        total = lax.fori_loop(
-            LAGMAX, days, add_day, jnp.zeros((step, degrees), jnp.float32), unroll=4
-        )
+        total = jnp.zeros((step, degrees), jnp.float32)
+        for start, stop in ranges:
+            total = lax.fori_loop(start, stop, add_day, total, unroll=4)
         coarse = total.astype(jnp.bfloat16)
         fine = (total - coarse.astype(jnp.float32)).astype(jnp.bfloat16)
         for owner in range(narrow_count):
             own = slice(owner * deg_local, (owner + 1) * deg_local)
-            block_ref[owner, :LAGMAX, rows, :] = series_ref[:LAGMAX, rows, own]
-            block_ref[owner, LAGMAX : 2 * LAGMAX, rows, :] = series_ref[days - LAGMAX :, rows, own]
-            block_ref[owner, 2 * LAGMAX, rows, :] = coarse[:, own]
-            block_ref[owner, 2 * LAGMAX + 1, rows, :] = fine[:, own]
+            if kind != "last":
+                block_ref[owner, :LAGMAX, rows, :] = series_ref[:LAGMAX, rows, own]
+                block_ref[owner, LAGMAX : 2 * LAGMAX, rows, :] = series_ref[days - LAGMAX :, rows, own]
+            block_ref[owner, block_ref.shape[1] - 2, rows, :] = coarse[:, own]
+            block_ref[owner, block_ref.shape[1] - 1, rows, :] = fine[:, own]
+    for made_ref in made_refs:
+        for index, first in enumerate((spans[0][1] - LAGMAX, spans[1][0])):
+            made_ref[index * LAGMAX : (index + 1) * LAGMAX] = series_ref[first : first + LAGMAX]
     for pick_ref in pick_refs:
         for owner in range(narrow_count):
             kept = slice(owner * (ROW_DEG + 1), (owner + 1) * (ROW_DEG + 1))
@@ -242,28 +256,36 @@
         send[...] = block_ref[peer(me, hop, narrow_count)[0]]
 
 
-def digest(lag_days, me, received, lat_table, weights, narrow_count, wants_picks, after):
+def digest(lag_days, me, received, lat_table, weights, narrow_count, days_local, spans, kind, edges, after):
+    ranges = [(LAGMAX, days_local)]
+    if kind == "edges":
+        ranges = [(LAGMAX, spans[0][1]), (spans[1][0] + LAGMAX, days_local)]
+    if kind == "last":
+        ranges = [(spans[0][0], spans[0][1] + LAGMAX)]
     by_hop = received[0] if isinstance(received[0], list) else []
     received = received[1:] if by_hop else received
     sources, slots, _ = received[0].shape
     latitudes, degrees = lat_table.shape[-2], lat_table.shape[-1] // 2
     lat_local = latitudes // sources
-    days_local = sum(block.shape[-1] for block in by_hop[:1] + received) // lat_local
     deg_local = degrees // narrow_count
     padded = 2 * (-(-(slots // 2) // 8) * 8)
-    message = (2 * LAGMAX + 2, slots, deg_local)
-    picked = (days_local, slots, narrow_count * (ROW_DEG + 1))
+    message = (2 if kind == "last" else 2 * LAGMAX + 2, slots, deg_local)
+    extras = {
+        "picks": [(days_local, slots, narrow_count * (ROW_DEG + 1))],
+        "edges": [(2 * LAGMAX, slots, degrees)],
+    }.get(kind, [])
     return pl.pallas_call(
         functools.partial(
-            digest_kernel, (len(received), len(by_hop), narrow_count, lat_local, len(after))
+            digest_kernel, (len(received), len(by_hop), narrow_count, lat_local, len(after), spans, ranges, kind)
         ),
         in_specs=[IN_SMEM, IN_SMEM, IN_VMEM, IN_HBM if lat_table.ndim == 3 else IN_VMEM]
+        + [IN_VMEM] * len(edges)
         + [ANY] * len(by_hop)
         + [IN_VMEM] * len(received)
         + [ANY] * len(after),
-        out_specs=[IN_VMEM] * (narrow_count + wants_picks),
+        out_specs=[IN_VMEM] * (narrow_count + len(extras)),
         out_shape=[jax.ShapeDtypeStruct(message, jnp.bfloat16)] * narrow_count
-        + [jax.ShapeDtypeStruct(picked, jnp.bfloat16)] * wants_picks,
+        + [jax.ShapeDtypeStruct(shape, jnp.bfloat16) for shape in extras],
         scratch_shapes=[
             pltpu.VMEM((days_local, padded, latitudes), jnp.bfloat16),
             pltpu.VMEM((days_local, slots, degrees), jnp.bfloat16),
@@ -272,13 +294,13 @@
             pltpu.VMEM((sources,) + by_hop[0].shape if by_hop else (8, 128), jnp.bfloat16),
             pltpu.SemaphoreType.DMA((len(by_hop) + 1,)),
         ],
-        compiler_params=pltpu.CompilerParams(vmem_limit_bytes=FULL_VMEM if slots > 32 else VMEM // 2),
+        compiler_params=pltpu.CompilerParams(vmem_limit_bytes=FULL_VMEM if kind == "picks" else VMEM // 2),
         cost_estimate=pl.CostEstimate(
             flops=4 * slots * days_local * latitudes * degrees,
             bytes_accessed=2 * slots * days_local * (latitudes + degrees),
             transcendentals=0,
         ),
-    )(lag_days, me, weights, lat_table, *by_hop, *received, *after)
+    )(lag_days, me, weights, lat_table, *edges, *by_hop, *received, *after)
 
 
 def tie(array, after):
@@ -312,18 +334,20 @@
 def combine_kernel(count, final, lag_ref, me_ref, weight_ref, *refs):
     got, others, (out_ref, seam_ref, sum_ref) = refs[:count], refs[count:-3], refs[-3:]
     me = me_ref[0]
+    seams = got[0].shape[0] > 2
     total = jnp.zeros(sum_ref.shape[1:], jnp.float32)
     for hop in range(count):
         source = peer(me, hop, count)[1]
-        seam_ref[source, LAGMAX:] = got[hop][:LAGMAX]
-        seam_ref[source + 1, :LAGMAX] = got[hop][LAGMAX : 2 * LAGMAX]
-        sums = got[hop][2 * LAGMAX :].astype(jnp.float32)
+        if seams:
+            seam_ref[source, LAGMAX:] = got[hop][:LAGMAX]
+            seam_ref[source + 1, :LAGMAX] = got[hop][LAGMAX : 2 * LAGMAX]
+        sums = got[hop][got[hop].shape[0] - 2 :].astype(jnp.float32)
         sum_ref[source] = sums[0] + sums[1]
     for source in range(count):
         total = total + sum_ref[source]
     lags = [lag_ref[i] for i in range(3)]
     weights = [weight_ref[i] for i in range(3)]
-    for block in range(1, count):
+    for block in range(1, count) if seams else []:
         for day in range(LAGMAX, 2 * LAGMAX):
             residual = seam_ref[block, day].astype(jnp.float32)
             for lag, weight in zip(lags, weights):
@@ -332,8 +356,11 @@
     if final is None:
         out_ref[...] = total
         return
+    kept_days, places = final
     sum_ref[0] = total
-    kept_days, places = final
+    if not seams:
+        sum_ref[0] = total + others[-1][...]
+        others = others[:-1]
     for source, (part, first, last) in zip([*others, sum_ref.at[0]], places):
         held = last - first
         for parity in range(2):
@@ -398,10 +425,10 @@
 
 def plan_of(slot_local, days_local, day_block, wide_count):
     pairs, blocks = slot_local // 2, days_local // day_block
-    every = (0, blocks)
-    if slot_local % 48 == 0 and blocks > 1 and wide_count & (wide_count - 1) == 0:
-        cut = pairs * 2 // 3
-        sent = [(0, 0, pairs, (0, 1)), (0, 0, pairs, (1, blocks)), (1, 0, cut, every), (1, cut, pairs, every)]
+    every = (0, blocks, 0)
+    if slot_local % 16 == 0 and blocks > 2 and wide_count & (wide_count - 1) == 0:
+        sent = [(0, 0, pairs, (0, 1, 0)), (0, 0, pairs, (1, blocks, 0))]
+        sent += [(1, 0, pairs, (0, blocks, 1)), (1, 0, pairs, (1, 2, 0))]
         return sent, [(0, 1), (2,), (3,)]
     return [(0, 0, pairs, every), (1, 0, pairs, every)], [(0,), (1,)]
 
@@ -451,8 +478,14 @@
         spectra = spectra.reshape(wide_count, -1, spectra.shape[1])
         return lax.all_to_all(spectra, "wide", split_axis=0, concat_axis=0, tiled=True)
 
-    def finish(job, after, table, others=(), final=None):
-        part, first, last, _ = sent[job[0]]
+    def finish(job, after, table, others=(), final=None, edges=()):
+        part, first, last, (begin, end, skip) = sent[job[0]]
+        spans = []
+        for index in job:
+            begin, end, skip = sent[index][3]
+            cuts = [(begin, end)] if not skip else [(begin, begin + 1), (begin + 1 + skip, end)]
+            spans += [(a * day_block, b * day_block) for a, b in cuts]
+        kind = "picks" if part == 0 else "edges" if skip else "last" if edges else "sums"
         out = digest(
             lag_days,
             me,
@@ -460,10 +493,13 @@
             table,
             rows_of(all_weights, part, first, last),
             narrow_count,
-            part == 0,
+            days_local,
+            spans,
+            kind,
+            edges,
             after,
         )
-        sends, picks = out[:narrow_count], out[narrow_count:]
+        sends, extras = out[:narrow_count], out[narrow_count:]
         total = combine(
             lag_days,
             me,
@@ -474,9 +510,9 @@
         )
         for parity in range(2):
             rows = slice(parity * (last - first), (parity + 1) * (last - first))
-            if picks:
-                picked[parity, first] = picks[0][:, rows]
-        return total, sends[0]
+            if part == 0:
+                picked[parity, first] = extras[0][:, rows]
+        return total, extras
 
     def panel_rows():
         series = jnp.stack(
@@ -532,12 +568,13 @@
     if len(sent) > 2:
         received.append(exchange(tie(spectra[len(sent) - 1], done + [far])))
     panel = panel_of(rows, column, far)
+    edges = []
     for job in jobs[1:-1]:
-        total, message = finish(job, [], lat_table)
-        table = hold(lat_table, [message])
+        total, edges = finish(job, [], lat_table)
+        table = hold(lat_table, [total])
         done.append(total)
-    places = [sent[job[0]][:3] for job in jobs]
-    variances, _ = finish(jobs[-1], done + [panel], table, done, (kept_days, places))
+    places = [sent[job[0]][:3] for job in (jobs[0], jobs[-1])]
+    variances, _ = finish(jobs[-1], done + [panel], table, done, (kept_days, places), edges)
     noise_variance = jnp.transpose(variances, (2, 0, 1))
     return (noise_variance, panel)
 

time: 236 us -> 235 us (level)
  Pallas kernels: 67.8 us -> 64.1 us
    pallas_call x3, Pallas kernels: 35 us -> 32.3 us  [spectra_of(): pl.pallas_call(functools.partial(spectra_kernel, owned), grid=(last - fir...]
  transfers between devices with their start and end apart: 26 -> 26, of which waited for: 14 -> 15; matrix products, arithmetic and copies ran while one was open for 6% -> 6% of each run, Pallas kernels for 24% -> 22%
where the time goes in v7:
time: 235 us; the launch traced here: 234 us
  waiting for transfers between devices  102 us (43%)
  Pallas kernels  64.1 us (27%)
  starting transfers between devices  47.5 us (20%)
  local copies, waits for them, and re-layouts  11.6 us (5%)
  between operations  4.94 us (2%)
  other arithmetic  3.7 us (2%)
    ppermute x7, waiting for transfers between devices, gather_swap(): return lax.ppermute(held, axis, [(i, i ^ reach) for i in range(count)])  46.4 us
    all_to_all x3, waiting for transfers between devices, exchange(): lax.all_to_all(spectra, 'wide', split_axis=0, concat_axis=0, tiled=True)  46 us
    pallas_call x3, Pallas kernels, spectra_of(): pl.pallas_call(functools.partial(spectra_kernel, owned), grid=(last - fir...  32.3 us
    pallas_call x3, Pallas kernels, digest(): pl.pallas_call(functools.partial(digest_kernel, (len(received), len(by_ho...  21.9 us
    ppermute x16, starting transfers between devices, swap(): lax.ppermute(sends[hop], axis, [(i, peer(i, hop, count)[0]) for i in rang...  20 us
    all_to_all x3, starting transfers between devices, exchange(): lax.all_to_all(spectra, 'wide', split_axis=0, concat_axis=0, tiled=True)  17.7 us
    ppermute x16, waiting for transfers between devices, swap(): lax.ppermute(sends[hop], axis, [(i, peer(i, hop, count)[0]) for i in rang...  9.78 us
    ppermute x7, starting transfers between devices, gather_swap(): return lax.ppermute(held, axis, [(i, i ^ reach) for i in range(count)])  9.76 us
  transfers between devices with their start and end apart: 26, of which 15 were waited for; matrix products, arithmetic and copies ran while one was open for 6% of the time, Pallas kernels for 22%

profile of v7, /device:TPU:0, one launch (start us, length us, event | category | flops | bytes accessed | tf_op | source)
XLA Modules:
  0.0 234.3 jit_solution(1736311275057483069)
XLA Ops:
  0.6 6.7 %shard_map.77 = (bf16[48,1408]{1,0:T(8,128)(2,1)}, bf16[48,1408]{1,0:T(8,128)(2,1)}, bf16[48,1408]{1,0:T(8,128)(2,1)}, bf16[48,1408]{1,0:T(8,128)(2,1)}, bf16[48...) custom-call(s32[384]{0:T(512)} %order_ref.7, ...), custom_call_target="tpu_custom_call" | custom-call | flops 1557135360 | bytes 6242304 | tf_op jit(solution)/shard_map/pallas_call | solution.py:108
  7.4 3.0 %collective-permute-start.2 = (bf16[48,1408]{1,0:T(8,128)(2,1)}, bf16[48,1408]{1,0:T(8,128)(2,1)}, u32[]{:S(2)}, u32[]{:S(2)}) collective-permute-start(bf16[48,1408]{1,0:T(8,128)(2,1)} %get-tuple-element.25), channel_id=1, source_target_pairs={{0,4},{4,0},{8,12},{12,8},{16,20},{20,16},{24,28},{28,24},{1,5},{5... | collective-permute-start | bytes 405512 | tf_op jit(solution)/shard_map/ppermute | solution.py:401
  12.0 3.0 %collective-permute-start.5 = (bf16[48,1408]{1,0:T(8,128)(2,1)}, bf16[48,1408]{1,0:T(8,128)(2,1)}, u32[]{:S(2)}, u32[]{:S(2)}) collective-permute-start(bf16[48,1408]{1,0:T(8,128)(2,1)} %get-tuple-element.28), channel_id=1, source_target_pairs={{0,16},{4,20},{8,24},{12,28},{16,0},{20,4},{24,8},{28,12},{1,17},{... | collective-permute-start | bytes 405512 | tf_op jit(solution)/shard_map/ppermute | solution.py:401
  16.2 3.6 %collective-permute-start.7 = (bf16[48,1408]{1,0:T(8,128)(2,1)}, bf16[48,1408]{1,0:T(8,128)(2,1)}, u32[]{:S(2)}, u32[]{:S(2)}) collective-permute-start(bf16[48,1408]{1,0:T(8,128)(2,1)} %get-tuple-element.30), channel_id=1, source_target_pairs={{0,24},{4,28},{8,16},{12,20},{16,8},{20,12},{24,0},{28,4},{1,25},{... | collective-permute-start | bytes 405512 | tf_op jit(solution)/shard_map/ppermute | solution.py:401
  19.8 1.9 collective-permute-done.3.refs_2_
  22.5 12.5 %shard_map.78.refs_0_ = bf16[384,4224]{1,0:T(8,128)(2,1)} custom-call(s32[384]{0:T(512)} %order_ref.7, bf16[2,1440,384]{2,1,0:T(8,128)(2,1)} %constant.42.clone.part_hbm.part_ref, bf16[5632,1440]{1,0:T(8,128)(2,1)} %bitcast.100, bf16[48,1408]{1,0:T(8,128)(2,1)} %get-tuple-element.24.refs_0_), custom_call_target="tpu_custom_call" | custom-call | flops 4671406080 | bytes 16515072 | tf_op jit(solution)/shard_map/pallas_call | solution.py:141
  35.2 8.2 %all-to-all-start.1 = ((bf16[8,48,4224]{2,1,0:T(8,128)(2,1)}), bf16[8,48,4224]{2,1,0:T(8,128)(2,1)}, u32[]{:S(2)}, u32[]{:S(2)}) async-start(bf16[8,48,4224]{2,1,0:T(8,128)(2,1)} %bitcast.103), calls=%async_computation.1 | async-start | bytes 6488064 | tf_op jit(solution)/shard_map/all_to_all | solution.py:479
  45.0 3.6 %collective-permute-done = f32[2,2,3,24,96]{4,3,2,1,0:T(8,128)S(1)} collective-permute-done((f32[2,2,3,24,96]{4,3,2,1,0:T(8,128)S(1)}, f32[2,2,3,24,96]{4,3,2,1,0:T(8,128)S(1)}, u32[]{:S(2)}, u32[]{:S(2)}) %collective-permute-start) | collective-permute-done | bytes 110624 | tf_op jit(solution)/shard_map/ppermute | solution.py:409
  52.7 7.2 %shard_map.80.refs_0_ = bf16[384,1408]{1,0:T(8,128)(2,1)} custom-call(s32[384]{0:T(512)} %order_ref.7, bf16[2,1440,384]{2,1,0:T(8,128)(2,1)} %constant.42.clone.part_hbm.part_ref, bf16[5632,1440]{1,0:T(8,128)(2,1)} %bitcast.101, bf16[384,4224]{1,0:T(8,128)(2,1)} %shard_map.79.refs_0_, f32[2,2,3,24,384]{4,3,2,1,0:T(8,128)} %reshape.65.refs_1_), custom_call_target="tpu_custom_call" | custom-call | flops 1557135360 | bytes 6242304 | tf_op jit(solution)/shard_map/pallas_call | solution.py:141
  60.0 12.5 %shard_map.81 = bf16[384,4224]{1,0:T(8,128)(2,1)} custom-call(s32[384]{0:T(512)} %order_ref.7, bf16[2,1440,384]{2,1,0:T(8,128)(2,1)} %constant.42.clone.part_hbm.part_ref, bf16[5632,1440]{1,0:T(8,128)(2,1)} %bitcast.102, bf16[384,1408]{1,0:T(8,128)(2,1)} %shard_map.80.refs_0_, f32[2,2,3,24,384]{4,3,2,1,0:T(8,128)} %reshape.65.refs_1_), custom_call_target="tpu_custom_call" | custom-call | flops 4671406080 | bytes 16515072 | tf_op jit(solution)/shard_map/pallas_call | solution.py:141
  72.5 43.6 %all-to-all-done.1.refs_8_ = bf16[8,48,4224]{2,1,0:T(8,128)(2,1)} async-done(((bf16[8,48,4224]{2,1,0:T(8,128)(2,1)}), bf16[8,48,4224]{2,1,0:T(8,128)(2,1)}, u32[]{:S(2)}, u32[]{:S(2)}) %all-to-all-start.1) | async-done | bytes 3244064 | tf_op jit(solution)/shard_map/all_to_all | solution.py:479
  116.1 4.8 %all-to-all-start = ((bf16[8,48,4224]{2,1,0:T(8,128)(2,1)}), bf16[8,48,4224]{2,1,0:T(8,128)(2,1)}, u32[]{:S(2)}, u32[]{:S(2)}) async-start(bf16[8,48,4224]{2,1,0:T(8,128)(2,1)} %bitcast.105), calls=%async_computation | async-start | bytes 6488064 | tf_op jit(solution)/shard_map/all_to_all | solution.py:479
  129.5 11.7 %shard_map.85 = (bf16[18,48,96]{2,1,0:T(8,128)(2,1)}, bf16[18,48,96]{2,1,0:T(8,128)(2,1)}, bf16[18,48,96]{2,1,0:T(8,128)(2,1)}, bf16[18,48,96]{2,1,0:T(8,128)(2,1)}, bf16[64,48,16]{2,1,0:T(8,128)(2,1)}) custom-call(s32[3]{0:T(128)} %lag_ref.11, s32[2]{0:T(128)} %pad_add_fusion.me_ref, f32[3,48,384]{2,1,0:T(8,128)} %pad_maximum_fusion.4.weight_ref, ...), custom_call_target="tpu_custom_call" | custom-call | flops 3321888768 | bytes 6684672 | tf_op jit(solution)/shard_map/pallas_call | solution.py:277
  145.0 2.8 %collective-permute-done.15 = bf16[48,1024]{1,0:T(8,128)(2,1)S(1)} collective-permute-done((bf16[48,1024]{1,0:T(8,128)(2,1)S(1)}, bf16[48,1024]{1,0:T(8,128)(2,1)S(1)}, u32[]{:S(2)}, u32[]{:S(2)}) %collective-permute-start.15) | collective-permute-done | bytes 98336 | tf_op jit(solution)/shard_map/ppermute | solution.py:409
  153.5 2.7 %collective-permute-start.17 = (bf16[48,248]{1,0:T(8,128)(2,1)S(1)}, bf16[48,248]{1,0:T(8,128)(2,1)S(1)}, u32[]{:S(2)}, u32[]{:S(2)}) collective-permute-start(bf16[48,248]{1,0:T(8,128)(2,1)S(1)} %dynamic-slice_bitcast_fusion), channel_id=1, source_target_pairs={{0,16},{4,20},{8,24},{12,28},{16,0},{20,4},{24,8},{28,12},{1,17},{... | collective-permute-start | bytes 71432 | tf_op jit(solution)/shard_map/ppermute | solution.py:409
  157.5 3.1 %collective-permute-done.14.refs_3_ = bf16[18,48,96]{2,1,0:T(8,128)(2,1)S(1)} collective-permute-done((bf16[18,48,96]{2,1,0:T(8,128)(2,1)S(1)}, bf16[18,48,96]{2,1,0:T(8,128)(2,1)S(1)}, u32[]{:S(2)}, u32[]{:S(2)}) %collective-permute-start.14) | collective-permute-done | bytes 165920 | tf_op jit(solution)/shard_map/ppermute | solution.py:401
  162.2 30.5 %collective-permute-done.17.refs_2_ = bf16[48,248]{1,0:T(8,128)(2,1)S(1)} collective-permute-done((bf16[48,248]{1,0:T(8,128)(2,1)S(1)}, bf16[48,248]{1,0:T(8,128)(2,1)S(1)}, u32[]{:S(2)}, u32[]{:S(2)}) %collective-permute-start.17) | collective-permute-done | bytes 23840 | tf_op jit(solution)/shard_map/ppermute | solution.py:409
  193.4 4.6 %all-to-all-start.2 = ((bf16[8,48,1408]{2,1,0:T(8,128)(2,1)}), bf16[8,48,1408]{2,1,0:T(8,128)(2,1)}, u32[]{:S(2)}, u32[]{:S(2)}) async-start(bf16[8,48,1408]{2,1,0:T(8,128)(2,1)} %bitcast.104), calls=%async_computation.2 | async-start | bytes 2162688 | tf_op jit(solution)/shard_map/all_to_all | solution.py:479
  199.8 6.7 %shard_map.82 = (bf16[18,48,96]{2,1,0:T(8,128)(2,1)S(1)}, bf16[18,48,96]{2,1,0:T(8,128)(2,1)S(1)}, bf16[18,48,96]{2,1,0:T(8,128)(2,1)S(1)}, bf16[18,48,96]{2,1,0:T(8,128)(2,1)S(1)}, bf16[16,48,384]{2,1,0:T(8,128)(2,1)S(1)}) custom-call(s32[3]{0:T(128)S(1)} %copy-done.8, s32[2]{0:T(128)S(1)} %copy-done.9, f32[3,48,384]{2,1,0:T(8,128)S(1)} %pad_maximum_fusion.3.weight_ref, ...), custom_call_target="tpu_custom_call" | custom-call | flops 3321888768 | bytes 6684672 | tf_op jit(solution)/shard_map/pallas_call | solution.py:277
  206.5 2.1 collective-permute-start.10
  208.7 7.2 %collective-permute-done.18 = bf16[2,48,248]{2,1,0:T(8,128)(2,1)S(1)} collective-permute-done((bf16[2,48,248]{2,1,0:T(8,128)(2,1)S(1)}, bf16[2,48,248]{2,1,0:T(8,128)(2,1)S(1)}, u32[]{:S(2)}, u32[]{:S(2)}) %collective-permute-start.18) | collective-permute-done | bytes 47648 | tf_op jit(solution)/shard_map/ppermute | solution.py:409
  221.7 2.4 %all-to-all-done.2.refs_1_ = bf16[8,48,1408]{2,1,0:T(8,128)(2,1)} async-done(((bf16[8,48,1408]{2,1,0:T(8,128)(2,1)}), bf16[8,48,1408]{2,1,0:T(8,128)(2,1)}, u32[]{:S(2)}, u32[]{:S(2)}) %all-to-all-start.2) | async-done | bytes 1081376 | tf_op jit(solution)/shard_map/all_to_all | solution.py:479
  224.1 3.5 %shard_map.88 = (bf16[2,48,96]{2,1,0:T(8,128)(2,1)S(1)}, bf16[2,48,96]{2,1,0:T(8,128)(2,1)S(1)}, bf16[2,48,96]{2,1,0:T(8,128)(2,1)S(1)}, bf16[2,48,96]{2,1,0:T(8,128)(2,1)S(1)}) custom-call(s32[3]{0:T(128)S(1)} %copy-done.8, s32[2]{0:T(128)S(1)} %copy-done.9, f32[3,48,384]{2,1,0:T(8,128)S(1)} %copy-done.5, bf16[704,768]{1,0:T(8,128)(2,1)S(1)} %shard_map.84.lat_hbm, ...), custom_call_target="tpu_custom_call" | custom-call | flops 3321888768 | bytes 6684672 | tf_op jit(solution)/shard_map/pallas_call | solution.py:277
  227.7 2.1 collective-permute-start.21
  (145 shorter events, 39.0 us)
Async XLA Ops:
  7.4 8.9 %collective-permute-start.2 = (bf16[48,1408]{1,0:T(8,128)(2,1)}, bf16[48,1408]{1,0:T(8,128)(2,1)}, u32[]{:S(2)}, u32[]{:S(2)}) collective-permute-start(bf16[48,1408]{1,0:T(8,128)(2,1)} %get-tuple-element.25), channel_id=1, source_target_pairs={{0,4},{4,0},{8,12},{12,8},{16,20},{20,16},{24,28},{28,24},{1,5},{5... | collective-permute-start | bytes 405512 | tf_op jit(solution)/shard_map/ppermute | solution.py:401
  10.4 11.4 %collective-permute-start.3 = (bf16[48,1408]{1,0:T(8,128)(2,1)}, bf16[48,1408]{1,0:T(8,128)(2,1)}, u32[]{:S(2)}, u32[]{:S(2)}) collective-permute-start(bf16[48,1408]{1,0:T(8,128)(2,1)} %get-tuple-element.26), channel_id=1, source_target_pairs={{0,8},{4,12},{8,0},{12,4},{16,24},{20,28},{24,16},{28,20},{1,9},{5... | collective-permute-start | bytes 405512 | tf_op jit(solution)/shard_map/ppermute | solution.py:401
  12.0 23.1 %collective-permute-start.4 = (bf16[48,1408]{1,0:T(8,128)(2,1)}, bf16[48,1408]{1,0:T(8,128)(2,1)}, u32[]{:S(2)}, u32[]{:S(2)}) collective-permute-start(bf16[48,1408]{1,0:T(8,128)(2,1)} %get-tuple-element.27), channel_id=1, source_target_pairs={{0,12},{4,8},{8,4},{12,0},{16,28},{20,24},{24,20},{28,16},{1,13},{... | collective-permute-start | bytes 405512 | tf_op jit(solution)/shard_map/ppermute | solution.py:401
  12.0 23.1 %collective-permute-start.5 = (bf16[48,1408]{1,0:T(8,128)(2,1)}, bf16[48,1408]{1,0:T(8,128)(2,1)}, u32[]{:S(2)}, u32[]{:S(2)}) collective-permute-start(bf16[48,1408]{1,0:T(8,128)(2,1)} %get-tuple-element.28), channel_id=1, source_target_pairs={{0,16},{4,20},{8,24},{12,28},{16,0},{20,4},{24,8},{28,12},{1,17},{... | collective-permute-start | bytes 405512 | tf_op jit(solution)/shard_map/ppermute | solution.py:401
  14.9 20.2 %collective-permute-start.6 = (bf16[48,1408]{1,0:T(8,128)(2,1)}, bf16[48,1408]{1,0:T(8,128)(2,1)}, u32[]{:S(2)}, u32[]{:S(2)}) collective-permute-start(bf16[48,1408]{1,0:T(8,128)(2,1)} %get-tuple-element.29), channel_id=1, source_target_pairs={{0,20},{4,16},{8,28},{12,24},{16,4},{20,0},{24,12},{28,8},{1,21},{... | collective-permute-start | bytes 405512 | tf_op jit(solution)/shard_map/ppermute | solution.py:401
  16.2 19.0 %collective-permute-start.7 = (bf16[48,1408]{1,0:T(8,128)(2,1)}, bf16[48,1408]{1,0:T(8,128)(2,1)}, u32[]{:S(2)}, u32[]{:S(2)}) collective-permute-start(bf16[48,1408]{1,0:T(8,128)(2,1)} %get-tuple-element.30), channel_id=1, source_target_pairs={{0,24},{4,28},{8,16},{12,20},{16,8},{20,12},{24,0},{28,4},{1,25},{... | collective-permute-start | bytes 405512 | tf_op jit(solution)/shard_map/ppermute | solution.py:401
  21.8 13.4 %collective-permute-start.8 = (bf16[48,1408]{1,0:T(8,128)(2,1)}, bf16[48,1408]{1,0:T(8,128)(2,1)}, u32[]{:S(2)}, u32[]{:S(2)}) collective-permute-start(bf16[48,1408]{1,0:T(8,128)(2,1)} %get-tuple-element.31), channel_id=1, source_target_pairs={{0,28},{4,24},{8,20},{12,16},{16,12},{20,8},{24,4},{28,0},{1,29},{... | collective-permute-start | bytes 405512 | tf_op jit(solution)/shard_map/ppermute | solution.py:401
  35.2 80.9 %all-to-all-start.1 = ((bf16[8,48,4224]{2,1,0:T(8,128)(2,1)}), bf16[8,48,4224]{2,1,0:T(8,128)(2,1)}, u32[]{:S(2)}, u32[]{:S(2)}) async-start(bf16[8,48,4224]{2,1,0:T(8,128)(2,1)} %bitcast.103), calls=%async_computation.1 | async-start | bytes 6488064 | tf_op jit(solution)/shard_map/all_to_all | solution.py:479
  43.4 5.2 %collective-permute-start = (f32[2,2,3,24,96]{4,3,2,1,0:T(8,128)S(1)}, f32[2,2,3,24,96]{4,3,2,1,0:T(8,128)S(1)}, u32[]{:S(2)}, u32[]{:S(2)}) collective-permute-start(f32[2,2,3,24,96]{4,3,2,1,0:T(8,128)S(1)} %bitcast.112), channel_id=1, source_target_pairs={{0,2},{1,3},{2,0},{3,1},{4,6},{5,7},{6,4},{7,5},{8,10},{9,11},{10,... | collective-permute-start | bytes 331784 | tf_op jit(solution)/shard_map/ppermute | solution.py:409
  116.1 77.2 %all-to-all-start = ((bf16[8,48,4224]{2,1,0:T(8,128)(2,1)}), bf16[8,48,4224]{2,1,0:T(8,128)(2,1)}, u32[]{:S(2)}, u32[]{:S(2)}) async-start(bf16[8,48,4224]{2,1,0:T(8,128)(2,1)} %bitcast.105), calls=%async_computation | async-start | bytes 6488064 | tf_op jit(solution)/shard_map/all_to_all | solution.py:479
  143.2 4.7 %collective-permute-start.15 = (bf16[48,1024]{1,0:T(8,128)(2,1)S(1)}, bf16[48,1024]{1,0:T(8,128)(2,1)S(1)}, u32[]{:S(2)}, u32[]{:S(2)}) collective-permute-start(bf16[48,1024]{1,0:T(8,128)(2,1)S(1)} %reshape.70), channel_id=1, source_target_pairs={{0,2},{1,3},{2,0},{3,1},{4,6},{5,7},{6,4},{7,5},{8,10},{9,11},{10,... | collective-permute-start | bytes 294920 | tf_op jit(solution)/shard_map/ppermute | solution.py:409
  148.5 7.7 %collective-permute-start.12 = (bf16[18,48,96]{2,1,0:T(8,128)(2,1)}, bf16[18,48,96]{2,1,0:T(8,128)(2,1)S(1)}, u32[]{:S(2)}, u32[]{:S(2)}) collective-permute-start(bf16[18,48,96]{2,1,0:T(8,128)(2,1)} %get-tuple-element.38), channel_id=1, source_target_pairs={{0,1},{1,0},{2,3},{3,2},{4,5},{5,4},{6,7},{7,6},{8,9},{9,8},{10,11... | collective-permute-start | bytes 497672 | tf_op jit(solution)/shard_map/ppermute | solution.py:401
  149.0 8.5 %collective-permute-start.13 = (bf16[18,48,96]{2,1,0:T(8,128)(2,1)}, bf16[18,48,96]{2,1,0:T(8,128)(2,1)S(1)}, u32[]{:S(2)}, u32[]{:S(2)}) collective-permute-start(bf16[18,48,96]{2,1,0:T(8,128)(2,1)} %get-tuple-element.39), channel_id=1, source_target_pairs={{0,2},{1,3},{2,0},{3,1},{4,6},{5,7},{6,4},{7,5},{8,10},{9,11},{10,... | collective-permute-start | bytes 497672 | tf_op jit(solution)/shard_map/ppermute | solution.py:401
  150.8 9.9 %collective-permute-start.14 = (bf16[18,48,96]{2,1,0:T(8,128)(2,1)S(1)}, bf16[18,48,96]{2,1,0:T(8,128)(2,1)S(1)}, u32[]{:S(2)}, u32[]{:S(2)}) collective-permute-start(bf16[18,48,96]{2,1,0:T(8,128)(2,1)S(1)} %copy-done.25), channel_id=1, source_target_pairs={{0,3},{1,2},{2,1},{3,0},{4,7},{5,6},{6,5},{7,4},{8,11},{9,10},{10,... | collective-permute-start | bytes 497672 | tf_op jit(solution)/shard_map/ppermute | solution.py:401
  153.5 39.3 %collective-permute-start.17 = (bf16[48,248]{1,0:T(8,128)(2,1)S(1)}, bf16[48,248]{1,0:T(8,128)(2,1)S(1)}, u32[]{:S(2)}, u32[]{:S(2)}) collective-permute-start(bf16[48,248]{1,0:T(8,128)(2,1)S(1)} %dynamic-slice_bitcast_fusion), channel_id=1, source_target_pairs={{0,16},{4,20},{8,24},{12,28},{16,0},{20,4},{24,8},{28,12},{1,17},{... | collective-permute-start | bytes 71432 | tf_op jit(solution)/shard_map/ppermute | solution.py:409
  193.4 30.7 %all-to-all-start.2 = ((bf16[8,48,1408]{2,1,0:T(8,128)(2,1)}), bf16[8,48,1408]{2,1,0:T(8,128)(2,1)}, u32[]{:S(2)}, u32[]{:S(2)}) async-start(bf16[8,48,1408]{2,1,0:T(8,128)(2,1)} %bitcast.104), calls=%async_computation.2 | async-start | bytes 2162688 | tf_op jit(solution)/shard_map/all_to_all | solution.py:479
  198.1 17.8 %collective-permute-start.18 = (bf16[2,48,248]{2,1,0:T(8,128)(2,1)S(1)}, bf16[2,48,248]{2,1,0:T(8,128)(2,1)S(1)}, u32[]{:S(2)}, u32[]{:S(2)}) collective-permute-start(bf16[2,48,248]{2,1,0:T(8,128)(2,1)S(1)} %pad_maximum_fusion.11), channel_id=1, source_target_pairs={{0,8},{4,12},{8,0},{12,4},{16,24},{20,28},{24,16},{28,20},{1,9},{5... | collective-permute-start | bytes 142856 | tf_op jit(solution)/shard_map/ppermute | solution.py:409
  206.5 11.4 %collective-permute-start.9 = (bf16[18,48,96]{2,1,0:T(8,128)(2,1)S(1)}, bf16[18,48,96]{2,1,0:T(8,128)(2,1)S(1)}, u32[]{:S(2)}, u32[]{:S(2)}) collective-permute-start(bf16[18,48,96]{2,1,0:T(8,128)(2,1)S(1)} %get-tuple-element.33), channel_id=1, source_target_pairs={{0,1},{1,0},{2,3},{3,2},{4,5},{5,4},{6,7},{7,6},{8,9},{9,8},{10,11... | collective-permute-start | bytes 497672 | tf_op jit(solution)/shard_map/ppermute | solution.py:401
  206.5 11.3 %collective-permute-start.10 = (bf16[18,48,96]{2,1,0:T(8,128)(2,1)S(1)}, bf16[18,48,96]{2,1,0:T(8,128)(2,1)S(1)}, u32[]{:S(2)}, u32[]{:S(2)}) collective-permute-start(bf16[18,48,96]{2,1,0:T(8,128)(2,1)S(1)} %get-tuple-element.34), channel_id=1, source_target_pairs={{0,2},{1,3},{2,0},{3,1},{4,6},{5,7},{6,4},{7,5},{8,10},{9,11},{10,... | collective-permute-start | bytes 497672 | tf_op jit(solution)/shard_map/ppermute | solution.py:401
  208.7 10.5 %collective-permute-start.11 = (bf16[18,48,96]{2,1,0:T(8,128)(2,1)S(1)}, bf16[18,48,96]{2,1,0:T(8,128)(2,1)S(1)}, u32[]{:S(2)}, u32[]{:S(2)}) collective-permute-start(bf16[18,48,96]{2,1,0:T(8,128)(2,1)S(1)} %get-tuple-element.35), channel_id=1, source_target_pairs={{0,3},{1,2},{2,1},{3,0},{4,7},{5,6},{6,5},{7,4},{8,11},{9,10},{10,... | collective-permute-start | bytes 497672 | tf_op jit(solution)/shard_map/ppermute | solution.py:401
  215.9 4.9 %collective-permute-start.19 = (bf16[2,2,48,248]{3,2,0,1:T(8,128)(2,1)S(1)}, bf16[2,2,48,248]{3,2,0,1:T(8,128)(2,1)S(1)}, u32[]{:S(2)}, u32[]{:S(2)}) collective-permute-start(bf16[2,2,48,248]{3,2,0,1:T(8,128)(2,1)S(1)} %pad_maximum_fusion.8), channel_id=1, source_target_pairs={{0,4},{4,0},{8,12},{12,8},{16,20},{20,16},{24,28},{28,24},{1,5},{5... | collective-permute-start | bytes 285704 | tf_op jit(solution)/shard_map/ppermute | solution.py:409
  227.6 3.5 %collective-permute-start.20 = (bf16[2,48,96]{2,1,0:T(8,128)(2,1)S(1)}, bf16[2,48,96]{2,1,0:T(8,128)(2,1)S(1)}, u32[]{:S(2)}, u32[]{:S(2)}) collective-permute-start(bf16[2,48,96]{2,1,0:T(8,128)(2,1)S(1)} %get-tuple-element.43), channel_id=1, source_target_pairs={{0,1},{1,0},{2,3},{3,2},{4,5},{5,4},{6,7},{7,6},{8,9},{9,8},{10,11... | collective-permute-start | bytes 55304 | tf_op jit(solution)/shard_map/ppermute | solution.py:401
  227.7 3.9 %collective-permute-start.21 = (bf16[2,48,96]{2,1,0:T(8,128)(2,1)S(1)}, bf16[2,48,96]{2,1,0:T(8,128)(2,1)S(1)}, u32[]{:S(2)}, u32[]{:S(2)}) collective-permute-start(bf16[2,48,96]{2,1,0:T(8,128)(2,1)S(1)} %get-tuple-element.44), channel_id=1, source_target_pairs={{0,2},{1,3},{2,0},{3,1},{4,6},{5,7},{6,4},{7,5},{8,10},{9,11},{10,... | collective-permute-start | bytes 55304 | tf_op jit(solution)/shard_map/ppermute | solution.py:401
  229.8 3.3 %collective-permute-start.22 = (bf16[2,48,96]{2,1,0:T(8,128)(2,1)S(1)}, bf16[2,48,96]{2,1,0:T(8,128)(2,1)S(1)}, u32[]{:S(2)}, u32[]{:S(2)}) collective-permute-start(bf16[2,48,96]{2,1,0:T(8,128)(2,1)S(1)} %get-tuple-element.45), channel_id=1, source_target_pairs={{0,3},{1,2},{2,1},{3,0},{4,7},{5,6},{6,5},{7,4},{8,11},{9,10},{10,... | collective-permute-start | bytes 55304 | tf_op jit(solution)/shard_map/ppermute | solution.py:401
  (29 other events, 304.0 us)

commit v8 on v7

--- a/solution.py
+++ b/solution.py
@@ -332,7 +332,7 @@
 
 
 def combine_kernel(count, final, lag_ref, me_ref, weight_ref, *refs):
-    got, others, (out_ref, seam_ref, sum_ref) = refs[:count], refs[count:-3], refs[-3:]
+    got, others, (out_ref, seam_ref, sum_ref) = refs[:count][::-1], refs[count:-3], refs[-3:]
     me = me_ref[0]
     seams = got[0].shape[0] > 2
     total = jnp.zeros(sum_ref.shape[1:], jnp.float32)
@@ -392,7 +392,7 @@
             bytes_accessed=2 * count * days * slots * degrees,
             transcendentals=0,
         ),
-    )(lag_days, me, weights, *got, *others)
+    )(lag_days, me, weights, *got[::-1], *others)
 
 
 def swap(sends, axis):

time: 235 us -> 234 us (level)
  transfers between devices with their start and end apart: 26 -> 26, of which waited for: 15 -> 14; matrix products, arithmetic and copies ran while one was open for 6% -> 6% of each run, Pallas kernels for 22% -> 23%
where the time goes in v8:
time: 234 us; the launch traced here: 233 us
  waiting for transfers between devices  101 us (43%)
  Pallas kernels  64.1 us (27%)
  starting transfers between devices  47.3 us (20%)
  local copies, waits for them, and re-layouts  11.5 us (5%)
  between operations  4.94 us (2%)
  other arithmetic  3.7 us (2%)
    all_to_all x3, waiting for transfers between devices, exchange(): lax.all_to_all(spectra, 'wide', split_axis=0, concat_axis=0, tiled=True)  46 us
    ppermute x7, waiting for transfers between devices, gather_swap(): return lax.ppermute(held, axis, [(i, i ^ reach) for i in range(count)])  45.9 us
    pallas_call x3, Pallas kernels, spectra_of(): pl.pallas_call(functools.partial(spectra_kernel, owned), grid=(last - fir...  32.3 us
    pallas_call x3, Pallas kernels, digest(): pl.pallas_call(functools.partial(digest_kernel, (len(received), len(by_ho...  21.9 us
    ppermute x16, starting transfers between devices, swap(): lax.ppermute(sends[hop], axis, [(i, peer(i, hop, count)[0]) for i in rang...  19.8 us
    all_to_all x3, starting transfers between devices, exchange(): lax.all_to_all(spectra, 'wide', split_axis=0, concat_axis=0, tiled=True)  17.7 us
    ppermute x7, starting transfers between devices, gather_swap(): return lax.ppermute(held, axis, [(i, i ^ reach) for i in range(count)])  9.75 us
    ppermute x16, waiting for transfers between devices, swap(): lax.ppermute(sends[hop], axis, [(i, peer(i, hop, count)[0]) for i in rang...  9.22 us
  transfers between devices with their start and end apart: 26, of which 14 were waited for; matrix products, arithmetic and copies ran while one was open for 6% of the time, Pallas kernels for 23%

profile of v8, /device:TPU:0, one launch (start us, length us, event | category | flops | bytes accessed | tf_op | source)
XLA Modules:
  0.0 233.0 jit_solution(11993491425963897684)
XLA Ops:
  0.6 6.7 %shard_map.77 = (bf16[48,1408]{1,0:T(8,128)(2,1)}, bf16[48,1408]{1,0:T(8,128)(2,1)}, bf16[48,1408]{1,0:T(8,128)(2,1)}, bf16[48,1408]{1,0:T(8,128)(2,1)}, bf16[48...) custom-call(s32[384]{0:T(512)} %order_ref.7, ...), custom_call_target="tpu_custom_call" | custom-call | flops 1557135360 | bytes 6242304 | tf_op jit(solution)/shard_map/pallas_call | solution.py:108
  7.4 3.0 %collective-permute-start.2 = (bf16[48,1408]{1,0:T(8,128)(2,1)}, bf16[48,1408]{1,0:T(8,128)(2,1)}, u32[]{:S(2)}, u32[]{:S(2)}) collective-permute-start(bf16[48,1408]{1,0:T(8,128)(2,1)} %get-tuple-element.25), channel_id=1, source_target_pairs={{0,4},{4,0},{8,12},{12,8},{16,20},{20,16},{24,28},{28,24},{1,5},{5... | collective-permute-start | bytes 405512 | tf_op jit(solution)/shard_map/ppermute | solution.py:401
  12.0 3.0 %collective-permute-start.5 = (bf16[48,1408]{1,0:T(8,128)(2,1)}, bf16[48,1408]{1,0:T(8,128)(2,1)}, u32[]{:S(2)}, u32[]{:S(2)}) collective-permute-start(bf16[48,1408]{1,0:T(8,128)(2,1)} %get-tuple-element.28), channel_id=1, source_target_pairs={{0,16},{4,20},{8,24},{12,28},{16,0},{20,4},{24,8},{28,12},{1,17},{... | collective-permute-start | bytes 405512 | tf_op jit(solution)/shard_map/ppermute | solution.py:401
  16.2 3.6 %collective-permute-start.7 = (bf16[48,1408]{1,0:T(8,128)(2,1)}, bf16[48,1408]{1,0:T(8,128)(2,1)}, u32[]{:S(2)}, u32[]{:S(2)}) collective-permute-start(bf16[48,1408]{1,0:T(8,128)(2,1)} %get-tuple-element.30), channel_id=1, source_target_pairs={{0,24},{4,28},{8,16},{12,20},{16,8},{20,12},{24,0},{28,4},{1,25},{... | collective-permute-start | bytes 405512 | tf_op jit(solution)/shard_map/ppermute | solution.py:401
  19.8 1.9 collective-permute-done.3.refs_2_
  22.5 12.5 %shard_map.78.refs_0_ = bf16[384,4224]{1,0:T(8,128)(2,1)} custom-call(s32[384]{0:T(512)} %order_ref.7, bf16[2,1440,384]{2,1,0:T(8,128)(2,1)} %constant.42.clone.part_hbm.part_ref, bf16[5632,1440]{1,0:T(8,128)(2,1)} %bitcast.100, bf16[48,1408]{1,0:T(8,128)(2,1)} %get-tuple-element.24.refs_0_), custom_call_target="tpu_custom_call" | custom-call | flops 4671406080 | bytes 16515072 | tf_op jit(solution)/shard_map/pallas_call | solution.py:141
  35.2 8.2 %all-to-all-start.1 = ((bf16[8,48,4224]{2,1,0:T(8,128)(2,1)}), bf16[8,48,4224]{2,1,0:T(8,128)(2,1)}, u32[]{:S(2)}, u32[]{:S(2)}) async-start(bf16[8,48,4224]{2,1,0:T(8,128)(2,1)} %bitcast.103), calls=%async_computation.1 | async-start | bytes 6488064 | tf_op jit(solution)/shard_map/all_to_all | solution.py:479
  45.0 3.6 %collective-permute-done = f32[2,2,3,24,96]{4,3,2,1,0:T(8,128)S(1)} collective-permute-done((f32[2,2,3,24,96]{4,3,2,1,0:T(8,128)S(1)}, f32[2,2,3,24,96]{4,3,2,1,0:T(8,128)S(1)}, u32[]{:S(2)}, u32[]{:S(2)}) %collective-permute-start) | collective-permute-done | bytes 110624 | tf_op jit(solution)/shard_map/ppermute | solution.py:409
  52.7 7.2 %shard_map.80.refs_0_ = bf16[384,1408]{1,0:T(8,128)(2,1)} custom-call(s32[384]{0:T(512)} %order_ref.7, bf16[2,1440,384]{2,1,0:T(8,128)(2,1)} %constant.42.clone.part_hbm.part_ref, bf16[5632,1440]{1,0:T(8,128)(2,1)} %bitcast.101, bf16[384,4224]{1,0:T(8,128)(2,1)} %shard_map.79.refs_0_, f32[2,2,3,24,384]{4,3,2,1,0:T(8,128)} %reshape.65.refs_1_), custom_call_target="tpu_custom_call" | custom-call | flops 1557135360 | bytes 6242304 | tf_op jit(solution)/shard_map/pallas_call | solution.py:141
  60.0 12.5 %shard_map.81 = bf16[384,4224]{1,0:T(8,128)(2,1)} custom-call(s32[384]{0:T(512)} %order_ref.7, bf16[2,1440,384]{2,1,0:T(8,128)(2,1)} %constant.42.clone.part_hbm.part_ref, bf16[5632,1440]{1,0:T(8,128)(2,1)} %bitcast.102, bf16[384,1408]{1,0:T(8,128)(2,1)} %shard_map.80.refs_0_, f32[2,2,3,24,384]{4,3,2,1,0:T(8,128)} %reshape.65.refs_1_), custom_call_target="tpu_custom_call" | custom-call | flops 4671406080 | bytes 16515072 | tf_op jit(solution)/shard_map/pallas_call | solution.py:141
  72.5 43.6 %all-to-all-done.1.refs_8_ = bf16[8,48,4224]{2,1,0:T(8,128)(2,1)} async-done(((bf16[8,48,4224]{2,1,0:T(8,128)(2,1)}), bf16[8,48,4224]{2,1,0:T(8,128)(2,1)}, u32[]{:S(2)}, u32[]{:S(2)}) %all-to-all-start.1) | async-done | bytes 3244064 | tf_op jit(solution)/shard_map/all_to_all | solution.py:479
  116.1 4.8 %all-to-all-start = ((bf16[8,48,4224]{2,1,0:T(8,128)(2,1)}), bf16[8,48,4224]{2,1,0:T(8,128)(2,1)}, u32[]{:S(2)}, u32[]{:S(2)}) async-start(bf16[8,48,4224]{2,1,0:T(8,128)(2,1)} %bitcast.105), calls=%async_computation | async-start | bytes 6488064 | tf_op jit(solution)/shard_map/all_to_all | solution.py:479
  129.5 11.7 %shard_map.85 = (bf16[18,48,96]{2,1,0:T(8,128)(2,1)}, bf16[18,48,96]{2,1,0:T(8,128)(2,1)}, bf16[18,48,96]{2,1,0:T(8,128)(2,1)}, bf16[18,48,96]{2,1,0:T(8,128)(2,1)}, bf16[64,48,16]{2,1,0:T(8,128)(2,1)}) custom-call(s32[3]{0:T(128)} %lag_ref.11, s32[2]{0:T(128)} %pad_add_fusion.me_ref, f32[3,48,384]{2,1,0:T(8,128)} %pad_maximum_fusion.4.weight_ref, ...), custom_call_target="tpu_custom_call" | custom-call | flops 3321888768 | bytes 6684672 | tf_op jit(solution)/shard_map/pallas_call | solution.py:277
  145.0 2.8 %collective-permute-done.15 = bf16[48,1024]{1,0:T(8,128)(2,1)S(1)} collective-permute-done((bf16[48,1024]{1,0:T(8,128)(2,1)S(1)}, bf16[48,1024]{1,0:T(8,128)(2,1)S(1)}, u32[]{:S(2)}, u32[]{:S(2)}) %collective-permute-start.15) | collective-permute-done | bytes 98336 | tf_op jit(solution)/shard_map/ppermute | solution.py:409
  153.4 2.6 %collective-permute-start.17 = (bf16[48,248]{1,0:T(8,128)(2,1)S(1)}, bf16[48,248]{1,0:T(8,128)(2,1)S(1)}, u32[]{:S(2)}, u32[]{:S(2)}) collective-permute-start(bf16[48,248]{1,0:T(8,128)(2,1)S(1)} %dynamic-slice_bitcast_fusion), channel_id=1, source_target_pairs={{0,16},{4,20},{8,24},{12,28},{16,0},{20,4},{24,8},{28,12},{1,17},{... | collective-permute-start | bytes 71432 | tf_op jit(solution)/shard_map/ppermute | solution.py:409
  156.5 4.8 %collective-permute-done.13.refs_1_ = bf16[18,48,96]{2,1,0:T(8,128)(2,1)S(1)} collective-permute-done((bf16[18,48,96]{2,1,0:T(8,128)(2,1)}, bf16[18,48,96]{2,1,0:T(8,128)(2,1)S(1)}, u32[]{:S(2)}, u32[]{:S(2)}) %collective-permute-start.13) | collective-permute-done | bytes 165920 | tf_op jit(solution)/shard_map/ppermute | solution.py:401
  162.9 29.9 %collective-permute-done.17.refs_2_ = bf16[48,248]{1,0:T(8,128)(2,1)S(1)} collective-permute-done((bf16[48,248]{1,0:T(8,128)(2,1)S(1)}, bf16[48,248]{1,0:T(8,128)(2,1)S(1)}, u32[]{:S(2)}, u32[]{:S(2)}) %collective-permute-start.17) | collective-permute-done | bytes 23840 | tf_op jit(solution)/shard_map/ppermute | solution.py:409
  193.4 4.6 %all-to-all-start.2 = ((bf16[8,48,1408]{2,1,0:T(8,128)(2,1)}), bf16[8,48,1408]{2,1,0:T(8,128)(2,1)}, u32[]{:S(2)}, u32[]{:S(2)}) async-start(bf16[8,48,1408]{2,1,0:T(8,128)(2,1)} %bitcast.104), calls=%async_computation.2 | async-start | bytes 2162688 | tf_op jit(solution)/shard_map/all_to_all | solution.py:479
  199.8 6.7 %shard_map.82 = (bf16[18,48,96]{2,1,0:T(8,128)(2,1)S(1)}, bf16[18,48,96]{2,1,0:T(8,128)(2,1)S(1)}, bf16[18,48,96]{2,1,0:T(8,128)(2,1)S(1)}, bf16[18,48,96]{2,1,0:T(8,128)(2,1)S(1)}, bf16[16,48,384]{2,1,0:T(8,128)(2,1)S(1)}) custom-call(s32[3]{0:T(128)S(1)} %copy-done.8, s32[2]{0:T(128)S(1)} %copy-done.9, f32[3,48,384]{2,1,0:T(8,128)S(1)} %pad_maximum_fusion.3.weight_ref, ...), custom_call_target="tpu_custom_call" | custom-call | flops 3321888768 | bytes 6684672 | tf_op jit(solution)/shard_map/pallas_call | solution.py:277
  208.7 7.2 %collective-permute-done.18 = bf16[2,48,248]{2,1,0:T(8,128)(2,1)S(1)} collective-permute-done((bf16[2,48,248]{2,1,0:T(8,128)(2,1)S(1)}, bf16[2,48,248]{2,1,0:T(8,128)(2,1)S(1)}, u32[]{:S(2)}, u32[]{:S(2)}) %collective-permute-start.18) | collective-permute-done | bytes 47648 | tf_op jit(solution)/shard_map/ppermute | solution.py:409
  215.9 1.9 collective-permute-start.19
  221.7 2.4 %all-to-all-done.2.refs_1_ = bf16[8,48,1408]{2,1,0:T(8,128)(2,1)} async-done(((bf16[8,48,1408]{2,1,0:T(8,128)(2,1)}), bf16[8,48,1408]{2,1,0:T(8,128)(2,1)}, u32[]{:S(2)}, u32[]{:S(2)}) %all-to-all-start.2) | async-done | bytes 1081376 | tf_op jit(solution)/shard_map/all_to_all | solution.py:479
  224.1 3.5 %shard_map.88 = (bf16[2,48,96]{2,1,0:T(8,128)(2,1)S(1)}, bf16[2,48,96]{2,1,0:T(8,128)(2,1)S(1)}, bf16[2,48,96]{2,1,0:T(8,128)(2,1)S(1)}, bf16[2,48,96]{2,1,0:T(8,128)(2,1)S(1)}) custom-call(s32[3]{0:T(128)S(1)} %copy-done.8, s32[2]{0:T(128)S(1)} %copy-done.9, f32[3,48,384]{2,1,0:T(8,128)S(1)} %copy-done.5, bf16[704,768]{1,0:T(8,128)(2,1)S(1)} %shard_map.84.lat_hbm, ...), custom_call_target="tpu_custom_call" | custom-call | flops 3321888768 | bytes 6684672 | tf_op jit(solution)/shard_map/pallas_call | solution.py:277
  227.7 2.1 collective-permute-start.21
  (145 shorter events, 36.9 us)
Async XLA Ops:
  7.4 8.9 %collective-permute-start.2 = (bf16[48,1408]{1,0:T(8,128)(2,1)}, bf16[48,1408]{1,0:T(8,128)(2,1)}, u32[]{:S(2)}, u32[]{:S(2)}) collective-permute-start(bf16[48,1408]{1,0:T(8,128)(2,1)} %get-tuple-element.25), channel_id=1, source_target_pairs={{0,4},{4,0},{8,12},{12,8},{16,20},{20,16},{24,28},{28,24},{1,5},{5... | collective-permute-start | bytes 405512 | tf_op jit(solution)/shard_map/ppermute | solution.py:401
  10.4 11.4 %collective-permute-start.3 = (bf16[48,1408]{1,0:T(8,128)(2,1)}, bf16[48,1408]{1,0:T(8,128)(2,1)}, u32[]{:S(2)}, u32[]{:S(2)}) collective-permute-start(bf16[48,1408]{1,0:T(8,128)(2,1)} %get-tuple-element.26), channel_id=1, source_target_pairs={{0,8},{4,12},{8,0},{12,4},{16,24},{20,28},{24,16},{28,20},{1,9},{5... | collective-permute-start | bytes 405512 | tf_op jit(solution)/shard_map/ppermute | solution.py:401
  12.0 23.1 %collective-permute-start.4 = (bf16[48,1408]{1,0:T(8,128)(2,1)}, bf16[48,1408]{1,0:T(8,128)(2,1)}, u32[]{:S(2)}, u32[]{:S(2)}) collective-permute-start(bf16[48,1408]{1,0:T(8,128)(2,1)} %get-tuple-element.27), channel_id=1, source_target_pairs={{0,12},{4,8},{8,4},{12,0},{16,28},{20,24},{24,20},{28,16},{1,13},{... | collective-permute-start | bytes 405512 | tf_op jit(solution)/shard_map/ppermute | solution.py:401
  12.0 23.1 %collective-permute-start.5 = (bf16[48,1408]{1,0:T(8,128)(2,1)}, bf16[48,1408]{1,0:T(8,128)(2,1)}, u32[]{:S(2)}, u32[]{:S(2)}) collective-permute-start(bf16[48,1408]{1,0:T(8,128)(2,1)} %get-tuple-element.28), channel_id=1, source_target_pairs={{0,16},{4,20},{8,24},{12,28},{16,0},{20,4},{24,8},{28,12},{1,17},{... | collective-permute-start | bytes 405512 | tf_op jit(solution)/shard_map/ppermute | solution.py:401
  14.9 20.2 %collective-permute-start.6 = (bf16[48,1408]{1,0:T(8,128)(2,1)}, bf16[48,1408]{1,0:T(8,128)(2,1)}, u32[]{:S(2)}, u32[]{:S(2)}) collective-permute-start(bf16[48,1408]{1,0:T(8,128)(2,1)} %get-tuple-element.29), channel_id=1, source_target_pairs={{0,20},{4,16},{8,28},{12,24},{16,4},{20,0},{24,12},{28,8},{1,21},{... | collective-permute-start | bytes 405512 | tf_op jit(solution)/shard_map/ppermute | solution.py:401
  16.2 19.0 %collective-permute-start.7 = (bf16[48,1408]{1,0:T(8,128)(2,1)}, bf16[48,1408]{1,0:T(8,128)(2,1)}, u32[]{:S(2)}, u32[]{:S(2)}) collective-permute-start(bf16[48,1408]{1,0:T(8,128)(2,1)} %get-tuple-element.30), channel_id=1, source_target_pairs={{0,24},{4,28},{8,16},{12,20},{16,8},{20,12},{24,0},{28,4},{1,25},{... | collective-permute-start | bytes 405512 | tf_op jit(solution)/shard_map/ppermute | solution.py:401
  21.8 13.4 %collective-permute-start.8 = (bf16[48,1408]{1,0:T(8,128)(2,1)}, bf16[48,1408]{1,0:T(8,128)(2,1)}, u32[]{:S(2)}, u32[]{:S(2)}) collective-permute-start(bf16[48,1408]{1,0:T(8,128)(2,1)} %get-tuple-element.31), channel_id=1, source_target_pairs={{0,28},{4,24},{8,20},{12,16},{16,12},{20,8},{24,4},{28,0},{1,29},{... | collective-permute-start | bytes 405512 | tf_op jit(solution)/shard_map/ppermute | solution.py:401
  35.2 80.9 %all-to-all-start.1 = ((bf16[8,48,4224]{2,1,0:T(8,128)(2,1)}), bf16[8,48,4224]{2,1,0:T(8,128)(2,1)}, u32[]{:S(2)}, u32[]{:S(2)}) async-start(bf16[8,48,4224]{2,1,0:T(8,128)(2,1)} %bitcast.103), calls=%async_computation.1 | async-start | bytes 6488064 | tf_op jit(solution)/shard_map/all_to_all | solution.py:479
  43.4 5.2 %collective-permute-start = (f32[2,2,3,24,96]{4,3,2,1,0:T(8,128)S(1)}, f32[2,2,3,24,96]{4,3,2,1,0:T(8,128)S(1)}, u32[]{:S(2)}, u32[]{:S(2)}) collective-permute-start(f32[2,2,3,24,96]{4,3,2,1,0:T(8,128)S(1)} %bitcast.112), channel_id=1, source_target_pairs={{0,2},{1,3},{2,0},{3,1},{4,6},{5,7},{6,4},{7,5},{8,10},{9,11},{10,... | collective-permute-start | bytes 331784 | tf_op jit(solution)/shard_map/ppermute | solution.py:409
  116.1 77.2 %all-to-all-start = ((bf16[8,48,4224]{2,1,0:T(8,128)(2,1)}), bf16[8,48,4224]{2,1,0:T(8,128)(2,1)}, u32[]{:S(2)}, u32[]{:S(2)}) async-start(bf16[8,48,4224]{2,1,0:T(8,128)(2,1)} %bitcast.105), calls=%async_computation | async-start | bytes 6488064 | tf_op jit(solution)/shard_map/all_to_all | solution.py:479
  143.2 4.7 %collective-permute-start.15 = (bf16[48,1024]{1,0:T(8,128)(2,1)S(1)}, bf16[48,1024]{1,0:T(8,128)(2,1)S(1)}, u32[]{:S(2)}, u32[]{:S(2)}) collective-permute-start(bf16[48,1024]{1,0:T(8,128)(2,1)S(1)} %reshape.70), channel_id=1, source_target_pairs={{0,2},{1,3},{2,0},{3,1},{4,6},{5,7},{6,4},{7,5},{8,10},{9,11},{10,... | collective-permute-start | bytes 294920 | tf_op jit(solution)/shard_map/ppermute | solution.py:409
  147.9 2.7 %collective-permute-start.16 = (bf16[2,48,1024]{2,1,0:T(8,128)(2,1)S(1)}, bf16[2,48,1024]{2,1,0:T(8,128)(2,1)S(1)}, u32[]{:S(2)}, u32[]{:S(2)}) collective-permute-start(bf16[2,48,1024]{2,1,0:T(8,128)(2,1)S(1)} %pad_maximum_fusion.6), channel_id=1, source_target_pairs={{0,1},{1,0},{2,3},{3,2},{4,5},{5,4},{6,7},{7,6},{8,9},{9,8},{10,11... | collective-permute-start | bytes 589832 | tf_op jit(solution)/shard_map/ppermute | solution.py:409
  148.5 8.0 %collective-permute-start.12 = (bf16[18,48,96]{2,1,0:T(8,128)(2,1)}, bf16[18,48,96]{2,1,0:T(8,128)(2,1)S(1)}, u32[]{:S(2)}, u32[]{:S(2)}) collective-permute-start(bf16[18,48,96]{2,1,0:T(8,128)(2,1)} %get-tuple-element.37), channel_id=1, source_target_pairs={{0,3},{1,2},{2,1},{3,0},{4,7},{5,6},{6,5},{7,4},{8,11},{9,10},{10,... | collective-permute-start | bytes 497672 | tf_op jit(solution)/shard_map/ppermute | solution.py:401
  150.4 10.9 %collective-permute-start.13 = (bf16[18,48,96]{2,1,0:T(8,128)(2,1)}, bf16[18,48,96]{2,1,0:T(8,128)(2,1)S(1)}, u32[]{:S(2)}, u32[]{:S(2)}) collective-permute-start(bf16[18,48,96]{2,1,0:T(8,128)(2,1)} %get-tuple-element.38), channel_id=1, source_target_pairs={{0,2},{1,3},{2,0},{3,1},{4,6},{5,7},{6,4},{7,5},{8,10},{9,11},{10,... | collective-permute-start | bytes 497672 | tf_op jit(solution)/shard_map/ppermute | solution.py:401
  150.6 10.7 %collective-permute-start.14 = (bf16[18,48,96]{2,1,0:T(8,128)(2,1)S(1)}, bf16[18,48,96]{2,1,0:T(8,128)(2,1)S(1)}, u32[]{:S(2)}, u32[]{:S(2)}) collective-permute-start(bf16[18,48,96]{2,1,0:T(8,128)(2,1)S(1)} %copy-done.25), channel_id=1, source_target_pairs={{0,1},{1,0},{2,3},{3,2},{4,5},{5,4},{6,7},{7,6},{8,9},{9,8},{10,11... | collective-permute-start | bytes 497672 | tf_op jit(solution)/shard_map/ppermute | solution.py:401
  153.4 39.4 %collective-permute-start.17 = (bf16[48,248]{1,0:T(8,128)(2,1)S(1)}, bf16[48,248]{1,0:T(8,128)(2,1)S(1)}, u32[]{:S(2)}, u32[]{:S(2)}) collective-permute-start(bf16[48,248]{1,0:T(8,128)(2,1)S(1)} %dynamic-slice_bitcast_fusion), channel_id=1, source_target_pairs={{0,16},{4,20},{8,24},{12,28},{16,0},{20,4},{24,8},{28,12},{1,17},{... | collective-permute-start | bytes 71432 | tf_op jit(solution)/shard_map/ppermute | solution.py:409
  193.4 30.7 %all-to-all-start.2 = ((bf16[8,48,1408]{2,1,0:T(8,128)(2,1)}), bf16[8,48,1408]{2,1,0:T(8,128)(2,1)}, u32[]{:S(2)}, u32[]{:S(2)}) async-start(bf16[8,48,1408]{2,1,0:T(8,128)(2,1)} %bitcast.104), calls=%async_computation.2 | async-start | bytes 2162688 | tf_op jit(solution)/shard_map/all_to_all | solution.py:479
  198.1 17.8 %collective-permute-start.18 = (bf16[2,48,248]{2,1,0:T(8,128)(2,1)S(1)}, bf16[2,48,248]{2,1,0:T(8,128)(2,1)S(1)}, u32[]{:S(2)}, u32[]{:S(2)}) collective-permute-start(bf16[2,48,248]{2,1,0:T(8,128)(2,1)S(1)} %pad_maximum_fusion.11), channel_id=1, source_target_pairs={{0,8},{4,12},{8,0},{12,4},{16,24},{20,28},{24,16},{28,20},{1,9},{5... | collective-permute-start | bytes 142856 | tf_op jit(solution)/shard_map/ppermute | solution.py:409
  206.5 11.4 %collective-permute-start.9 = (bf16[18,48,96]{2,1,0:T(8,128)(2,1)S(1)}, bf16[18,48,96]{2,1,0:T(8,128)(2,1)S(1)}, u32[]{:S(2)}, u32[]{:S(2)}) collective-permute-start(bf16[18,48,96]{2,1,0:T(8,128)(2,1)S(1)} %get-tuple-element.32), channel_id=1, source_target_pairs={{0,3},{1,2},{2,1},{3,0},{4,7},{5,6},{6,5},{7,4},{8,11},{9,10},{10,... | collective-permute-start | bytes 497672 | tf_op jit(solution)/shard_map/ppermute | solution.py:401
  206.8 12.2 %collective-permute-start.10 = (bf16[18,48,96]{2,1,0:T(8,128)(2,1)S(1)}, bf16[18,48,96]{2,1,0:T(8,128)(2,1)S(1)}, u32[]{:S(2)}, u32[]{:S(2)}) collective-permute-start(bf16[18,48,96]{2,1,0:T(8,128)(2,1)S(1)} %get-tuple-element.33), channel_id=1, source_target_pairs={{0,2},{1,3},{2,0},{3,1},{4,6},{5,7},{6,4},{7,5},{8,10},{9,11},{10,... | collective-permute-start | bytes 497672 | tf_op jit(solution)/shard_map/ppermute | solution.py:401
  208.7 10.3 %collective-permute-start.11 = (bf16[18,48,96]{2,1,0:T(8,128)(2,1)S(1)}, bf16[18,48,96]{2,1,0:T(8,128)(2,1)S(1)}, u32[]{:S(2)}, u32[]{:S(2)}) collective-permute-start(bf16[18,48,96]{2,1,0:T(8,128)(2,1)S(1)} %get-tuple-element.34), channel_id=1, source_target_pairs={{0,1},{1,0},{2,3},{3,2},{4,5},{5,4},{6,7},{7,6},{8,9},{9,8},{10,11... | collective-permute-start | bytes 497672 | tf_op jit(solution)/shard_map/ppermute | solution.py:401
  215.9 4.9 %collective-permute-start.19 = (bf16[2,2,48,248]{3,2,0,1:T(8,128)(2,1)S(1)}, bf16[2,2,48,248]{3,2,0,1:T(8,128)(2,1)S(1)}, u32[]{:S(2)}, u32[]{:S(2)}) collective-permute-start(bf16[2,2,48,248]{3,2,0,1:T(8,128)(2,1)S(1)} %pad_maximum_fusion.8), channel_id=1, source_target_pairs={{0,4},{4,0},{8,12},{12,8},{16,20},{20,16},{24,28},{28,24},{1,5},{5... | collective-permute-start | bytes 285704 | tf_op jit(solution)/shard_map/ppermute | solution.py:409
  227.6 3.4 %collective-permute-start.20 = (bf16[2,48,96]{2,1,0:T(8,128)(2,1)S(1)}, bf16[2,48,96]{2,1,0:T(8,128)(2,1)S(1)}, u32[]{:S(2)}, u32[]{:S(2)}) collective-permute-start(bf16[2,48,96]{2,1,0:T(8,128)(2,1)S(1)} %get-tuple-element.42), channel_id=1, source_target_pairs={{0,3},{1,2},{2,1},{3,0},{4,7},{5,6},{6,5},{7,4},{8,11},{9,10},{10,... | collective-permute-start | bytes 55304 | tf_op jit(solution)/shard_map/ppermute | solution.py:401
  227.7 4.1 %collective-permute-start.21 = (bf16[2,48,96]{2,1,0:T(8,128)(2,1)S(1)}, bf16[2,48,96]{2,1,0:T(8,128)(2,1)S(1)}, u32[]{:S(2)}, u32[]{:S(2)}) collective-permute-start(bf16[2,48,96]{2,1,0:T(8,128)(2,1)S(1)} %get-tuple-element.43), channel_id=1, source_target_pairs={{0,2},{1,3},{2,0},{3,1},{4,6},{5,7},{6,4},{7,5},{8,10},{9,11},{10,... | collective-permute-start | bytes 55304 | tf_op jit(solution)/shard_map/ppermute | solution.py:401
  (29 other events, 305.8 us)
